TPU v7x, 32 devices: a whole 2x2x4 slice. The times are simulated.
32 devices in a mesh: group: 4 (over x, core), shard: 8 (over z, y).
Axes of the slice: x: 2, y: 2, z: 4, core: 2. Of those that a mesh axis runs over, the one named last changes fastest.
Arguments:
- data: float32 [2, 32768], P(None, ('group', 'shard')), as said below
- inv_noise: bfloat16 [32768], P(('group', 'shard')), may hold values from 0.5 to 2
- mbh_amp: float32 [128, 6, 3, 32], P('shard', None, None, 'group'), may hold values from -0.15 to 0.15
- mbh_phase: float32 [128, 6, 3, 32], P('shard', None, None, 'group'), may hold values from -1024 to 1024
- bin_amp: float32 [32, 512], P(('group', 'shard')), may hold values from 0.15 to 0.4
- bin_phase: float32 [32, 512], P(('group', 'shard')), may hold values from -3.140625 to 3.140625
- bin_slope: float32 [32, 512], P(('group', 'shard')), may hold values from -3 to 3
- bin_curve: float32 [32, 512], P(('group', 'shard')), may hold values from -0.01 to 0.01
- bin_start: int32 [32, 512], P(('group', 'shard')), may hold values from 0 to 1023, as said below
- bin_count: int32 [32], P(('group', 'shard')), may hold values from 64 to 512, as said below
Outputs:
- accept_prob: float32 [64, 16384], P(None, ('group', 'shard'))
- residual_new: float32 [64, 2, 32768], P(None, None, ('group', 'shard'))
- noise_fit: float32 [32], P(('group', 'shard'))
Inputs may be any that keep to these rules, and one draw needn't show every extreme that they name: data has a scale that varies from bin to bin and shrinks from the first band to the last. Slots p < bin_count[n] of band n are live, the others are empty; each band's count is 512, 256, 128 or 64, and some band holds 512. `bin_start`: in the last band every start is at most 896, so that no waveform passes the last bin; in every other band slot 0 starts from 960 to 992, so that its waveform passes into the next band.
All inputs are finite; a program needn't handle non-finite values.
Results may differ from a plain program's by a relative error of at most 0.0025.
The roundings to bfloat16 on the way count: a program that leaves them out, or rounds other values in their place, can miss the bound.
Values may be sent and summed in bfloat16 or wider, within the bound.
No kernel may reach another device: no remote copies, remote signals or barrier semaphores. Data moves between devices by JAX's collectives and lax.ppermute only.
A program may use at most 64 MiB of HBM per device.

v0:
```python
import jax
import jax.numpy as jnp
from jax import lax
from jax.sharding import PartitionSpec as P

W = 64
Q = 128
NCOEF = 8


def shifted_2(x, axis, by):
    peers = lax.axis_size(axis)
    pairs = [(i, i + by) for i in range(peers) if 0 <= i + by < peers]
    return lax.ppermute(x, axis, pairs)


def half_templates(coef_amp, coef_phase, band_bins):
    fraction = jnp.arange(band_bins, dtype=jnp.float32) / band_bins
    amp_curve = (
        coef_amp[:, :, 0, :, None]
        + coef_amp[:, :, 1, :, None] * fraction
        + coef_amp[:, :, 2, :, None] * fraction * fraction
    )
    phase_curve = (
        coef_phase[:, :, 0, :, None]
        + coef_phase[:, :, 1, :, None] * fraction
        + coef_phase[:, :, 2, :, None] * fraction * fraction
    )
    real_part = jnp.sum(amp_curve * jnp.cos(phase_curve), axis=1)
    imag_part = jnp.sum(amp_curve * jnp.sin(phase_curve), axis=1)
    return jnp.stack([real_part, imag_part], axis=1).astype(jnp.bfloat16)


def make_wave(
    amplitude, phase_zero, slope, curvature, first_bin, slot_index, live_count, extent, window
):
    offsets = jnp.arange(extent, dtype=jnp.int32)[None, :] - first_bin[:, None]
    inside = (offsets >= 0) & (offsets < window) & (slot_index < live_count)[:, None]
    shifted = offsets.astype(jnp.float32)
    envelope = jnp.sin(jnp.pi * (shifted + 0.5) / window) ** 2
    phase_angle = (
        phase_zero[:, None] + slope[:, None] * shifted + curvature[:, None] * shifted * shifted
    )
    real_part = jnp.where(inside, amplitude[:, None] * envelope * jnp.cos(phase_angle), 0.0)
    imag_part = jnp.where(inside, amplitude[:, None] * envelope * jnp.sin(phase_angle), 0.0)
    return jnp.stack([real_part, imag_part], axis=1).astype(jnp.bfloat16)


def chebyshev(position):
    terms = [jnp.ones_like(position), position]
    for degree in range(2, NCOEF):
        terms.append(2.0 * position * terms[-1] - terms[-2])
    return jnp.stack(terms[:NCOEF], axis=-1)


def cholesky_solve(gram, moment):
    lower = jnp.linalg.cholesky(gram)
    order_count = gram.shape[0]
    forward = []
    for row_index in range(order_count):
        partial_sum = moment[row_index]
        for col_index in range(row_index):
            partial_sum = partial_sum - lower[row_index, col_index] * forward[col_index]
        forward.append(partial_sum / lower[row_index, row_index])
    backward = [None] * order_count
    for row_index in reversed(range(order_count)):
        partial_sum = forward[row_index]
        for col_index in range(row_index + 1, order_count):
            partial_sum = partial_sum - lower[col_index, row_index] * backward[col_index]
        backward[row_index] = partial_sum / lower[row_index, row_index]
    return jnp.stack(backward)


def local(
    data,
    inv_noise,
    mbh_amp,
    mbh_phase,
    bin_amp,
    bin_phase,
    bin_slope,
    bin_curve,
    bin_start,
    bin_count,
):
    band_bins = data.shape[1]
    slots = bin_amp.shape[1]
    local_halves = half_templates(mbh_amp, mbh_phase, band_bins)
    arrived = lax.all_to_all(local_halves, "shard", split_axis=2, concat_axis=0, tiled=True)
    halves = arrived[:, :, 0, :]
    template = halves.reshape(W, 2, 2, band_bins).astype(jnp.float32).sum(axis=1)
    residual = data[None] - template
    weighted = (residual * inv_noise.astype(jnp.float32)[None, None, :]).astype(jnp.bfloat16)
    weighted_rim, noise_rim = shifted_2((weighted[:, :, :Q], inv_noise[:Q]), ("group", "shard"), -1)
    extent = band_bins + Q
    weighted_flat = jnp.concatenate([weighted, weighted_rim], axis=2).reshape(W, 2 * extent)
    noise_ext = jnp.concatenate([inv_noise, noise_rim], axis=0).astype(jnp.float32)
    live_count = bin_count[0]
    block_rows = min(128, slots)
    block_count = (live_count + block_rows - 1) // block_rows

    def score_block(block_index, running):
        accept_all, correction = running
        first_slot = block_index * block_rows
        amplitude = lax.dynamic_slice_in_dim(bin_amp[0], first_slot, block_rows)
        phase_zero = lax.dynamic_slice_in_dim(bin_phase[0], first_slot, block_rows)
        slope = lax.dynamic_slice_in_dim(bin_slope[0], first_slot, block_rows)
        curvature = lax.dynamic_slice_in_dim(bin_curve[0], first_slot, block_rows)
        first_bin = lax.dynamic_slice_in_dim(bin_start[0], first_slot, block_rows)
        slot_index = first_slot + jnp.arange(block_rows, dtype=jnp.int32)
        wave = make_wave(
            amplitude, phase_zero, slope, curvature, first_bin, slot_index, live_count, extent, Q
        )
        wave_flat = wave.reshape(block_rows, 2 * extent)
        correlation = lax.dot_general(
            wave_flat, weighted_flat, (((1,), (1,)), ((), ())), preferred_element_type=jnp.float32
        )
        self_power = jnp.sum(wave.astype(jnp.float32) ** 2 * noise_ext[None, None, :], axis=(1, 2))
        live = slot_index < live_count
        accept = jnp.where(
            live[:, None], jax.nn.sigmoid(correlation - 0.5 * self_power[:, None]), 0.0
        )
        accept_all = lax.dynamic_update_slice_in_dim(accept_all, accept.T, first_slot, 1)
        correction = correction + lax.dot_general(
            accept.astype(jnp.bfloat16),
            wave_flat,
            (((0,), (0,)), ((), ())),
            preferred_element_type=jnp.float32,
        )
        return (accept_all, correction)

    initial = (jnp.zeros((W, slots), jnp.float32), jnp.zeros((W, 2 * extent), jnp.float32))
    accept_prob, correction = lax.fori_loop(0, block_count, score_block, initial)
    correction = correction.reshape(W, 2, extent)
    carried = shifted_2(
        correction[:, :, band_bins:].astype(jnp.bfloat16), ("group", "shard"), 1
    ).astype(jnp.float32)
    updated = residual - correction[:, :, :band_bins]
    residual_new = jnp.concatenate([updated[:, :, :Q] - carried, updated[:, :, Q:]], axis=2)
    log_power = jnp.log(jnp.mean(residual_new * residual_new) + 1e-06)
    band_total = lax.axis_size("group") * lax.axis_size("shard")
    band_index = lax.axis_index("group") * lax.axis_size("shard") + lax.axis_index("shard")
    position = (2 * band_index + 1).astype(jnp.float32) / band_total - 1.0
    basis = chebyshev(position)
    gram, moment = lax.psum(
        (basis[:, None] * basis[None, :], basis * log_power), ("group", "shard")
    )
    coef = cholesky_solve(gram, moment)
    noise_fit = jnp.sum(basis * coef)[None]
    return (accept_prob, residual_new, noise_fit)


def solution(mesh):
    in_specs = (
        P(None, ("group", "shard")),
        P(("group", "shard")),
        P("shard", None, None, "group"),
        P("shard", None, None, "group"),
        P(("group", "shard"), None),
        P(("group", "shard"), None),
        P(("group", "shard"), None),
        P(("group", "shard"), None),
        P(("group", "shard"), None),
        P(("group", "shard")),
    )
    out_specs = (
        P(None, ("group", "shard")),
        P(None, None, ("group", "shard")),
        P(("group", "shard")),
    )
    return jax.shard_map(local, mesh=mesh, in_specs=in_specs, out_specs=out_specs, check_vma=False)
```

profile of v0, /device:TPU:0, one launch (start us, length us, event | category | flops | bytes accessed | tf_op | source)
XLA Modules:
  0.0 184.4 jit_solution(6036355721476900659)
XLA Ops:
  0.6 0.8 slice_bitcast_fusion.5
  1.4 0.1 copy.54
  1.5 0.1 copy.55
  1.6 0.1 copy.56
  1.7 0.8 slice_bitcast_fusion.2
  2.5 0.1 copy.57
  2.6 0.1 copy.58
  2.7 0.1 copy.59
  2.8 13.1 %multiply_reduce_fusion.2 = (bf16[16,8,1024]{2,1,0:T(8,128)(2,1)S(1)}, bf16[16,8,1024]{2,1,0:T(8,128)(2,1)S(1)}) fusion(f32[16,6,8]{2,1,0:T(8,128)S(1)} %copy.59, f32[16,6,8]{2,1,0:T(8,128)S(1)} %copy.58, f32[16,6,8]{2,1,0:T(8,128)S(1)} %copy.57, f32[16,6,8]{2,1,0:T(8,128)S(1)} %copy.56, f32[1024]{0:T(1024)S(1)} %iota_multiply_fusion, ...), kind=kLoop, calls=%fused_computation.34 | loop fusion | flops 10747904 | bytes 546816 | tf_op jit(solution)/shard_map/reduce_sum | solution.py:29
  15.9 0.1 pad_maximum_fusion
  16.0 1.1 copy.60
  17.1 7.3 %all-to-all-start = ((bf16[16,2,8,1024]{3,0,1,2:T(8,128)(2,1)}), bf16[16,2,8,1024]{3,0,1,2:T(8,128)(2,1)S(1)}, u32[]{:S(2)}, u32[]{:S(2)}) async-start(bf16[16,2,8,1024]{3,0,1,2:T(8,128)(2,1)} %copy.60), calls=%async_computation | async-start | bytes 1048576 | tf_op jit(solution)/shard_map/all_to_all | solution.py:89
  24.4 1.3 collective-permute-start.1
  26.4 0.1 stack.82
  26.5 0.1 broadcast_multiply_fusion.1
  26.5 12.3 %all-to-all-done = bf16[16,2,8,1024]{3,0,1,2:T(8,128)(2,1)S(1)} async-done(((bf16[16,2,8,1024]{3,0,1,2:T(8,128)(2,1)}), bf16[16,2,8,1024]{3,0,1,2:T(8,128)(2,1)S(1)}, u32[]{:S(2)}, u32[]{:S(2)}) %all-to-all-start) | async-done | bytes 524320 | tf_op jit(solution)/shard_map/all_to_all | solution.py:89
  38.8 0.1 convert_bitcast_fusion
  38.9 0.8 copy.61
  39.8 1.0 reduce_sum.60
  40.8 0.2 multiply_convert_fusion
  41.0 1.3 collective-permute-start
  42.4 4.5 %collective-permute-done = bf16[64,2,128]{2,1,0:T(2,128)(2,1)S(1)} collective-permute-done((bf16[64,2,128]{2,1,0:T(2,128)(2,1)S(1)}, bf16[64,2,128]{2,1,0:T(2,128)(2,1)S(1)}, u32[]{:S(2)}, u32[]{:S(2)}) %collective-permute-start) | collective-permute-done | bytes 32800 | tf_op jit(solution)/shard_map/ppermute | solution.py:14
  46.8 0.3 pad_maximum_fusion.2
  47.2 8.2 %while.15 = (s32[]{:T(128)}, f32[64,512]{1,0:T(8,128)S(1)}, f32[64,2304]{1,0:T(8,128)S(1)}, s32[]{:T(128)}, s32[]{:T(128)}, /*index=5*/s32[1,512]{1,0:T(1,128)},...) while((s32[]{:T(128)}, f32[64,512]{1,0:T(8,128)S(1)}, ...), condition=%wide.region_5.6_spmd, body=%wide.region_3.5_spmd.sunk | while | flops 79970560 | bytes 4504539 | solution.py:133
  47.3 0.7 fusion.35
  47.9 0.7 fusion.36
  48.6 0.7 fusion.37
  49.3 0.7 add_compare_fusion.2
  49.9 4.4 %multiply_select_fusion.3 = (bf16[128,1,1152]{0,2,1:T(8,128)(2,1)S(1)}, bf16[128,1,1152]{0,2,1:T(8,128)(2,1)S(1)}) fusion(f32[128]{0:T(128)S(1)} %get-tuple-element.365, f32[128]{0:T(128)S(1)} %get-tuple-element.366, f32[128]{0:T(128)S(1)} %get-tuple-element.367, f32[128]{0:T(128)S(1)} %get-tuple-element.368, s32[128]{0:T(128)S(1)} %fusion.37, ...), kind=kLoop, calls=%fused_computation.12.clone.1 | loop fusion | flops 2801664 | bytes 592512 | tf_op jit(solution)/shard_map/while/body/jit(_where)/select_n | solution.py:44
  54.4 0.4 multiply_reduce_fusion.6
  54.8 0.3 bitcast_dynamic-update-slice_fusion.2
  55.0 0.3 convolution_add_fusion.2
  55.4 0.3 reshape.511
  55.8 28.7 %collective-permute-start.2 = (bf16[64,2,128]{2,1,0:T(2,128)(2,1)S(1)}, bf16[64,2,128]{2,1,0:T(2,128)(2,1)S(1)}, u32[]{:S(2)}, u32[]{:S(2)}) collective-permute-start(bf16[64,2,128]{2,1,0:T(2,128)(2,1)S(1)} %slice.281), channel_id=1, source_target_pairs={{0,1},{1,2},{2,3},{3,4},{4,5},{5,6},{6,7},{7,8},{8,9},{9,10},{10,1... | collective-permute-start | bytes 98312 | tf_op jit(solution)/shard_map/ppermute | solution.py:14
  84.5 0.3 slice_subtract_fusion
  84.8 0.1 slice.271
  84.9 1.2 collective-permute-done.2
  86.1 1.9 %multiply_reduce_fusion.3 = (f32[]{:T(128)}, f32[64,2,1024]{2,1,0:T(2,128)}) fusion(f32[64,2,896]{2,1,0:T(2,128)S(1)} %slice.271, f32[64,2,128]{2,1,0:T(2,128)S(1)} %slice_subtract_fusion.1), kind=kLoop, calls=%fused_computation.41 | loop fusion | flops 393215 | bytes 1048580 | tf_op jit(solution)/shard_map/reduce_sum | solution.py:140
  88.7 40.1 %all-reduce = (f32[8]{0:T(128)S(1)}, f32[8,8]{0,1:T(8,128)S(1)}) all-reduce(f32[8]{0:T(128)S(1)} %broadcast_multiply_fusion.2, f32[8,8]{0,1:T(8,128)S(1)} %broadcast_multiply_fusion.1), channel_id=1, replica_groups=mesh['group'=4,'shard'=8] {'group','shard'}, use_global_device_ids=true, to_apply=%region_7.8 | all-reduce | flops 72 | bytes 576 | tf_op jit(solution)/shard_map/psum | solution.py:145
  128.8 0.1 copy.62
  128.9 0.7 cholesky.18
  129.6 0.6 compare_reduce_fusion
  130.3 0.6 select_select_fusion
  130.9 0.7 fusion.18
  131.6 0.7 fusion.17
  132.4 0.7 fusion.19
  183.7 0.1 stack.91
  183.8 0.6 multiply_reduce_fusion.4
  (21 shorter events, 0.3 us)
Async XLA Ops:
  16.0 8.4 %copy-start.2 = (bf16[1024]{0:T(1024)(128)(2,1)S(1)}, bf16[1024]{0:T(1024)(128)(2,1)}, u32[]{:S(2)}) copy-start(bf16[1024]{0:T(1024)(128)(2,1)} %param.13) | copy-start | bytes 6148
  17.1 21.8 %all-to-all-start = ((bf16[16,2,8,1024]{3,0,1,2:T(8,128)(2,1)}), bf16[16,2,8,1024]{3,0,1,2:T(8,128)(2,1)S(1)}, u32[]{:S(2)}, u32[]{:S(2)}) async-start(bf16[16,2,8,1024]{3,0,1,2:T(8,128)(2,1)} %copy.60), calls=%async_computation | async-start | bytes 1048576 | tf_op jit(solution)/shard_map/all_to_all | solution.py:89
  24.4 18.0 %collective-permute-start.1 = (bf16[128]{0:T(256)(128)(2,1)S(1)}, bf16[128]{0:T(256)(128)(2,1)S(1)}, u32[]{:S(2)}, u32[]{:S(2)}) collective-permute-start(bf16[128]{0:T(256)(128)(2,1)S(1)} %slice.218), channel_id=1, source_target_pairs={{1,0},{2,1},{3,2},{4,3},{5,4},{6,5},{7,6},{8,7},{9,8},{10,9},{11,1... | collective-permute-start | bytes 776 | tf_op jit(solution)/shard_map/ppermute | solution.py:14
  39.8 1.0 copy-start.1
  41.0 5.8 %collective-permute-start = (bf16[64,2,128]{2,1,0:T(2,128)(2,1)S(1)}, bf16[64,2,128]{2,1,0:T(2,128)(2,1)S(1)}, u32[]{:S(2)}, u32[]{:S(2)}) collective-permute-start(bf16[64,2,128]{2,1,0:T(2,128)(2,1)S(1)} %slice.267), channel_id=1, source_target_pairs={{1,0},{2,1},{3,2},{4,3},{5,4},{6,5},{7,6},{8,7},{9,8},{10,9},{11,1... | collective-permute-start | bytes 98312 | tf_op jit(solution)/shard_map/ppermute | solution.py:14
  55.4 29.4 %copy-start = (f32[64,512]{1,0:T(8,128)}, f32[64,512]{1,0:T(8,128)S(1)}, u32[]{:S(2)}) copy-start(f32[64,512]{1,0:T(8,128)S(1)} %get-tuple-element.184) | copy-start | bytes 393220
  55.8 30.3 %collective-permute-start.2 = (bf16[64,2,128]{2,1,0:T(2,128)(2,1)S(1)}, bf16[64,2,128]{2,1,0:T(2,128)(2,1)S(1)}, u32[]{:S(2)}, u32[]{:S(2)}) collective-permute-start(bf16[64,2,128]{2,1,0:T(2,128)(2,1)S(1)} %slice.281), channel_id=1, source_target_pairs={{0,1},{1,2},{2,3},{3,4},{4,5},{5,6},{6,7},{7,8},{8,9},{9,10},{10,1... | collective-permute-start | bytes 98312 | tf_op jit(solution)/shard_map/ppermute | solution.py:14
where the time goes:
time: 186 us; the launch traced here: 184 us
  between operations  53 us (28%)
  blocking collectives  40.1 us (22%)
  starting transfers between devices  38.6 us (21%)
  other arithmetic  25.2 us (14%)
  waiting for transfers between devices  18 us (10%)
  local copies, waits for them, and re-layouts  8.89 us (5%)
    psum x1, blocking collectives, local(): lax.psum((basis[:, None] * basis[None, :], basis * log_power), ('group',...  40.1 us
    ppermute x3, starting transfers between devices, shifted_2(): return lax.ppermute(x, axis, pairs)  31.3 us
    reduce_sum x1, other arithmetic, half_templates(): real_part = jnp.sum(amp_curve * jnp.cos(phase_curve), axis=1)  13.1 us
    all_to_all x1, waiting for transfers between devices, local(): lax.all_to_all(local_halves, 'shard', split_axis=2, concat_axis=0, tiled=...  12.3 us
    all_to_all x1, starting transfers between devices, local(): lax.all_to_all(local_halves, 'shard', split_axis=2, concat_axis=0, tiled=...  7.28 us
    ppermute x3, waiting for transfers between devices, shifted_2(): return lax.ppermute(x, axis, pairs)  5.7 us
    select_n x1, other arithmetic, make_wave(): jnp.where(inside, amplitude[:, None] * envelope * jnp.cos(phase_angle), 0.0)  4.45 us
  transfers between devices with their start and end apart: 4, of which 3 were waited for; matrix products, arithmetic and copies ran while one was open for 1% of the time, Pallas kernels for 0%

commit v1 on v0

v1 whole, which is shorter than its diff:
```python
import functools
import math

import jax
import jax.numpy as jnp
import numpy as np
from jax import lax
from jax.experimental import pallas as pl
from jax.experimental.pallas import tpu as pltpu
from jax.sharding import PartitionSpec as P

Q = 128
NCOEF = 8
LANES = 128
SUB = 8
F32 = jnp.float32
BF16 = jnp.bfloat16
BOTH = ("group", "shard")

INV_TAU = np.float32(1.0 / (2.0 * math.pi))
TAU_A = np.float32(round(2.0 * math.pi * 512) / 512)
TAU_B = np.float32(round((2.0 * math.pi - float(TAU_A)) * 2**22) / 2**22)
TAU_C = np.float32(2.0 * math.pi - float(TAU_A) - float(TAU_B))
MAGIC = np.float32(1.5 * 2**23)
SIN2 = (6.283185160089475, -10.33541375785372, 5.100062754574036, -1.1960903483123309, 0.15444025802555503)
COS1 = (0.9999999534666666, -4.934792858675247, 4.058411914166824, -1.3318801612473732, 0.2196967986012024)


def nearest(x):
    return (x + MAGIC) - MAGIC


def poly(y, coefs):
    total = np.float32(coefs[-1])
    for c in coefs[-2::-1]:
        total = total * y + np.float32(c)
    return total


def cis_turns(r):
    y = r * r
    s2 = poly(y, SIN2) * r
    c1 = poly(y, COS1)
    return np.float32(1.0) - np.float32(0.5) * (s2 * s2), s2 * c1


def turns(angle):
    n = nearest(angle * INV_TAU)
    return (((angle - n * TAU_A) - n * TAU_B) - n * TAU_C) * INV_TAU


def frac(t):
    return t - nearest(t)


def col(x, lane, rows=SUB):
    return jnp.broadcast_to(x[:, lane : lane + 1], (rows, LANES))


def lane_iota(rows=SUB):
    return lax.broadcasted_iota(jnp.int32, (rows, LANES), 1)


def pack_kernel(amp_ref, phase_ref, out_ref):
    harmonics, powers, _, rows = amp_ref.shape
    width = out_ref.shape[1] // (2 * powers)
    for which, ref in enumerate((amp_ref, phase_ref)):
        for power in range(powers):
            start = (which * powers + power) * width
            parts = [ref[h, power] for h in range(harmonics)]
            if width > harmonics * rows:
                parts.append(jnp.zeros((ref.shape[2], width - harmonics * rows), F32))
            out_ref[:, start : start + width] = jnp.concatenate(parts, axis=1)


def make_template(rec_ref, compact_ref, harmonics, rows, band_bins, first_block, block_count, emit):
    peers = rec_ref.shape[0]
    width = rec_ref.shape[1] // 6
    pairs = rows // 2
    share = LANES / band_bins
    p0, p1, p2 = (rec_ref[:, (3 + k) * width : (4 + k) * width] for k in range(3))
    f0 = turns(p0)
    f1 = turns(p1 * np.float32(share))
    f2 = turns(p2 * np.float32(share * share))
    kb = first_block
    lin = (p1 + p2 * np.float32(2 * kb * share)) * np.float32(1.0 / band_bins) * INV_TAU
    quad = p2 * np.float32(1.0 / band_bins**2) * INV_TAU
    step_const = f1 + np.float32(2 * kb + 1) * f2
    step_lin = p2 * np.float32(2 * share / band_bins) * INV_TAU
    twist_cos, twist_sin = cis_turns(frac(np.float32(2.0) * f2))
    entries = [
        rec_ref[:, 0:width],
        rec_ref[:, width : 2 * width],
        rec_ref[:, 2 * width : 3 * width],
        frac(f0 + np.float32(kb) * f1 + np.float32(kb * kb) * f2),
        lin,
        quad,
    ]
    if block_count > 1:
        entries += [frac(step_const), step_lin, twist_cos, twist_sin]
    for i, entry in enumerate(entries):
        compact_ref[i] = entry

    lane = lane_iota().astype(F32)
    lane_sq = lane * lane
    u = (lane + np.float32(kb * LANES)) * np.float32(1.0 / band_bins)
    u_sq = u * u
    grow = np.float32(share * share) + np.float32(2 * share) * u

    def block(step, _):
        which, pair = step // pairs, step % pairs
        shift = (width - 2 * pair) % width
        rolled = [
            pltpu.roll(compact_ref[i, pl.ds(which * SUB, SUB), :], shift, 1)
            if pairs > 1
            else compact_ref[i, pl.ds(which * SUB, SUB), :]
            for i in range(len(entries))
        ]
        total_re = [None] * block_count
        total_im = [None] * block_count
        for s in range(2):
            re = [None] * block_count
            im = [None] * block_count
            for h in range(harmonics):
                c = [col(x, h * rows + s) for x in rolled]
                a = c[0] + c[1] * u + c[2] * u_sq
                z_re, z_im = cis_turns(frac(c[3] + c[4] * lane + c[5] * lane_sq))
                if block_count > 1:
                    da = c[1] * np.float32(share) + c[2] * grow
                    dda = c[2] * np.float32(2 * share * share)
                    w_re, w_im = cis_turns(frac(c[6] + c[7] * lane))
                for k in range(block_count):
                    x, y = a * z_re, a * z_im
                    re[k] = x if h == 0 else re[k] + x
                    im[k] = y if h == 0 else im[k] + y
                    if k + 1 < block_count:
                        z_re, z_im = z_re * w_re - z_im * w_im, z_re * w_im + z_im * w_re
                        a = a + da
                    if k + 2 < block_count:
                        w_re, w_im = w_re * c[8] - w_im * c[9], w_re * c[9] + w_im * c[8]
                        da = da + dda
            for k in range(block_count):
                half_re = re[k].astype(BF16).astype(F32)
                half_im = im[k].astype(BF16).astype(F32)
                total_re[k] = half_re if s == 0 else total_re[k] + half_re
                total_im[k] = half_im if s == 0 else total_im[k] + half_im
        emit(pl.multiple_of(pair * peers + which * SUB, SUB), total_re, total_im)
        return 0

    lax.fori_loop(0, pairs * (peers // SUB), block, 0)


def first_kernel(harmonics, rows, rec_ref, data_ref, noise_ref, resid_ref, rim_ref, compact_ref):
    band_bins = data_ref.shape[1]
    walkers = resid_ref.shape[0]

    def emit(row, re, im):
        at = pl.ds(row, SUB)
        resid_ref[at, :LANES] = data_ref[0:1, :LANES] - re[0]
        resid_ref[at, LANES:] = data_ref[1:2, :LANES] - im[0]

    make_template(rec_ref, compact_ref, harmonics, rows, band_bins, 0, 1, emit)
    noise = noise_ref[0:1, :LANES]
    noise = jnp.concatenate([noise, noise], axis=1)
    rim_ref[:walkers, :] = (resid_ref[...] * noise).astype(BF16)
    rim_ref[walkers:, :] = jnp.broadcast_to(noise, (rim_ref.shape[0] - walkers, 2 * LANES)).astype(BF16)


def rest_kernel(
    harmonics, rows, rec_ref, data_ref, noise_ref, first_ref, rim_ref, resid_ref, weighted_ref, compact_ref
):
    band_bins = data_ref.shape[1]
    blocks = band_bins // LANES
    walkers = resid_ref.shape[0]

    def emit(row, re, im):
        at = pl.ds(row, SUB)
        for k in range(1, blocks):
            here = slice(k * LANES, (k + 1) * LANES)
            there = slice(band_bins + k * LANES, band_bins + (k + 1) * LANES)
            resid_ref[at, here] = data_ref[0:1, here] - re[k - 1]
            resid_ref[at, there] = data_ref[1:2, here] - im[k - 1]

    for part in range(2):
        there = slice(part * band_bins, part * band_bins + LANES)
        resid_ref[:, there] = first_ref[:, part * LANES : (part + 1) * LANES]
        weighted_ref[:, there] = rim_ref[:walkers, part * LANES : (part + 1) * LANES]
    make_template(rec_ref, compact_ref, harmonics, rows, band_bins, 1, blocks - 1, emit)
    for part in range(2):
        there = slice(part * band_bins + LANES, (part + 1) * band_bins)
        weighted_ref[:, there] = (resid_ref[:, there] * noise_ref[0:1, LANES:]).astype(BF16)


def fit_rows(band, bands):
    width = -(-bands // LANES) * LANES
    place = lax.broadcasted_iota(jnp.int32, (NCOEF, width), 1)
    order = lax.broadcasted_iota(jnp.int32, (NCOEF, width), 0)
    x = (2 * place + 1).astype(F32) * np.float32(1.0 / bands) - np.float32(1.0)
    term, after = jnp.ones_like(x), x
    basis = jnp.zeros_like(x)
    for degree in range(NCOEF):
        basis = jnp.where(order == degree, term, basis)
        term, after = after, np.float32(2.0) * x * after - term
    basis = jnp.where(place < bands, basis, 0.0)
    row = lax.broadcasted_iota(jnp.int32, (NCOEF, LANES), 0)
    lane = lax.broadcasted_iota(jnp.int32, (NCOEF, LANES), 1)
    gram = jnp.zeros((NCOEF, LANES), F32)
    for j in range(NCOEF):
        gram = jnp.where(lane == j, jnp.sum(basis * basis[j : j + 1, :], axis=1, keepdims=True), gram)
    side = basis
    for i in range(NCOEF):
        scale = np.float32(1.0) / jnp.sqrt(gram[i : i + 1, i : i + 1])
        upper = gram[i : i + 1, :] * scale
        factor = gram[:, i : i + 1] * scale
        solved = side[i : i + 1, :] * scale
        below = row > i
        gram = jnp.where(below, gram - factor * upper, jnp.where(row == i, upper, gram))
        side = jnp.where(order > i, side - factor * solved, jnp.where(order == i, solved, side))
    for i in reversed(range(NCOEF)):
        solved = side[i : i + 1, :] / gram[i : i + 1, i : i + 1]
        side = jnp.where(order < i, side - gram[:, i : i + 1] * solved, jnp.where(order == i, solved, side))
    mine = jnp.sum(jnp.where(place == band, side, 0.0), axis=1, keepdims=True)
    return jnp.sum(basis * mine, axis=0, keepdims=True)


def wave_kernel(
    bands, count_ref, band_ref, amp_ref, phase_ref, slope_ref, curve_ref, start_ref, noise_ref,
    wave_ref, power_ref, noise_out_ref, fit_ref, cols_ref,
):
    slots = amp_ref.shape[1]
    band_bins = noise_ref.shape[1]
    blocks = band_bins // LANES
    noise_out_ref[...] = noise_ref[...].astype(F32)
    live = lax.broadcasted_iota(jnp.int32, (1, slots), 1) < count_ref[0]
    start = start_ref[...]
    stacked = jnp.concatenate(
        [
            jnp.where(live, amp_ref[...], 0.0),
            phase_ref[...],
            slope_ref[...],
            curve_ref[...],
            (start % LANES).astype(F32),
            (start // LANES).astype(F32),
            jnp.zeros((2, slots), F32),
        ],
        axis=0,
    )
    cols_ref[...] = jnp.concatenate([stacked.T, jnp.zeros((slots, LANES - SUB), F32)], axis=1)
    rows = 2 * SUB
    lane = lane_iota(rows).astype(F32)

    def block(step, _):
        at = pl.ds(pl.multiple_of(step * rows, rows), rows)
        params = cols_ref[at, :]
        amp, phase, slope, curve, low, high = (col(params, i, rows) for i in range(6))
        offset = lane - low
        wrapped = offset < 0.0
        j = jnp.where(wrapped, offset + np.float32(Q), offset)
        home = jnp.where(wrapped, high + 1.0, high)
        angle = phase + slope * j + curve * j * j
        c, s = cis_turns(turns(angle))
        y = (j + np.float32(0.5)) * np.float32(1.0 / Q) - np.float32(0.5)
        envelope = poly(y * y, COS1)
        scale = amp * (envelope * envelope)
        re = (scale * c).astype(BF16).astype(F32)
        im = (scale * s).astype(BF16).astype(F32)
        noise = jnp.zeros((rows, LANES), F32)
        for k in range(blocks):
            inside = home == np.float32(k)
            noise = jnp.where(inside, noise_out_ref[0:1, k * LANES : (k + 1) * LANES], noise)
            wave_ref[at, k * LANES : (k + 1) * LANES] = jnp.where(inside, re, 0.0).astype(BF16)
            wave_ref[at, band_bins + k * LANES : band_bins + (k + 1) * LANES] = jnp.where(inside, im, 0.0).astype(BF16)
        inside = home == np.float32(blocks)
        wave_ref[at, 2 * band_bins : 2 * band_bins + LANES] = jnp.where(inside, re, 0.0).astype(BF16)
        wave_ref[at, 2 * band_bins + LANES :] = jnp.where(inside, im, 0.0).astype(BF16)
        power_ref[at, :] = (re * re + im * im) * noise
        return 0

    lax.fori_loop(0, slots // rows, block, 0)
    fit = fit_rows(band_ref[0], bands)
    fit = jnp.broadcast_to(fit, (SUB, fit.shape[1])).T
    fit_ref[...] = jnp.broadcast_to(fit[:bands, 0:1], (bands, LANES))


def score_kernel(count_ref, weighted_ref, rim_ref, wave_ref, power_ref, accept_ref, half_ref, carry_ref):
    walkers, own = weighted_ref.shape
    slots = wave_ref.shape[0]
    over_lanes = (((1,), (1,)), ((), ()))
    corr = lax.dot_general(weighted_ref[...], wave_ref[:, :own], over_lanes, preferred_element_type=F32)
    corr += lax.dot_general(rim_ref[:walkers, :], wave_ref[:, own:], over_lanes, preferred_element_type=F32)
    rim = wave_ref[:, own:].astype(F32)
    re, im = rim[:, :LANES], rim[:, LANES:]
    noise = rim_ref[walkers : walkers + 2 * SUB, :LANES].astype(F32)[0:1]
    power = power_ref[...] + (re * re + im * im) * noise
    total = lax.dot_general(
        jnp.ones((SUB, LANES), F32), power, over_lanes, precision=lax.Precision.HIGHEST, preferred_element_type=F32
    )
    live = lax.broadcasted_iota(jnp.int32, (walkers, slots), 1) < count_ref[0]
    accept = jnp.where(live, jax.nn.sigmoid(corr - np.float32(0.5) * total[0:1, :]), 0.0)
    accept_ref[...] = accept
    half = accept.astype(BF16)
    half_ref[...] = half
    carry_ref[...] = jnp.dot(half, wave_ref[:, own:], preferred_element_type=F32).astype(BF16)


def update_kernel(half_ref, wave_ref, resid_ref, new_ref, squares_ref):
    walkers, own = resid_ref.shape
    half = half_ref[...]
    squares = jnp.zeros((walkers, LANES), F32)
    chunk = 2 * LANES
    for start in range(0, own, chunk):
        here = slice(start, start + chunk)
        new = resid_ref[:, here] - jnp.dot(half, wave_ref[:, here], preferred_element_type=F32)
        new_ref[:, here] = new
        for lane in range(0, chunk, LANES):
            if (start + lane) % (own // 2):
                squares += new[:, lane : lane + LANES] * new[:, lane : lane + LANES]
    squares_ref[...] = squares


def power_kernel(new_ref, carry_ref, squares_ref, edge_ref, log_ref):
    walkers, own = new_ref.shape
    total = squares_ref[...]
    for part in range(2):
        lanes = slice(part * LANES, (part + 1) * LANES)
        start = part * (own // 2)
        edge = new_ref[:, start : start + LANES] - carry_ref[:, lanes].astype(F32)
        edge_ref[:, lanes] = edge
        total += edge * edge
    total = jnp.sum(jnp.sum(total, axis=0, keepdims=True), axis=1, keepdims=True)
    log_power = jnp.log(total * np.float32(1.0 / (walkers * own)) + np.float32(1e-6))
    log_ref[...] = jnp.broadcast_to(log_power, log_ref.shape)


def output_kernel(peers, accept_ref, new_ref, edge_ref, prob_ref, out_ref):
    walkers, own = new_ref.shape
    pairs = walkers // peers
    half = own // 2

    def in_order(x):
        if pairs == 1:
            return x
        return jnp.swapaxes(x.reshape(pairs, peers, x.shape[1]), 0, 1).reshape(x.shape)

    prob_ref[...] = in_order(accept_ref[...])
    for part in range(2):
        out_ref[:, part, :LANES] = in_order(edge_ref[:, part * LANES : (part + 1) * LANES])
        out_ref[:, part, LANES:] = in_order(new_ref[:, part * half + LANES : (part + 1) * half])


def call(kernel, outs, args, scratch=(), smem=0, flops=0, name=None):
    vmem = pl.BlockSpec(memory_space=pltpu.VMEM)
    return pl.pallas_call(
        kernel,
        out_shape=outs,
        in_specs=[pl.BlockSpec(memory_space=pltpu.SMEM)] * smem + [vmem] * (len(args) - smem),
        out_specs=[vmem] * len(outs),
        scratch_shapes=scratch,
        compiler_params=pltpu.CompilerParams(vmem_limit_bytes=32 * 2**20),
        cost_estimate=pl.CostEstimate(flops=flops, bytes_accessed=2**20, transcendentals=0),
        name=name,
    )(*args)


def shape(dims, dtype):
    return jax.ShapeDtypeStruct(dims, dtype)


def moved(x, by):
    devices = lax.axis_size(BOTH)
    return lax.ppermute(x, BOTH, [(i, i + by) for i in range(devices) if 0 <= i + by < devices])


def local(
    data,
    inv_noise,
    mbh_amp,
    mbh_phase,
    bin_amp,
    bin_phase,
    bin_slope,
    bin_curve,
    bin_start,
    bin_count,
):
    band_bins = data.shape[1]
    slots = bin_amp.shape[1]
    rows, harmonics, powers, peers = mbh_amp.shape
    walkers = rows * peers // 2
    bands = lax.axis_size(BOTH)
    band = lax.axis_index(BOTH).astype(jnp.int32)[None]
    own = 2 * band_bins

    def padded(count):
        return -(-count // LANES) * LANES

    (packed,) = call(
        pack_kernel,
        [shape((peers, 2 * powers * padded(harmonics * rows)), F32)],
        [mbh_amp.transpose(1, 2, 3, 0), mbh_phase.transpose(1, 2, 3, 0)],
        name="pack",
    )
    received = lax.all_to_all(packed, "shard", split_axis=0, concat_axis=0, tiled=True)
    if rows % 2:
        pieces = received.reshape(peers // 2, 2, 2 * powers, -1)[..., : harmonics * rows]
        pieces = pieces.reshape(peers // 2, 2, 2 * powers, harmonics, rows).transpose(0, 2, 3, 1, 4)
        rows, peers = 2 * rows, peers // 2
        pieces = pieces.reshape(peers, 2 * powers, harmonics * rows)
        pieces = jnp.pad(pieces, ((0, 0), (0, 0), (0, padded(harmonics * rows) - harmonics * rows)))
        received = pieces.reshape(peers, -1)
    width = received.shape[1] // (2 * powers)

    wave, slot_power, noise, fit = call(
        functools.partial(wave_kernel, bands),
        [
            shape((slots, own + 2 * LANES), BF16),
            shape((slots, LANES), F32),
            shape((1, band_bins), F32),
            shape((bands, LANES), F32),
        ],
        [bin_count, band, bin_amp, bin_phase, bin_slope, bin_curve, bin_start, inv_noise[None, :]],
        scratch=[pltpu.VMEM((slots, LANES), F32)],
        smem=2,
        name="waves",
    )
    first, rim = call(
        functools.partial(first_kernel, harmonics, rows),
        [shape((walkers, 2 * LANES), F32), shape((walkers + 2 * SUB, 2 * LANES), BF16)],
        [received, data, noise],
        scratch=[pltpu.VMEM((10, peers, width), F32)],
        name="first_bins",
    )
    rim_next = moved(rim, -1)
    resid, weighted = call(
        functools.partial(rest_kernel, harmonics, rows),
        [shape((walkers, own), F32), shape((walkers, own), BF16)],
        [received, data, noise, first, rim],
        scratch=[pltpu.VMEM((10, peers, width), F32)],
        flops=10**9,
        name="other_bins",
    )
    accept, half, carry = call(
        score_kernel,
        [shape((walkers, slots), F32), shape((walkers, slots), BF16), shape((walkers, 2 * LANES), BF16)],
        [bin_count, weighted, rim_next, wave, slot_power],
        smem=1,
        name="scores",
    )
    carried = moved(carry, 1)
    updated, squares = call(
        update_kernel,
        [shape((walkers, own), F32), shape((walkers, LANES), F32)],
        [half, wave, resid],
        flops=10**9,
        name="update",
    )
    edge, log_power = call(
        power_kernel,
        [shape((walkers, 2 * LANES), F32), shape((bands, LANES), F32)],
        [updated, carried, squares],
        name="log_power",
    )
    log_powers = lax.all_to_all(log_power, BOTH, split_axis=0, concat_axis=0, tiled=True)
    accept_prob, residual_new = call(
        functools.partial(output_kernel, peers),
        [shape((walkers, slots), F32), shape((walkers, 2, band_bins), F32)],
        [accept, updated, edge],
        name="outputs",
    )
    noise_fit = jnp.sum(fit * log_powers, axis=0)[:1]
    return (accept_prob, residual_new, noise_fit)


def solution(mesh):
    in_specs = (
        P(None, BOTH),
        P(BOTH),
        P("shard", None, None, "group"),
        P("shard", None, None, "group"),
        P(BOTH, None),
        P(BOTH, None),
        P(BOTH, None),
        P(BOTH, None),
        P(BOTH, None),
        P(BOTH),
    )
    out_specs = (P(None, BOTH), P(None, None, BOTH), P(BOTH))
    return jax.shard_map(local, mesh=mesh, in_specs=in_specs, out_specs=out_specs, check_vma=False)
```

time: 186 us -> 52.7 us (0.28)
  between operations: 53 us -> 1.37 us
  blocking collectives: 40.1 us -> 0 us
  other arithmetic: 25.2 us -> 0.53 us
  starting transfers between devices: 38.6 us -> 20.9 us
  Pallas kernels: 0 us -> 14 us
  waiting for transfers between devices: 18 us -> 8.16 us
    psum x1 -> x0, blocking collectives: 40.1 us -> none  [local(): lax.psum((basis[:, None] * basis[None, :], basis * log_power), ('group',...]
    ppermute x3 -> x2, starting transfers between devices: 31.3 us -> 6.11 us  [moved(): lax.ppermute(x, BOTH, [(i, i + by) for i in range(devices) if 0 <= i + by...]
    reduce_sum x5 -> x1, other arithmetic: 17 us -> 0.53 us  [local(): noise_fit = jnp.sum(fit * log_powers, axis=0)[:1]]
    pallas_call x0 -> x8, Pallas kernels: none -> 14 us  [call(): pl.pallas_call(kernel, out_shape=outs, in_specs=[pl.BlockSpec(memory_spac...]
    all_to_all x1 -> x2, starting transfers between devices: 7.28 us -> 14.8 us  [the longest x1 7.53 us: local(): lax.all_to_all(log_power, BOTH, split_axis=0, concat_axis=0, tiled=True)]
    all_to_all x1 -> x2, waiting for transfers between devices: 12.3 us -> 6.07 us  [the longest x1 6.07 us: local(): lax.all_to_all(log_power, BOTH, split_axis=0, concat_axis=0, tiled=True)]
    unnamed x7 -> x17, local copies, waits for them, and re-layouts: 0.05 us -> 5.89 us
    select_n x2 -> x0, other arithmetic: 5.09 us -> none  [the longest x1 4.45 us: make_wave(): jnp.where(inside, amplitude[:, None] * envelope * jnp.cos(phase_angle), 0.0)]
  transfers between devices with their start and end apart: 4 -> 4, of which waited for: 3 -> 3; matrix products, arithmetic and copies ran while one was open for 1% -> 1% of each run, Pallas kernels for 0% -> 19%
where the time goes in v1:
time: 52.7 us; the launch traced here: 52.2 us
  starting transfers between devices  20.9 us (40%)
  Pallas kernels  14 us (27%)
  waiting for transfers between devices  8.16 us (15%)
  local copies, waits for them, and re-layouts  7.21 us (14%)
  between operations  1.37 us (3%)
  other arithmetic  0.53 us (1%)
    pallas_call x8, Pallas kernels, call(): pl.pallas_call(kernel, out_shape=outs, in_specs=[pl.BlockSpec(memory_spac...  14 us
    all_to_all x1, starting transfers between devices, local(): lax.all_to_all(log_power, BOTH, split_axis=0, concat_axis=0, tiled=True)  7.53 us
    all_to_all x1, starting transfers between devices, local(): lax.all_to_all(packed, 'shard', split_axis=0, concat_axis=0, tiled=True)  7.28 us
    ppermute x2, starting transfers between devices, moved(): lax.ppermute(x, BOTH, [(i, i + by) for i in range(devices) if 0 <= i + by...  6.11 us
    all_to_all x1, waiting for transfers between devices, local(): lax.all_to_all(log_power, BOTH, split_axis=0, concat_axis=0, tiled=True)  6.07 us
    unnamed x17, local copies, waits for them, and re-layouts  5.89 us
    ppermute x2, waiting for transfers between devices, moved(): lax.ppermute(x, BOTH, [(i, i + by) for i in range(devices) if 0 <= i + by...  2.09 us
  transfers between devices with their start and end apart: 4, of which 3 were waited for; matrix products, arithmetic and copies ran while one was open for 1% of the time, Pallas kernels for 19%

profile of v1, /device:TPU:0, one launch (start us, length us, event | category | flops | bytes accessed | tf_op | source)
XLA Modules:
  0.0 52.2 jit_solution(3303049120115390672)
XLA Ops:
  0.6 0.0 copy-start
  0.6 0.9 %copy-done = f32[16,6,3,8]{0,3,2,1:T(8,128)S(1)} copy-done((f32[16,6,3,8]{0,3,2,1:T(8,128)S(1)}, f32[16,6,3,8]{0,3,2,1:T(8,128)}, u32[]{:S(2)}) %copy-start) | copy-done | bytes 9240
  1.5 0.0 copy-start.1
  1.5 0.9 %copy-done.1 = f32[16,6,3,8]{0,3,2,1:T(8,128)S(1)} copy-done((f32[16,6,3,8]{0,3,2,1:T(8,128)S(1)}, f32[16,6,3,8]{0,3,2,1:T(8,128)}, u32[]{:S(2)}) %copy-start.1) | copy-done | bytes 9240
  2.4 0.1 pack.1
  2.5 0.6 %copy.13 = f32[8,1,768]{2,1,0:T(1,128)} copy(f32[8,1,768]{2,0,1:T(8,128)S(1)} %bitcast.14) | data formatting | bytes 49152 | tf_op jit(solution)/shard_map/all_to_all | solution.py:403
  3.1 7.3 %all-to-all-start = ((f32[8,1,768]{2,1,0:T(1,128)}), f32[8,1,768]{2,1,0:T(1,128)S(1)}, u32[]{:S(2)}, u32[]{:S(2)}) async-start(f32[8,1,768]{2,1,0:T(1,128)} %copy.13), calls=%async_computation | async-start | bytes 49152 | tf_op jit(solution)/shard_map/all_to_all | solution.py:403
  11.1 0.7 %broadcast_in_dim.7.noise_ref = bf16[1,1024]{1,0:T(2,128)(2,1)S(1)} reshape(bf16[1024]{0:T(1024)(128)(2,1)} %param.11) | data formatting | bytes 4096 | tf_op jit(solution)/shard_map/broadcast_in_dim | solution.py:421
  11.8 0.0 copy-start.3
  11.8 0.7 %copy-done.3 = f32[1,512]{1,0:T(1,128)S(1)} copy-done((f32[1,512]{1,0:T(1,128)S(1)}, f32[1,512]{1,0:T(1,128)}, u32[]{:S(2)}) %copy-start.3) | copy-done | bytes 2072
  12.4 0.0 copy-start.4
  12.4 0.7 %copy-done.4 = f32[1,512]{1,0:T(1,128)S(1)} copy-done((f32[1,512]{1,0:T(1,128)S(1)}, f32[1,512]{1,0:T(1,128)}, u32[]{:S(2)}) %copy-start.4) | copy-done | bytes 2072
  13.1 0.0 copy-start.5
  13.1 0.7 %copy-done.5 = f32[1,512]{1,0:T(1,128)S(1)} copy-done((f32[1,512]{1,0:T(1,128)S(1)}, f32[1,512]{1,0:T(1,128)}, u32[]{:S(2)}) %copy-start.5) | copy-done | bytes 2072
  13.8 0.0 copy-start.6
  13.8 0.7 %copy-done.6 = f32[1,512]{1,0:T(1,128)S(1)} copy-done((f32[1,512]{1,0:T(1,128)S(1)}, f32[1,512]{1,0:T(1,128)}, u32[]{:S(2)}) %copy-start.6) | copy-done | bytes 2072
  14.5 0.0 copy-start.7
  14.5 0.7 %copy-done.7 = s32[1,512]{1,0:T(1,128)S(1)} copy-done((s32[1,512]{1,0:T(1,128)S(1)}, s32[1,512]{1,0:T(1,128)}, u32[]{:S(2)}) %copy-start.7) | copy-done | bytes 2072
  15.2 4.9 %waves.1 = (bf16[512,2304]{1,0:T(8,128)(2,1)S(1)}, f32[512,128]{1,0:T(8,128)S(1)}, f32[1,1024]{1,0:T(1,128)S(1)}, f32[32,128]{1,0:T(8,128)S(1)}) custom-call(s32[1]{0:T(128)S(6)} %copy.18.count_ref, s32[1]{0:T(128)} %bitcast.3.band_ref, f32[1,512]{1,0:T(1,128)S(1)} %copy-done.3, f32[1,512]{1,0:T(1,128)S(1)} %copy-done.4, f32[1,512]{1,0:T(1,128)S(1)} %copy-done.5, ...), custom_call_target="tpu_custom_call" | custom-call | bytes 1048576 | tf_op jit(solution)/shard_map/waves/pallas_call | solution.py:353
  20.1 0.0 all-to-all-done
  20.1 0.0 copy-start.2
  20.1 0.7 %copy-done.2 = f32[2,1024]{1,0:T(2,128)S(1)} copy-done((f32[2,1024]{1,0:T(2,128)S(1)}, f32[2,1024]{1,0:T(2,128)}, u32[]{:S(2)}) %copy-start.2) | copy-done | bytes 8216
  20.8 2.0 %first_bins.1 = (f32[64,256]{1,0:T(8,128)S(1)}, bf16[80,256]{1,0:T(8,128)(2,1)S(1)}) custom-call(f32[8,768]{1,0:T(8,128)S(1)} %bitcast.12, f32[2,1024]{1,0:T(2,128)S(1)} %copy-done.2, f32[1,1024]{1,0:T(1,128)S(1)} %get-tuple-element.20.noise_ref), custom_call_target="tpu_custom_call" | custom-call | bytes 1048576 | tf_op jit(solution)/shard_map/first_bins/pallas_call | solution.py:353
  22.8 1.3 %collective-permute-start = (bf16[80,256]{1,0:T(8,128)(2,1)S(1)}, bf16[80,256]{1,0:T(8,128)(2,1)S(1)}, u32[]{:S(2)}, u32[]{:S(2)}) collective-permute-start(bf16[80,256]{1,0:T(8,128)(2,1)S(1)} %get-tuple-element.22.rim_ref), channel_id=1, source_target_pairs={{1,0},{2,1},{3,2},{4,3},{5,4},{6,5},{7,6},{8,7},{9,8},{10,9},{11,1... | collective-permute-start | bytes 122888 | tf_op jit(solution)/shard_map/ppermute | solution.py:371
  24.1 3.6 %other_bins.1 = (f32[64,2048]{1,0:T(8,128)S(1)}, bf16[64,2048]{1,0:T(8,128)(2,1)S(1)}) custom-call(f32[8,768]{1,0:T(8,128)S(1)} %bitcast.13, f32[2,1024]{1,0:T(2,128)S(1)} %copy-done.2, f32[1,1024]{1,0:T(1,128)S(1)} %get-tuple-element.20.noise_ref, f32[64,256]{1,0:T(8,128)S(1)} %get-tuple-element.21.first_ref, bf16[80,256]{1,0:T(8,128)(2,1)S(1)} %get-tuple-element.22.rim_ref), custom_call_target="tpu_custom_call" | custom-call | flops 1000000000 | bytes 1048576 | tf_op jit(solution)/shard_map/other_bins/pallas_call | solution.py:353
  27.7 1.0 %collective-permute-done.rim_ref = bf16[80,256]{1,0:T(8,128)(2,1)S(1)} collective-permute-done((bf16[80,256]{1,0:T(8,128)(2,1)S(1)}, bf16[80,256]{1,0:T(8,128)(2,1)S(1)}, u32[]{:S(2)}, u32[]{:S(2)}) %collective-permute-start) | collective-permute-done | bytes 40992 | tf_op jit(solution)/shard_map/ppermute | solution.py:371
  28.7 1.2 %scores.1 = (f32[64,512]{1,0:T(8,128)S(1)}, bf16[64,512]{1,0:T(8,128)(2,1)S(1)}, bf16[64,256]{1,0:T(8,128)(2,1)S(1)}) custom-call(s32[1]{0:T(128)S(6)} %copy.18.count_ref, bf16[64,2048]{1,0:T(8,128)(2,1)S(1)} %get-tuple-element.23.weighted_ref, bf16[80,256]{1,0:T(8,128)(2,1)S(1)} %collective-permute-done.rim_ref, ...), custom_call_target="tpu_custom_call" | custom-call | bytes 1048576 | tf_op jit(solution)/shard_map/scores/pallas_call | solution.py:353
  29.9 4.8 %collective-permute-start.1 = (bf16[64,256]{1,0:T(8,128)(2,1)S(1)}, bf16[64,256]{1,0:T(8,128)(2,1)S(1)}, u32[]{:S(2)}, u32[]{:S(2)}) collective-permute-start(bf16[64,256]{1,0:T(8,128)(2,1)S(1)} %get-tuple-element.30), channel_id=1, source_target_pairs={{0,1},{1,2},{2,3},{3,4},{4,5},{5,6},{6,7},{7,8},{8,9},{9,10},{10,1... | collective-permute-start | bytes 98312 | tf_op jit(solution)/shard_map/ppermute | solution.py:371
  34.7 0.5 update.1
  35.2 1.1 %collective-permute-done.1.carry_ref = bf16[64,256]{1,0:T(8,128)(2,1)S(1)} collective-permute-done((bf16[64,256]{1,0:T(8,128)(2,1)S(1)}, bf16[64,256]{1,0:T(8,128)(2,1)S(1)}, u32[]{:S(2)}, u32[]{:S(2)}) %collective-permute-start.1) | collective-permute-done | bytes 32800 | tf_op jit(solution)/shard_map/ppermute | solution.py:371
  36.3 0.7 %log_power.1 = (f32[64,256]{1,0:T(8,128)S(1)}, f32[32,128]{1,0:T(8,128)}) custom-call(f32[64,2048]{1,0:T(8,128)S(1)} %get-tuple-element.29.new_ref, bf16[64,256]{1,0:T(8,128)(2,1)S(1)} %collective-permute-done.1.carry_ref, f32[64,128]{1,0:T(8,128)S(1)} %get-tuple-element.31.squares_ref), custom_call_target="tpu_custom_call" | custom-call | bytes 1048576 | tf_op jit(solution)/shard_map/log_power/pallas_call | solution.py:353
  37.0 7.5 %all-to-all-start.1 = ((f32[32,1,128]{2,1,0:T(1,128)}), f32[32,1,128]{2,1,0:T(1,128)S(1)}, u32[]{:S(2)}, u32[]{:S(2)}) async-start(f32[32,1,128]{2,1,0:T(1,128)} %bitcast.5), calls=%async_computation.1 | async-start | bytes 32768 | tf_op jit(solution)/shard_map/all_to_all | solution.py:463
  44.6 1.0 %outputs.1 = (f32[64,512]{1,0:T(8,128)}, f32[64,2,1024]{2,1,0:T(2,128)}) custom-call(f32[64,512]{1,0:T(8,128)S(1)} %get-tuple-element.26.accept_ref, f32[64,2048]{1,0:T(8,128)S(1)} %get-tuple-element.29.new_ref, f32[64,256]{1,0:T(8,128)S(1)} %get-tuple-element.32.edge_ref), custom_call_target="tpu_custom_call" | custom-call | bytes 1048576 | tf_op jit(solution)/shard_map/outputs/pallas_call | solution.py:353
  45.6 6.1 %all-to-all-done.1 = f32[32,1,128]{2,1,0:T(1,128)S(1)} async-done(((f32[32,1,128]{2,1,0:T(1,128)}), f32[32,1,128]{2,1,0:T(1,128)S(1)}, u32[]{:S(2)}, u32[]{:S(2)}) %all-to-all-start.1) | async-done | bytes 16416 | tf_op jit(solution)/shard_map/all_to_all | solution.py:463
  51.7 0.5 %multiply_reduce_fusion = f32[128]{0:T(128)} fusion(f32[32,128]{1,0:T(8,128)S(1)} %get-tuple-element.35, f32[32,128]{1,0:T(8,128)S(1)} %bitcast.17), kind=kLoop, calls=%fused_computation.1 | loop fusion | flops 8064 | bytes 33280 | tf_op jit(solution)/shard_map/reduce_sum | solution.py:470
  (1 shorter events, 0.0 us)
Async XLA Ops:
  0.6 0.9 %copy-start = (f32[16,6,3,8]{0,3,2,1:T(8,128)S(1)}, f32[16,6,3,8]{0,3,2,1:T(8,128)}, u32[]{:S(2)}) copy-start(f32[16,6,3,8]{0,3,2,1:T(8,128)} %param.12) | copy-start | bytes 27652
  1.5 0.9 %copy-start.1 = (f32[16,6,3,8]{0,3,2,1:T(8,128)S(1)}, f32[16,6,3,8]{0,3,2,1:T(8,128)}, u32[]{:S(2)}) copy-start(f32[16,6,3,8]{0,3,2,1:T(8,128)} %param.13) | copy-start | bytes 27652
  3.1 16.9 %all-to-all-start = ((f32[8,1,768]{2,1,0:T(1,128)}), f32[8,1,768]{2,1,0:T(1,128)S(1)}, u32[]{:S(2)}, u32[]{:S(2)}) async-start(f32[8,1,768]{2,1,0:T(1,128)} %copy.13), calls=%async_computation | async-start | bytes 49152 | tf_op jit(solution)/shard_map/all_to_all | solution.py:403
  11.8 0.7 %copy-start.3 = (f32[1,512]{1,0:T(1,128)S(1)}, f32[1,512]{1,0:T(1,128)}, u32[]{:S(2)}) copy-start(f32[1,512]{1,0:T(1,128)} %amp_ref.1) | copy-start | bytes 6148
  12.4 0.7 %copy-start.4 = (f32[1,512]{1,0:T(1,128)S(1)}, f32[1,512]{1,0:T(1,128)}, u32[]{:S(2)}) copy-start(f32[1,512]{1,0:T(1,128)} %phase_ref.1) | copy-start | bytes 6148
  13.1 0.7 %copy-start.5 = (f32[1,512]{1,0:T(1,128)S(1)}, f32[1,512]{1,0:T(1,128)}, u32[]{:S(2)}) copy-start(f32[1,512]{1,0:T(1,128)} %slope_ref.1) | copy-start | bytes 6148
  13.8 0.7 %copy-start.6 = (f32[1,512]{1,0:T(1,128)S(1)}, f32[1,512]{1,0:T(1,128)}, u32[]{:S(2)}) copy-start(f32[1,512]{1,0:T(1,128)} %curve_ref.1) | copy-start | bytes 6148
  14.5 0.7 %copy-start.7 = (s32[1,512]{1,0:T(1,128)S(1)}, s32[1,512]{1,0:T(1,128)}, u32[]{:S(2)}) copy-start(s32[1,512]{1,0:T(1,128)} %start_ref.1) | copy-start | bytes 6148
  20.1 0.7 %copy-start.2 = (f32[2,1024]{1,0:T(2,128)S(1)}, f32[2,1024]{1,0:T(2,128)}, u32[]{:S(2)}) copy-start(f32[2,1024]{1,0:T(2,128)} %data_ref.3) | copy-start | bytes 24580
  22.8 5.9 %collective-permute-start = (bf16[80,256]{1,0:T(8,128)(2,1)S(1)}, bf16[80,256]{1,0:T(8,128)(2,1)S(1)}, u32[]{:S(2)}, u32[]{:S(2)}) collective-permute-start(bf16[80,256]{1,0:T(8,128)(2,1)S(1)} %get-tuple-element.22.rim_ref), channel_id=1, source_target_pairs={{1,0},{2,1},{3,2},{4,3},{5,4},{6,5},{7,6},{8,7},{9,8},{10,9},{11,1... | collective-permute-start | bytes 122888 | tf_op jit(solution)/shard_map/ppermute | solution.py:371
  29.9 6.4 %collective-permute-start.1 = (bf16[64,256]{1,0:T(8,128)(2,1)S(1)}, bf16[64,256]{1,0:T(8,128)(2,1)S(1)}, u32[]{:S(2)}, u32[]{:S(2)}) collective-permute-start(bf16[64,256]{1,0:T(8,128)(2,1)S(1)} %get-tuple-element.30), channel_id=1, source_target_pairs={{0,1},{1,2},{2,3},{3,4},{4,5},{5,6},{6,7},{7,8},{8,9},{9,10},{10,1... | collective-permute-start | bytes 98312 | tf_op jit(solution)/shard_map/ppermute | solution.py:371
  37.0 14.7 %all-to-all-start.1 = ((f32[32,1,128]{2,1,0:T(1,128)}), f32[32,1,128]{2,1,0:T(1,128)S(1)}, u32[]{:S(2)}, u32[]{:S(2)}) async-start(f32[32,1,128]{2,1,0:T(1,128)} %bitcast.5), calls=%async_computation.1 | async-start | bytes 32768 | tf_op jit(solution)/shard_map/all_to_all | solution.py:463

commit v2 on v1

v2 whole, which is shorter than its diff:
```python
import functools
import math

import jax
import jax.numpy as jnp
import numpy as np
from jax import lax
from jax.experimental import pallas as pl
from jax.experimental.pallas import tpu as pltpu
from jax.sharding import PartitionSpec as P

Q = 128
NCOEF = 8
LANES = 128
SUB = 8
F32 = jnp.float32
BF16 = jnp.bfloat16
BOTH = ("group", "shard")
UNROLL = 2

INV_TAU = np.float32(1.0 / (2.0 * math.pi))
TAU_A = np.float32(round(2.0 * math.pi * 512) / 512)
TAU_B = np.float32(round((2.0 * math.pi - float(TAU_A)) * 2**22) / 2**22)
TAU_C = np.float32(2.0 * math.pi - float(TAU_A) - float(TAU_B))
MAGIC = np.float32(1.5 * 2**23)
SIN2 = (6.283185160089475, -10.33541375785372, 5.100062754574036, -1.1960903483123309, 0.15444025802555503)
COS1 = (0.9999999534666666, -4.934792858675247, 4.058411914166824, -1.3318801612473732, 0.2196967986012024)


def nearest(x):
    return (x + MAGIC) - MAGIC


def poly(y, coefs):
    total = np.float32(coefs[-1])
    for c in coefs[-2::-1]:
        total = total * y + np.float32(c)
    return total


def cis_turns(r):
    y = r * r
    s2 = poly(y, SIN2) * r
    c1 = poly(y, COS1)
    return np.float32(1.0) - np.float32(0.5) * (s2 * s2), s2 * c1


def turns(angle):
    n = nearest(angle * INV_TAU)
    return (((angle - n * TAU_A) - n * TAU_B) - n * TAU_C) * INV_TAU


def frac(t):
    return t - nearest(t)


def col(x, lane, rows=SUB):
    return jnp.broadcast_to(x[:, lane : lane + 1], (rows, LANES))


def lane_iota(rows=SUB):
    return lax.broadcasted_iota(jnp.int32, (rows, LANES), 1)


def pack_kernel(
    place_ref, amp_hbm, phase_hbm, data_hbm, noise_hbm, bin_amp_hbm, bin_phase_hbm, bin_slope_hbm, bin_curve_hbm,
    bin_start_hbm, count_hbm, packed_ref, bins_ref, data_ref, noise_ref,
    amp_ref, phase_ref, rows_ref, start_ref, raw_noise_ref, count_ref, sems,
):
    copies = [
        pltpu.make_async_copy(source, target, sems.at[i])
        for i, (source, target) in enumerate(
            [
                (amp_hbm, amp_ref),
                (phase_hbm, phase_ref),
                (count_hbm, count_ref),
                (bin_amp_hbm, rows_ref.at[0]),
                (bin_phase_hbm, rows_ref.at[1]),
                (bin_slope_hbm, rows_ref.at[2]),
                (bin_curve_hbm, rows_ref.at[3]),
                (bin_start_hbm, start_ref),
                (data_hbm, data_ref),
                (noise_hbm, raw_noise_ref),
            ]
        )
    ]
    for copy in copies:
        copy.start()
    harmonics, powers, peers, rows = amp_ref.shape
    width = -(-harmonics * rows // LANES) * LANES
    span = 2 * powers * width
    slots = bins_ref.shape[1]
    band_bins = data_ref.shape[1]
    for copy in copies[:2]:
        copy.wait()
    for which, ref in enumerate((amp_ref, phase_ref)):
        for power in range(powers):
            start = (which * powers + power) * width
            parts = [ref[h, power] for h in range(harmonics)]
            if width > harmonics * rows:
                parts.append(jnp.zeros((peers, width - harmonics * rows), F32))
            packed = jnp.concatenate(parts, axis=1)
            packed_ref[:, 0, start : start + width] = packed
            packed_ref[:, 0, span + start : span + start + width] = jnp.concatenate([packed[-1:], packed[:-1]], axis=0)
            packed_ref[:, 0, 2 * span + start : 2 * span + start + width] = jnp.concatenate(
                [packed[1:], packed[:1]], axis=0
            )
    for copy in copies[2:]:
        copy.wait()
    live = lax.broadcasted_iota(jnp.int32, (1, slots), 1) < count_ref[0]
    start = start_ref[...]
    amp = jnp.where(live, rows_ref[0], 0.0)
    rows = [amp, rows_ref[1], rows_ref[2], rows_ref[3], start.astype(F32)]
    bins_ref[...] = jnp.concatenate([*rows, live.astype(F32), jnp.zeros((2, slots), F32)], axis=0)
    raw_noise = raw_noise_ref[...].astype(F32)
    noise = jnp.concatenate([raw_noise[i : i + 1] for i in range(raw_noise.shape[0])], axis=1)
    noise_ref[...] = noise
    place = place_ref[0]
    after = lax.rem(place + 1, peers)
    before = lax.rem(place + peers - 1, peers)
    data = data_ref[...]
    for device, lanes, slot_rows in (
        (before, slice(0, LANES), []),
        (after, slice(band_bins - LANES, band_bins), rows),
    ):
        for i, row in enumerate([data[0:1, lanes], data[1:2, lanes], noise[:, lanes], *slot_rows]):
            start = 3 * span + (i * LANES if i < 3 else 3 * LANES + (i - 3) * slots)
            packed_ref[pl.ds(device, 1), 0, start : start + row.shape[1]] = row


def cross_kernel(place_ref, rec_ref, _, out_ref):
    peers = rec_ref.shape[0]
    span = out_ref.shape[1]
    first = place_ref[0] == 0
    out_ref[:peers, :] = jnp.where(first, rec_ref[:, span : 2 * span], rec_ref[:, 2 * span : 3 * span])
    row = jnp.where(first, peers - 1, 0)
    extra = rec_ref.shape[1] - 3 * span
    for i in range(-(-extra // span)):
        lanes = min(span, extra - i * span)
        start = 3 * span + i * span
        out_ref[peers + i : peers + i + 1, :lanes] = rec_ref[pl.ds(row, 1), start : start + lanes]


def coefficients(rec, band_bins):
    width = rec.shape[1] // 6
    share = LANES / band_bins
    amps = [rec[:, k * width : (k + 1) * width] for k in range(3)]
    p0, p1, p2 = (rec[:, (3 + k) * width : (4 + k) * width] for k in range(3))
    return amps, (p1, p2), (turns(p0), turns(p1 * np.float32(share)), turns(p2 * np.float32(share * share)))


def block_entries(k, band_bins, linear, reduced):
    p1, p2 = linear
    f0, f1, f2 = reduced
    share = LANES / band_bins
    const = frac(f0 + np.float32(k) * f1 + np.float32(k * k) * f2)
    slope = (p1 + p2 * np.float32(2 * k * share)) * np.float32(1.0 / band_bins) * INV_TAU
    return [const, slope, p2 * np.float32(1.0 / band_bins**2) * INV_TAU]


def over_walkers(compact_ref, entries, rows, peers, body):
    for i, entry in enumerate(entries):
        compact_ref[i] = entry
    width = compact_ref.shape[2]
    pairs = rows // 2

    def block(step, _):
        which, pair = step // pairs, step % pairs
        shift = (width - 2 * pair) % width
        rolled = [compact_ref[i, pl.ds(which * SUB, SUB), :] for i in range(len(entries))]
        if pairs > 1:
            rolled = [pltpu.roll(x, shift, 1) for x in rolled]
        body(pl.multiple_of(pair * peers + which * SUB, SUB), lambda h, s: [col(x, h * rows + s) for x in rolled])
        return 0

    steps = pairs * (peers // SUB)
    lax.fori_loop(0, steps, block, 0, unroll=UNROLL)


def summed(halves):
    return [a.astype(BF16).astype(F32) + b.astype(BF16).astype(F32) for a, b in zip(*halves, strict=True)]


def template_kernel(harmonics, rows, rec_ref, data_ref, noise_ref, resid_ref, weighted_ref, compact_ref):
    band_bins = data_ref.shape[1]
    blocks = band_bins // LANES
    share = LANES / band_bins
    amps, linear, reduced = coefficients(rec_ref, band_bins)
    _, f1, f2 = reduced
    twist = cis_turns(frac(np.float32(2.0) * f2))
    step = [frac(f1 + f2), linear[1] * np.float32(2 * share / band_bins) * INV_TAU]
    entries = [*amps, *block_entries(0, band_bins, linear, reduced), *step, *twist]
    lane = lane_iota().astype(F32)
    lane_sq = lane * lane
    u = lane * np.float32(1.0 / band_bins)
    grow = np.float32(share * share) + np.float32(2 * share) * u

    def body(row, columns):
        halves = []
        for s in range(2):
            total = [None] * (2 * blocks)
            for h in range(harmonics):
                a0, a1, a2, const, slope, curve, step_const, step_slope, twist_re, twist_im = columns(h, s)
                z_re, z_im = cis_turns(frac((const + slope * lane) + curve * lane_sq))
                w_re, w_im = cis_turns(frac(step_const + step_slope * lane))
                a = a0 + (a1 + a2 * u) * u
                da = a1 * np.float32(share) + a2 * grow
                dda = a2 * np.float32(2 * share * share)
                for k in range(blocks):
                    terms = (a * z_re, a * z_im)
                    for i in range(2):
                        total[2 * k + i] = terms[i] if h == 0 else total[2 * k + i] + terms[i]
                    if k + 1 < blocks:
                        z_re, z_im = z_re * w_re - z_im * w_im, z_re * w_im + z_im * w_re
                        a = a + da
                    if k + 2 < blocks:
                        w_re, w_im = w_re * twist_re - w_im * twist_im, w_re * twist_im + w_im * twist_re
                        da = da + dda
            halves.append(total)
        for i, template in enumerate(summed(halves)):
            here = i // 2 * LANES
            there = i % 2 * band_bins + here
            part = data_ref[i % 2 : i % 2 + 1, here : here + LANES]
            resid_ref[pl.ds(row, SUB), there : there + LANES] = part - template

    over_walkers(compact_ref, entries, rows, rec_ref.shape[0], body)
    for part in range(2):
        lanes = slice(part * band_bins, (part + 1) * band_bins)
        weighted_ref[:, lanes] = (resid_ref[:, lanes] * noise_ref[0:1, :]).astype(BF16)


def slot_columns(bins, cols_ref):
    slots = bins.shape[1]
    cols_ref[...] = jnp.concatenate([bins.T, jnp.zeros((slots, LANES - SUB), F32)], axis=1)


def slot_wave(params, lane):
    rows = params.shape[0]
    amp, phase, slope, curve, start = (col(params, i, rows) for i in range(5))
    high = jnp.floor(start * np.float32(1.0 / LANES))
    low = start - high * np.float32(LANES)
    offset = lane - low
    wrapped = offset < 0.0
    j = jnp.where(wrapped, offset + np.float32(Q), offset)
    angle = phase + slope * j + curve * j * j
    c, s = cis_turns(turns(angle))
    y = (j + np.float32(0.5)) * np.float32(1.0 / Q) - np.float32(0.5)
    envelope = poly(y * y, COS1)
    scale = amp * (envelope * envelope)
    return scale * c, scale * s, wrapped, high


def wave_kernel(bins_ref, noise_ref, wave_ref, power_ref, cols_ref):
    slots = bins_ref.shape[1]
    band_bins = noise_ref.shape[1]
    blocks = band_bins // LANES
    slot_columns(bins_ref[...], cols_ref)
    rows = 2 * SUB
    lane = lane_iota(rows).astype(F32)

    def block(step, _):
        at = pl.ds(pl.multiple_of(step * rows, rows), rows)
        re, im, wrapped, high = slot_wave(cols_ref[at, :], lane)
        home = jnp.where(wrapped, high + 1.0, high)
        re_half, im_half = re.astype(BF16), im.astype(BF16)
        re, im = re_half.astype(F32), im_half.astype(F32)
        noise = jnp.zeros((rows, LANES), F32)
        for k in range(blocks + 1):
            inside = home == np.float32(k)
            if k < blocks:
                noise = jnp.where(inside, noise_ref[0:1, k * LANES : (k + 1) * LANES], noise)
            start = k * LANES if k < blocks else 2 * band_bins
            wave_ref[at, start : start + LANES] = jnp.where(inside, re, 0.0).astype(BF16)
            start += band_bins if k < blocks else LANES
            wave_ref[at, start : start + LANES] = jnp.where(inside, im, 0.0).astype(BF16)
        power_ref[at, :] = (re * re + im * im) * noise
        return 0

    lax.fori_loop(0, slots // rows, block, 0, unroll=4)


def fit_rows(band, bands):
    width = -(-bands // LANES) * LANES
    place = lax.broadcasted_iota(jnp.int32, (NCOEF, width), 1)
    order = lax.broadcasted_iota(jnp.int32, (NCOEF, width), 0)
    x = (2 * place + 1).astype(F32) * np.float32(1.0 / bands) - np.float32(1.0)
    term, after = jnp.ones_like(x), x
    basis = jnp.zeros_like(x)
    for degree in range(NCOEF):
        basis = jnp.where(order == degree, term, basis)
        term, after = after, np.float32(2.0) * x * after - term
    basis = jnp.where(place < bands, basis, 0.0)
    row = lax.broadcasted_iota(jnp.int32, (NCOEF, LANES), 0)
    lane = lax.broadcasted_iota(jnp.int32, (NCOEF, LANES), 1)
    gram = jnp.zeros((NCOEF, LANES), F32)
    for j in range(NCOEF):
        gram = jnp.where(lane == j, jnp.sum(basis * basis[j : j + 1, :], axis=1, keepdims=True), gram)
    side = basis
    for i in range(NCOEF):
        scale = np.float32(1.0) / jnp.sqrt(gram[i : i + 1, i : i + 1])
        upper = gram[i : i + 1, :] * scale
        factor = gram[:, i : i + 1] * scale
        solved = side[i : i + 1, :] * scale
        below = row > i
        gram = jnp.where(below, gram - factor * upper, jnp.where(row == i, upper, gram))
        side = jnp.where(order > i, side - factor * solved, jnp.where(order == i, solved, side))
    for i in reversed(range(NCOEF)):
        solved = side[i : i + 1, :] / gram[i : i + 1, i : i + 1]
        side = jnp.where(order < i, side - gram[:, i : i + 1] * solved, jnp.where(order == i, solved, side))
    mine = jnp.sum(jnp.where(place == band, side, 0.0), axis=1, keepdims=True)
    return jnp.sum(basis * mine, axis=0, keepdims=True)


OVER_LANES = (((1,), (1,)), ((), ()))


def accepted(corr, power):
    total = lax.dot_general(
        jnp.ones((SUB, LANES), F32), power, OVER_LANES, precision=lax.Precision.HIGHEST, preferred_element_type=F32
    )
    return jax.nn.sigmoid(corr - np.float32(0.5) * total[0:1, :])


def score_kernel(
    harmonics, rows, blocks, place_ref, weighted_ref, resid_ref, noise_ref, bins_ref, wave_ref, power_ref, rec_ref, extra_ref,
    cross_ref, accept_ref, new_ref, log_ref,
    cols_ref, prev_ref, prev_power_ref, beside_ref, beside_extra_ref, compact_ref, edge_ref, rim_ref,
):
    walkers, own = weighted_ref.shape
    slots = wave_ref.shape[0]
    band_bins = own // 2
    last = blocks - 1
    peers = rec_ref.shape[0]
    span = cross_ref.shape[1]
    sources = extra_ref.shape[0]
    place = place_ref[0]

    extra = extra_ref.shape[1]
    for i, (far, source) in enumerate(((0, lax.rem(place + sources - 1, sources)), (sources - 1, lax.rem(place + 1, sources)))):
        @pl.when(place == far)
        def _():
            beside_ref[i] = cross_ref[:peers, :]
            for j in range(-(-extra // span)):
                lanes = min(span, extra - j * span)
                beside_extra_ref[i : i + 1, j * span : j * span + lanes] = cross_ref[sources + j : sources + j + 1, :lanes]

        @pl.when(place != far)
        def _():
            beside_ref[i] = rec_ref[:, i * span : (i + 1) * span]
            beside_extra_ref[i : i + 1, :] = extra_ref[pl.ds(source, 1), :]

    lane = lane_iota().astype(F32)
    lane_sq = lane * lane
    entries = []
    for i, k in enumerate((last, 0)):
        amps, linear, reduced = coefficients(beside_ref[i], band_bins)
        entries += [*amps, *block_entries(k, band_bins, linear, reduced)]

    def body(row, columns):
        halves = []
        for s in range(2):
            total = None
            for h in range(harmonics):
                c = columns(h, s)
                terms = []
                for i, k in enumerate((last, 0)):
                    a0, a1, a2, const, slope, curve = c[6 * i : 6 * i + 6]
                    re, im = cis_turns(frac((const + slope * lane) + curve * lane_sq))
                    u = (lane + np.float32(k * LANES)) * np.float32(1.0 / band_bins)
                    a = a0 + (a1 + a2 * u) * u
                    terms += [a * re, a * im]
                total = terms if h == 0 else [x + y for x, y in zip(total, terms, strict=True)]
            halves.append(total)
        for i, template in enumerate(summed(halves)):
            part = beside_extra_ref[i // 2 : i // 2 + 1, i % 2 * LANES : (i % 2 + 1) * LANES]
            edge_ref[pl.ds(row, SUB), i * LANES : (i + 1) * LANES] = part - template

    over_walkers(compact_ref, entries, rows, peers, body)
    below = beside_extra_ref[0:1, 2 * LANES : 3 * LANES]
    above = beside_extra_ref[1:2, 2 * LANES : 3 * LANES]
    noise = jnp.concatenate([below, below, above, above], axis=1)
    rim_ref[...] = (edge_ref[...] * noise).astype(BF16)

    bins = [beside_extra_ref[0:1, 3 * LANES + i * slots : 3 * LANES + (i + 1) * slots] for i in range(5)]
    slot_columns(jnp.concatenate([*bins, jnp.zeros((3, slots), F32)], axis=0), cols_ref)
    group = 2 * SUB
    lane = lane_iota(group).astype(F32)
    first_noise = noise_ref[0:1, :LANES]

    def block(step, _):
        at = pl.ds(pl.multiple_of(step * group, group), group)
        re, im, wrapped, high = slot_wave(cols_ref[at, :], lane)
        passes = high == np.float32(last)
        re = jnp.where(passes, re, 0.0).astype(BF16).astype(F32)
        im = jnp.where(passes, im, 0.0).astype(BF16).astype(F32)
        prev_power_ref[at, :] = (re * re + im * im) * jnp.where(wrapped, first_noise, below)
        prev_ref[at, :LANES] = jnp.where(wrapped, 0.0, re).astype(BF16)
        prev_ref[at, LANES : 2 * LANES] = jnp.where(wrapped, 0.0, im).astype(BF16)
        prev_ref[at, 2 * LANES : 3 * LANES] = jnp.where(wrapped, re, 0.0).astype(BF16)
        prev_ref[at, 3 * LANES :] = jnp.where(wrapped, im, 0.0).astype(BF16)
        return 0

    lax.fori_loop(0, slots // group, block, 0, unroll=4)
    mine = jnp.concatenate([weighted_ref[:, :LANES], weighted_ref[:, band_bins : band_bins + LANES]], axis=1)
    tail = jnp.concatenate([rim_ref[:, : 2 * LANES], mine], axis=1)
    corr = lax.dot_general(tail, prev_ref[...], OVER_LANES, preferred_element_type=F32)
    half = accepted(corr, prev_power_ref[...]).astype(BF16)
    carried = jnp.dot(half, prev_ref[:, 2 * LANES :], preferred_element_type=F32)

    corr = lax.dot_general(weighted_ref[...], wave_ref[:, :own], OVER_LANES, preferred_element_type=F32)
    corr += lax.dot_general(rim_ref[:, 2 * LANES :], wave_ref[:, own:], OVER_LANES, preferred_element_type=F32)
    rim = wave_ref[:, own:].astype(F32)
    re, im = rim[:, :LANES], rim[:, LANES:]
    accept = accepted(corr, power_ref[...] + (re * re + im * im) * above)
    accept = jnp.where(bins_ref[5:6, :] > 0.0, accept, 0.0)
    accept_ref[...] = accept
    half = accept.astype(BF16)
    squares = jnp.zeros((walkers, LANES), F32)
    chunk = 2 * LANES
    for start in range(0, own, chunk):
        lanes = slice(start, start + chunk)
        new = resid_ref[:, lanes] - jnp.dot(half, wave_ref[:, lanes], preferred_element_type=F32)
        pieces = [new[:, i : i + LANES] for i in range(0, chunk, LANES)]
        if start % band_bins == 0:
            part = start // band_bins
            pieces[0] -= carried[:, part * LANES : (part + 1) * LANES]
        for i, piece in enumerate(pieces):
            new_ref[:, start + i * LANES : start + (i + 1) * LANES] = piece
            squares += piece * piece
    total = jnp.sum(jnp.sum(squares, axis=0, keepdims=True), axis=1, keepdims=True)
    log_power = jnp.log(total * np.float32(1.0 / (walkers * own)) + np.float32(1e-6))
    log_ref[:, 0, :] = jnp.broadcast_to(log_power, (log_ref.shape[0], log_ref.shape[2]))


def output_kernel(peers, bands, band_ref, accept_ref, new_ref, prob_ref, out_ref, fit_ref):
    walkers, own = new_ref.shape
    pairs = walkers // peers
    half = own // 2

    def in_order(x):
        if pairs == 1:
            return x
        return jnp.swapaxes(x.reshape(pairs, peers, x.shape[1]), 0, 1).reshape(x.shape)

    prob_ref[...] = in_order(accept_ref[...])
    for part in range(2):
        out_ref[:, part, :] = in_order(new_ref[:, part * half : (part + 1) * half])
    fit = fit_rows(band_ref[0], bands)
    fit = jnp.broadcast_to(fit, (SUB, fit.shape[1])).T
    fit_ref[...] = jnp.broadcast_to(fit[:bands, 0:1], (bands, LANES))


def call(kernel, outs, args, scratch=(), smem=0, flops=0, name=None, hbm=False, last_any=False):
    vmem = pl.BlockSpec(memory_space=pltpu.VMEM)
    rest = vmem
    if hbm:
        rest = pl.BlockSpec(memory_space=pl.ANY)
        args = [pltpu.with_memory_space_constraint(x, pltpu.HBM) if x.dtype != jnp.int32 or x.ndim > 1 else x for x in args]
    specs = [pl.BlockSpec(memory_space=pltpu.SMEM)] * smem + [rest] * (len(args) - smem)
    if last_any:
        specs[-1] = pl.BlockSpec(memory_space=pl.ANY)
    return pl.pallas_call(
        kernel,
        out_shape=outs,
        in_specs=specs,
        out_specs=[vmem] * len(outs),
        scratch_shapes=scratch,
        compiler_params=pltpu.CompilerParams(vmem_limit_bytes=32 * 2**20),
        cost_estimate=pl.CostEstimate(flops=flops, bytes_accessed=2**20, transcendentals=0),
        name=name,
    )(*args)


def shape(dims, dtype):
    return jax.ShapeDtypeStruct(dims, dtype)


def local(
    data,
    inv_noise,
    mbh_amp,
    mbh_phase,
    bin_amp,
    bin_phase,
    bin_slope,
    bin_curve,
    bin_start,
    bin_count,
):
    band_bins = data.shape[1]
    slots = bin_amp.shape[1]
    rows, harmonics, powers, peers = mbh_amp.shape
    sources = peers
    groups = lax.axis_size("group")
    walkers = rows * peers // 2
    bands = lax.axis_size(BOTH)
    place = lax.axis_index("shard").astype(jnp.int32)[None]
    band = lax.axis_index(BOTH).astype(jnp.int32)[None]
    own = 2 * band_bins

    def padded(count):
        return -(-count // LANES) * LANES

    width = padded(harmonics * rows)
    span = 2 * powers * width
    extra = 3 * LANES + 5 * slots
    packed, bins, data, noise = call(
        pack_kernel,
        [
            shape((peers, 1, 3 * span + extra), F32),
            shape((SUB, slots), F32),
            shape((2, band_bins), F32),
            shape((1, band_bins), F32),
        ],
        [
            place, mbh_amp.transpose(1, 2, 3, 0), mbh_phase.transpose(1, 2, 3, 0), data, inv_noise.reshape(-1, LANES),
            bin_amp, bin_phase, bin_slope, bin_curve, bin_start, bin_count,
        ],
        scratch=[
            pltpu.VMEM((harmonics, powers, peers, rows), F32),
            pltpu.VMEM((harmonics, powers, peers, rows), F32),
            pltpu.VMEM((4, 1, slots), F32),
            pltpu.VMEM((1, slots), jnp.int32),
            pltpu.VMEM((band_bins // LANES, LANES), BF16),
            pltpu.SMEM((1,), jnp.int32),
            pltpu.SemaphoreType.DMA((10,)),
        ],
        smem=1,
        hbm=True,
        name="pack",
    )
    received = lax.all_to_all(packed, "shard", split_axis=0, concat_axis=0, tiled=True)
    received = received.reshape(peers, -1)
    wave, slot_power = call(
        wave_kernel,
        [shape((slots, own + 2 * LANES), BF16), shape((slots, LANES), F32)],
        [bins, noise],
        scratch=[pltpu.VMEM((slots, LANES), F32)],
        flops=10**9,
        name="waves",
    )
    (to_cross,) = call(
        cross_kernel,
        [shape((sources + -(-extra // span // SUB) * SUB, span), F32)],
        [place, received, slot_power],
        smem=1,
        last_any=True,
        name="cross",
    )
    pairs = [(g * peers, (g + 1) * peers) for g in range(groups - 1)]
    pairs += [(g * peers + peers - 1, (g - 1) * peers + peers - 1) for g in range(1, groups)]
    crossed = lax.ppermute(to_cross, BOTH, pairs)

    extras = received[:, 3 * span :]
    if rows % 2:

        def paired(x):
            x = x.reshape(peers // 2, 2, 2 * powers, width)[..., : harmonics * rows]
            x = x.reshape(peers // 2, 2, 2 * powers, harmonics, rows).transpose(0, 2, 3, 1, 4)
            x = x.reshape(peers // 2, 2 * powers, 2 * harmonics * rows)
            x = jnp.pad(x, ((0, 0), (0, 0), (0, width - 2 * harmonics * rows)))
            return x.reshape(peers // 2, span)

        coefs, coefs_below, coefs_above = (paired(received[:, i * span : (i + 1) * span]) for i in range(3))
        coefs_beside = jnp.concatenate([coefs_below, coefs_above], axis=1)
        crossed = jnp.concatenate([paired(crossed[:peers]), jnp.zeros((peers // 2, span), F32), crossed[peers:]], axis=0)
        rows, peers = 2 * rows, peers // 2
    else:
        coefs = received[:, :span]
        coefs_beside = received[:, span : 3 * span]

    resid, weighted = call(
        functools.partial(template_kernel, harmonics, rows),
        [shape((walkers, own), F32), shape((walkers, own), BF16)],
        [coefs, data, noise],
        scratch=[pltpu.VMEM((10, peers, width), F32)],
        flops=10**9,
        name="template",
    )
    accept, updated, log_power = call(
        functools.partial(score_kernel, harmonics, rows, band_bins // LANES),
        [shape((walkers, slots), F32), shape((walkers, own), F32), shape((bands, 1, LANES), F32)],
        [place, weighted, resid, noise, bins, wave, slot_power, coefs_beside, extras, crossed],
        scratch=[
            pltpu.VMEM((slots, LANES), F32),
            pltpu.VMEM((slots, 4 * LANES), BF16),
            pltpu.VMEM((slots, LANES), F32),
            pltpu.VMEM((2, peers, span), F32),
            pltpu.VMEM((2, extra), F32),
            pltpu.VMEM((12, peers, width), F32),
            pltpu.VMEM((walkers, 4 * LANES), F32),
            pltpu.VMEM((walkers, 4 * LANES), BF16),
        ],
        smem=1,
        name="scores",
    )
    log_powers = lax.all_to_all(log_power, BOTH, split_axis=0, concat_axis=0, tiled=True)
    accept_prob, residual_new, fit = call(
        functools.partial(output_kernel, peers, bands),
        [shape((walkers, slots), F32), shape((walkers, 2, band_bins), F32), shape((bands, LANES), F32)],
        [band, accept, updated],
        smem=1,
        name="outputs",
    )
    noise_fit = jnp.sum(fit * log_powers[:, 0, :], axis=0)[:1]
    return (accept_prob, residual_new, noise_fit)


def solution(mesh):
    in_specs = (
        P(None, BOTH),
        P(BOTH),
        P("shard", None, None, "group"),
        P("shard", None, None, "group"),
        P(BOTH, None),
        P(BOTH, None),
        P(BOTH, None),
        P(BOTH, None),
        P(BOTH, None),
        P(BOTH),
    )
    out_specs = (P(None, BOTH), P(None, None, BOTH), P(BOTH))
    return jax.shard_map(local, mesh=mesh, in_specs=in_specs, out_specs=out_specs, check_vma=False)
```

time: 52.7 us -> 41.6 us (0.79)
  starting transfers between devices: 20.9 us -> 12.2 us
  local copies, waits for them, and re-layouts: 7.21 us -> 0.03 us
  waiting for transfers between devices: 8.16 us -> 10.8 us
  Pallas kernels: 14 us -> 16.3 us
    unnamed x17 -> x1, local copies, waits for them, and re-layouts: 5.89 us -> 0.01 us
    all_to_all x1, waiting for transfers between devices: 0.01 us -> 5.7 us  [local(): lax.all_to_all(packed, 'shard', split_axis=0, concat_axis=0, tiled=True)]
    ppermute x2 -> x1, starting transfers between devices: 6.11 us -> 1.29 us  [local(): crossed = lax.ppermute(to_cross, BOTH, pairs)]
    all_to_all x1, starting transfers between devices: 7.53 us -> 3.65 us  [local(): lax.all_to_all(log_power, BOTH, split_axis=0, concat_axis=0, tiled=True)]
    pallas_call x8 -> x6, Pallas kernels: 14 us -> 16.3 us  [call(): pl.pallas_call(kernel, out_shape=outs, in_specs=specs, out_specs=[vmem] *...]
    ppermute x2 -> x1, waiting for transfers between devices: 2.09 us -> 0.01 us  [local(): crossed = lax.ppermute(to_cross, BOTH, pairs)]
    all_to_all x1, waiting for transfers between devices: 6.07 us -> 5.08 us  [local(): lax.all_to_all(log_power, BOTH, split_axis=0, concat_axis=0, tiled=True)]
    broadcast_in_dim x1 -> x0, local copies, waits for them, and re-layouts: 0.69 us -> none  [local(): inv_noise[None, :]]
  transfers between devices with their start and end apart: 4 -> 3, of which waited for: 3 -> 2; matrix products, arithmetic and copies ran while one was open for 1% -> 0% of each run, Pallas kernels for 19% -> 18%
where the time goes in v2:
time: 41.6 us; the launch traced here: 41.3 us
  Pallas kernels  16.3 us (39%)
  starting transfers between devices  12.2 us (29%)
  waiting for transfers between devices  10.8 us (26%)
  between operations  1.38 us (3%)
  other arithmetic  0.53 us (1%)
    pallas_call x6, Pallas kernels, call(): pl.pallas_call(kernel, out_shape=outs, in_specs=specs, out_specs=[vmem] *...  16.3 us
    all_to_all x1, starting transfers between devices, local(): lax.all_to_all(packed, 'shard', split_axis=0, concat_axis=0, tiled=True)  7.29 us
    all_to_all x1, waiting for transfers between devices, local(): lax.all_to_all(packed, 'shard', split_axis=0, concat_axis=0, tiled=True)  5.7 us
    all_to_all x1, waiting for transfers between devices, local(): lax.all_to_all(log_power, BOTH, split_axis=0, concat_axis=0, tiled=True)  5.08 us
    all_to_all x1, starting transfers between devices, local(): lax.all_to_all(log_power, BOTH, split_axis=0, concat_axis=0, tiled=True)  3.65 us
    ppermute x1, starting transfers between devices, local(): crossed = lax.ppermute(to_cross, BOTH, pairs)  1.29 us
  transfers between devices with their start and end apart: 3, of which 2 were waited for; matrix products, arithmetic and copies ran while one was open for 0% of the time, Pallas kernels for 18%

profile of v2, /device:TPU:0, one launch (start us, length us, event | category | flops | bytes accessed | tf_op | source)
XLA Modules:
  0.0 41.3 jit_solution(507154504000413358)
XLA Ops:
  1.3 1.8 %pack.1 = (f32[8,1,5248]{2,1,0:T(1,128)}, f32[8,512]{1,0:T(8,128)S(1)}, f32[2,1024]{1,0:T(2,128)S(1)}, f32[1,1024]{1,0:T(1,128)S(1)}) custom-call(s32[1]{0:T(128)} %bitcast.1.place_ref, f32[6,3,8,16]{3,2,1,0:T(8,128)} %bitcast.14, f32[6,3,8,16]{3,2,1,0:T(8,128)} %bitcast.15, f32[2,1024]{1,0:T(2,128)} %data_hbm.1, bf16[8,128]{1,0:T(8,128)(2,1)} %bitcast.17, ...), custom_call_target="tpu_custom_call" | custom-call | bytes 1048576 | tf_op jit(solution)/shard_map/pack/pallas_call | solution.py:462
  3.1 7.3 %all-to-all-start = ((f32[8,1,5248]{2,1,0:T(1,128)}), f32[8,1,5248]{2,1,0:T(1,128)S(1)}, u32[]{:S(2)}, u32[]{:S(2)}) async-start(f32[8,1,5248]{2,1,0:T(1,128)} %get-tuple-element.17), calls=%async_computation | async-start | bytes 335872 | tf_op jit(solution)/shard_map/all_to_all | solution.py:532
  10.4 1.9 %waves.1 = (bf16[512,2304]{1,0:T(8,128)(2,1)S(1)}, f32[512,128]{1,0:T(8,128)S(1)}) custom-call(f32[8,512]{1,0:T(8,128)S(1)} %get-tuple-element.22.bins_ref, f32[1,1024]{1,0:T(1,128)S(1)} %get-tuple-element.19.noise_ref), custom_call_target="tpu_custom_call" | custom-call | flops 1000000000 | bytes 1048576 | tf_op jit(solution)/shard_map/waves/pallas_call | solution.py:462
  12.3 5.7 %all-to-all-done = f32[8,1,5248]{2,1,0:T(1,128)S(1)} async-done(((f32[8,1,5248]{2,1,0:T(1,128)}), f32[8,1,5248]{2,1,0:T(1,128)S(1)}, u32[]{:S(2)}, u32[]{:S(2)}) %all-to-all-start) | async-done | bytes 167968 | tf_op jit(solution)/shard_map/all_to_all | solution.py:532
  18.1 1.3 %collective-permute-start = (f32[16,768]{1,0:T(8,128)S(1)}, f32[16,768]{1,0:T(8,128)S(1)}, u32[]{:S(2)}, u32[]{:S(2)}) collective-permute-start(f32[16,768]{1,0:T(8,128)S(1)} %cross.1), channel_id=1, source_target_pairs={{0,8},{8,16},{16,24},{15,7},{23,15},{31,23}} | collective-permute-start | bytes 147464 | tf_op jit(solution)/shard_map/ppermute | solution.py:552
  19.4 3.7 %template.1 = (f32[64,2048]{1,0:T(8,128)S(1)}, bf16[64,2048]{1,0:T(8,128)(2,1)S(1)}) custom-call(f32[8,768]{1,0:T(8,128)S(1)} %slice.16.rec_ref, f32[2,1024]{1,0:T(2,128)S(1)} %get-tuple-element.18.data_ref, f32[1,1024]{1,0:T(1,128)S(1)} %get-tuple-element.19.noise_ref), custom_call_target="tpu_custom_call" | custom-call | flops 1000000000 | bytes 1048576 | tf_op jit(solution)/shard_map/template/pallas_call | solution.py:462
  23.1 0.0 collective-permute-done.cross_ref
  23.2 6.8 %scores.1 = (f32[64,512]{1,0:T(8,128)S(1)}, f32[64,2048]{1,0:T(8,128)S(1)}, f32[32,1,128]{2,1,0:T(1,128)}) custom-call(s32[1]{0:T(128)} %bitcast.1.place_ref, bf16[64,2048]{1,0:T(8,128)(2,1)S(1)} %get-tuple-element.20.weighted_ref, f32[64,2048]{1,0:T(8,128)S(1)} %get-tuple-element.21.resid_ref, f32[1,1024]{1,0:T(1,128)S(1)} %get-tuple-element.19.noise_ref, ...), custom_call_target="tpu_custom_call" | custom-call | bytes 1048576 | tf_op jit(solution)/shard_map/scores/pallas_call | solution.py:462
  30.0 3.6 %all-to-all-start.1 = ((f32[32,1,128]{2,1,0:T(1,128)}), f32[32,1,128]{2,1,0:T(1,128)S(1)}, u32[]{:S(2)}, u32[]{:S(2)}) async-start(f32[32,1,128]{2,1,0:T(1,128)} %get-tuple-element.30), calls=%async_computation.1 | async-start | bytes 32768 | tf_op jit(solution)/shard_map/all_to_all | solution.py:597
  33.6 2.0 %outputs.1 = (f32[64,512]{1,0:T(8,128)}, f32[64,2,1024]{2,1,0:T(2,128)}, f32[32,128]{1,0:T(8,128)S(1)}) custom-call(s32[1]{0:T(128)} %bitcast.band_ref, f32[64,512]{1,0:T(8,128)S(1)} %get-tuple-element.25.accept_ref, f32[64,2048]{1,0:T(8,128)S(1)} %get-tuple-element.26.new_ref), custom_call_target="tpu_custom_call" | custom-call | bytes 1048576 | tf_op jit(solution)/shard_map/outputs/pallas_call | solution.py:462
  35.7 5.1 %all-to-all-done.1 = f32[32,1,128]{2,1,0:T(1,128)S(1)} async-done(((f32[32,1,128]{2,1,0:T(1,128)}), f32[32,1,128]{2,1,0:T(1,128)S(1)}, u32[]{:S(2)}, u32[]{:S(2)}) %all-to-all-start.1) | async-done | bytes 16416 | tf_op jit(solution)/shard_map/all_to_all | solution.py:597
  40.8 0.5 %multiply_reduce_fusion = f32[128]{0:T(128)} fusion(f32[32,128]{1,0:T(8,128)S(1)} %get-tuple-element.29, f32[32,128]{1,0:T(8,128)S(1)} %bitcast.16), kind=kLoop, calls=%fused_computation.1 | loop fusion | flops 8064 | bytes 33280 | tf_op jit(solution)/shard_map/reduce_sum | solution.py:605
  (5 shorter events, 0.0 us)
Async XLA Ops:
  3.1 14.9 %all-to-all-start = ((f32[8,1,5248]{2,1,0:T(1,128)}), f32[8,1,5248]{2,1,0:T(1,128)S(1)}, u32[]{:S(2)}, u32[]{:S(2)}) async-start(f32[8,1,5248]{2,1,0:T(1,128)} %get-tuple-element.17), calls=%async_computation | async-start | bytes 335872 | tf_op jit(solution)/shard_map/all_to_all | solution.py:532
  18.1 5.0 %collective-permute-start = (f32[16,768]{1,0:T(8,128)S(1)}, f32[16,768]{1,0:T(8,128)S(1)}, u32[]{:S(2)}, u32[]{:S(2)}) collective-permute-start(f32[16,768]{1,0:T(8,128)S(1)} %cross.1), channel_id=1, source_target_pairs={{0,8},{8,16},{16,24},{15,7},{23,15},{31,23}} | collective-permute-start | bytes 147464 | tf_op jit(solution)/shard_map/ppermute | solution.py:552
  30.0 10.8 %all-to-all-start.1 = ((f32[32,1,128]{2,1,0:T(1,128)}), f32[32,1,128]{2,1,0:T(1,128)S(1)}, u32[]{:S(2)}, u32[]{:S(2)}) async-start(f32[32,1,128]{2,1,0:T(1,128)} %get-tuple-element.30), calls=%async_computation.1 | async-start | bytes 32768 | tf_op jit(solution)/shard_map/all_to_all | solution.py:597

commit v3 on v2

v3 whole, which is shorter than its diff:
```python
import functools
import math

import jax
import jax.numpy as jnp
import numpy as np
from jax import lax
from jax.experimental import pallas as pl
from jax.experimental.pallas import tpu as pltpu
from jax.sharding import PartitionSpec as P

Q = 128
NCOEF = 8
LANES = 128
SUB = 8
F32 = jnp.float32
BF16 = jnp.bfloat16
BOTH = ("group", "shard")

INV_TAU = np.float32(1.0 / (2.0 * math.pi))
TAU_A = np.float32(round(2.0 * math.pi * 512) / 512)
TAU_B = np.float32(round((2.0 * math.pi - float(TAU_A)) * 2**22) / 2**22)
TAU_C = np.float32(2.0 * math.pi - float(TAU_A) - float(TAU_B))
MAGIC = np.float32(1.5 * 2**23)
SIN2 = (6.283185160089475, -10.33541375785372, 5.100062754574036, -1.1960903483123309, 0.15444025802555503)
COS1 = (0.9999999534666666, -4.934792858675247, 4.058411914166824, -1.3318801612473732, 0.2196967986012024)


def nearest(x):
    return (x + MAGIC) - MAGIC


def padded(count):
    return -(-count // LANES) * LANES


def poly(y, coefs):
    total = np.float32(coefs[-1])
    for c in coefs[-2::-1]:
        total = total * y + np.float32(c)
    return total


def cis_turns(r):
    y = r * r
    s2 = poly(y, SIN2) * r
    c1 = poly(y, COS1)
    return np.float32(1.0) - np.float32(0.5) * (s2 * s2), s2 * c1


def turns(angle):
    n = nearest(angle * INV_TAU)
    return (((angle - n * TAU_A) - n * TAU_B) - n * TAU_C) * INV_TAU


def frac(t):
    return t - nearest(t)


def col(x, lane, rows=SUB):
    return jnp.broadcast_to(x[:, lane : lane + 1], (rows, LANES))


def lane_iota(rows=SUB):
    return lax.broadcasted_iota(jnp.int32, (rows, LANES), 1)


def pack_kernel(
    amp_hbm, phase_hbm, data_hbm, noise_hbm, bin_amp_hbm, bin_phase_hbm, bin_slope_hbm, bin_curve_hbm,
    bin_start_hbm, count_hbm, packed_ref, bins_ref, data_ref, noise_ref,
    amp_ref, phase_ref, rows_ref, start_ref, raw_noise_ref, count_ref, sems,
):
    copies = [
        pltpu.make_async_copy(source, target, sems.at[i])
        for i, (source, target) in enumerate(
            [
                (amp_hbm, amp_ref),
                (phase_hbm, phase_ref),
                (count_hbm, count_ref),
                (bin_amp_hbm, rows_ref.at[0]),
                (bin_phase_hbm, rows_ref.at[1]),
                (bin_slope_hbm, rows_ref.at[2]),
                (bin_curve_hbm, rows_ref.at[3]),
                (bin_start_hbm, start_ref),
                (data_hbm, data_ref),
                (noise_hbm, raw_noise_ref),
            ]
        )
    ]
    for copy in copies:
        copy.start()
    harmonics, powers, peers, rows = amp_ref.shape
    span = padded(2 * powers * harmonics * rows)
    slots = bins_ref.shape[1]
    band_bins = data_ref.shape[1]
    for copy in copies[2:]:
        copy.wait()
    live = lax.broadcasted_iota(jnp.int32, (1, slots), 1) < count_ref[0]
    amp = jnp.where(live, rows_ref[0], 0.0)
    slot_rows = [amp, rows_ref[1], rows_ref[2], rows_ref[3], start_ref[...].astype(F32)]
    bins_ref[...] = jnp.concatenate([*slot_rows, live.astype(F32), jnp.zeros((2, slots), F32)], axis=0)
    raw_noise = raw_noise_ref[...].astype(F32)
    noise = jnp.concatenate([raw_noise[i : i + 1] for i in range(raw_noise.shape[0])], axis=1)
    noise_ref[...] = noise
    start = 3 * span
    for lanes in (slice(0, LANES), slice(band_bins - LANES, band_bins)):
        for row in (data_ref[0:1, lanes], data_ref[1:2, lanes], noise[:, lanes]):
            packed_ref[:, 0, start : start + LANES] = jnp.broadcast_to(row, (peers, LANES))
            start += LANES
    for row in slot_rows:
        packed_ref[:, 0, start : start + slots] = jnp.broadcast_to(row, (peers, slots))
        start += slots
    for copy in copies[:2]:
        copy.wait()
    parts = [ref[h, power] for ref in (amp_ref, phase_ref) for power in range(powers) for h in range(harmonics)]
    if span > 2 * powers * harmonics * rows:
        parts.append(jnp.zeros((peers, span - 2 * powers * harmonics * rows), F32))
    packed = jnp.concatenate(parts, axis=1)
    if rows == 2 * SUB:
        lane = lax.broadcasted_iota(jnp.int32, (peers, LANES), 1)
        order = lane - lane % (2 * SUB) + lane % SUB * 2 + lane % (2 * SUB) // SUB
        blocks = [packed[:, i : i + LANES] for i in range(0, span, LANES)]
        blocks = [jnp.take_along_axis(x, order, axis=1, mode="promise_in_bounds") for x in blocks]
        packed = jnp.concatenate(blocks, axis=1)
    packed_ref[:, 0, :span] = packed
    packed_ref[:, 0, span : 2 * span] = jnp.concatenate([packed[-1:], packed[:-1]], axis=0)
    packed_ref[:, 0, 2 * span : 3 * span] = jnp.concatenate([packed[1:], packed[:1]], axis=0)


def cross_kernel(rec_ref, _, out_ref):
    peers = rec_ref.shape[0]
    span = out_ref.shape[1]
    first = lax.axis_index("shard") == 0
    out_ref[:peers, :] = jnp.where(first, rec_ref[:, span : 2 * span], rec_ref[:, 2 * span : 3 * span])
    start = 3 * span
    rim = rec_ref[0:1, start : start + 3 * LANES]
    start += 3 * LANES
    row = rec_ref[peers - 1 : peers, start:]
    row = jnp.concatenate([jnp.where(first, row[:, : 3 * LANES], rim), row[:, 3 * LANES :]], axis=1)
    for i, at in enumerate(range(0, row.shape[1], span)):
        lanes = min(span, row.shape[1] - at)
        out_ref[peers + i : peers + i + 1, :lanes] = row[:, at : at + lanes]


def coefficients(rec, width, band_bins):
    share = LANES / band_bins
    fill = jnp.zeros((rec.shape[0], LANES - width), F32)
    terms = [jnp.concatenate([rec[:, k * width : (k + 1) * width], fill], axis=1) for k in range(6)]
    amps, (p0, p1, p2) = terms[:3], terms[3:]
    return amps, (p1, p2), (turns(p0), turns(p1 * np.float32(share)), turns(p2 * np.float32(share * share)))


def phase_terms(k, band_bins, linear, reduced):
    p1, p2 = linear
    f0, f1, f2 = reduced
    share = LANES / band_bins
    const = frac(f0 + np.float32(k) * f1 + np.float32(k * k) * f2)
    slope = (p1 + p2 * np.float32(2 * k * share)) * np.float32(1.0 / band_bins) * INV_TAU
    return [const, slope, p2 * np.float32(1.0 / band_bins**2) * INV_TAU]


def amp_terms(k, band_bins, amps):
    a0, a1, a2 = amps
    at = k * LANES / band_bins
    slope = (a1 + a2 * np.float32(2 * at)) * np.float32(1.0 / band_bins)
    return [a0 + (a1 + a2 * np.float32(at)) * np.float32(at), slope, a2 * np.float32(1.0 / band_bins**2)]


def pieces(x):
    high = x.astype(BF16).astype(F32)
    rest = x - high
    middle = rest.astype(BF16).astype(F32)
    return [high, middle, (rest - middle).astype(BF16).astype(F32)]


QUAD = 16


def quad_rows(terms):
    terms = [pieces(x) for x in terms]
    rows = [*terms[0], *terms[1], *terms[2], *terms[2]]
    return rows + [jnp.zeros_like(rows[0])] * (QUAD - len(rows))


def lane_powers():
    row = lax.broadcasted_iota(jnp.int32, (QUAD, LANES), 0)
    lane = lax.broadcasted_iota(jnp.int32, (QUAD, LANES), 1)
    low = lane * lane % LANES
    table = jnp.where(row < 3, 1, jnp.where(row < 6, lane, jnp.where(row < 9, lane * lane - low, low)))
    table = jnp.where(row < 12, table, 0).astype(F32)
    zero = jnp.zeros((QUAD, LANES), F32)
    upper = jnp.concatenate([table, zero], axis=1)
    lower = jnp.concatenate([zero, table], axis=1)
    return jnp.concatenate([upper, lower], axis=0).astype(BF16)


def evaluator(pairs, stage_ref, values_ref):
    table = lane_powers()
    for pair, (first, second) in enumerate(pairs):
        for i, row in enumerate(quad_rows(first) + quad_rows(second)):
            stage_ref[pair, i] = row

    def evaluate(q):
        for pair in range(len(pairs)):
            rows = stage_ref[pair, :, q, :].T.astype(BF16)
            values_ref[pair, q * LANES : (q + 1) * LANES, :] = jnp.dot(rows, table, preferred_element_type=F32)

    return evaluate


def by_walkers(count, evaluate, block):
    evaluate(0)
    for q in range(count):
        if q + 1 < count:
            evaluate(q + 1)
        block(q)


def summed(halves):
    return [a.astype(BF16).astype(F32) + b.astype(BF16).astype(F32) for a, b in zip(*halves, strict=True)]


def template_kernel(harmonics, rec_ref, data_ref, noise_ref, resid_ref, weighted_ref, stage_ref, values_ref):
    band_bins = data_ref.shape[1]
    blocks = band_bins // LANES
    share = LANES / band_bins
    amps, linear, reduced = coefficients(rec_ref, harmonics * 2 * SUB, band_bins)
    _, f1, f2 = reduced
    zero = jnp.zeros_like(f1)
    twist_re, twist_im = cis_turns(frac(np.float32(2.0) * f2))
    step = [frac(f1 + f2), linear[1] * np.float32(2 * share / band_bins) * INV_TAU, zero]
    now, then = amp_terms(0, band_bins, amps), amp_terms(1, band_bins, amps)
    grow = [then[0] - now[0], amps[2] * np.float32(2 * share / band_bins), zero]
    evaluate = evaluator(
        [
            (phase_terms(0, band_bins, linear, reduced), now),
            (step, grow),
            ([twist_re, zero, zero], [twist_im, zero, zero]),
            ([amps[2] * np.float32(2 * share * share), zero, zero], [zero] * 3),
        ],
        stage_ref,
        values_ref,
    )

    def block(q):
        halves = []
        for s in range(2):
            total = [None] * (2 * blocks)
            for h in range(harmonics):
                at = pl.ds(q * LANES + (2 * h + s) * SUB, SUB)
                phase, a = values_ref[0, at, :LANES], values_ref[0, at, LANES:]
                w_phase, da = values_ref[1, at, :LANES], values_ref[1, at, LANES:]
                twist_re, twist_im = values_ref[2, at, :LANES], values_ref[2, at, LANES:]
                dda = values_ref[3, at, :LANES]
                z_re, z_im = cis_turns(frac(phase))
                w_re, w_im = cis_turns(frac(w_phase))
                for k in range(blocks):
                    terms = (a * z_re, a * z_im)
                    for i in range(2):
                        total[2 * k + i] = terms[i] if h == 0 else total[2 * k + i] + terms[i]
                    if k + 1 < blocks:
                        z_re, z_im = z_re * w_re - z_im * w_im, z_re * w_im + z_im * w_re
                        a = a + da
                    if k + 2 < blocks:
                        w_re, w_im = w_re * twist_re - w_im * twist_im, w_re * twist_im + w_im * twist_re
                        da = da + dda
            halves.append(total)
        row = q * SUB
        for i, template in enumerate(summed(halves)):
            here = i // 2 * LANES
            there = i % 2 * band_bins + here
            part = data_ref[i % 2 : i % 2 + 1, here : here + LANES]
            resid_ref[pl.ds(row, SUB), there : there + LANES] = part - template

    by_walkers(rec_ref.shape[0], evaluate, block)
    for part in range(2):
        lanes = slice(part * band_bins, (part + 1) * band_bins)
        weighted_ref[:, lanes] = (resid_ref[:, lanes] * noise_ref[0:1, :]).astype(BF16)


def slot_columns(bins, cols_ref):
    slots = bins.shape[1]
    cols_ref[...] = jnp.concatenate([bins.T, jnp.zeros((slots, LANES - SUB), F32)], axis=1)


def slot_wave(params, lane):
    rows = params.shape[0]
    amp, phase, slope, curve, start = (col(params, i, rows) for i in range(5))
    high = jnp.floor(start * np.float32(1.0 / LANES))
    low = start - high * np.float32(LANES)
    offset = lane - low
    wrapped = offset < 0.0
    j = jnp.where(wrapped, offset + np.float32(Q), offset)
    angle = phase + slope * j + curve * j * j
    c, s = cis_turns(turns(angle))
    y = (j + np.float32(0.5)) * np.float32(1.0 / Q) - np.float32(0.5)
    envelope = poly(y * y, COS1)
    scale = amp * (envelope * envelope)
    return scale * c, scale * s, wrapped, high


def wave_kernel(bins_ref, noise_ref, wave_ref, power_ref, cols_ref):
    slots = bins_ref.shape[1]
    band_bins = noise_ref.shape[1]
    blocks = band_bins // LANES
    slot_columns(bins_ref[...], cols_ref)
    rows = 2 * SUB
    lane = lane_iota(rows).astype(F32)

    def block(step, _):
        at = pl.ds(pl.multiple_of(step * rows, rows), rows)
        re, im, wrapped, high = slot_wave(cols_ref[at, :], lane)
        home = jnp.where(wrapped, high + 1.0, high)
        re_half, im_half = re.astype(BF16), im.astype(BF16)
        re, im = re_half.astype(F32), im_half.astype(F32)
        noise = jnp.zeros((rows, LANES), F32)
        for k in range(blocks + 1):
            inside = home == np.float32(k)
            if k < blocks:
                noise = jnp.where(inside, noise_ref[0:1, k * LANES : (k + 1) * LANES], noise)
            start = k * LANES if k < blocks else 2 * band_bins
            wave_ref[at, start : start + LANES] = jnp.where(inside, re, 0.0).astype(BF16)
            start += band_bins if k < blocks else LANES
            wave_ref[at, start : start + LANES] = jnp.where(inside, im, 0.0).astype(BF16)
        power_ref[at, :] = (re * re + im * im) * noise
        return 0

    lax.fori_loop(0, slots // rows, block, 0, unroll=4)


def fit_rows(band, bands):
    width = -(-bands // LANES) * LANES
    place = lax.broadcasted_iota(jnp.int32, (NCOEF, width), 1)
    order = lax.broadcasted_iota(jnp.int32, (NCOEF, width), 0)
    x = (2 * place + 1).astype(F32) * np.float32(1.0 / bands) - np.float32(1.0)
    term, after = jnp.ones_like(x), x
    basis = jnp.zeros_like(x)
    for degree in range(NCOEF):
        basis = jnp.where(order == degree, term, basis)
        term, after = after, np.float32(2.0) * x * after - term
    basis = jnp.where(place < bands, basis, 0.0)
    row = lax.broadcasted_iota(jnp.int32, (NCOEF, LANES), 0)
    lane = lax.broadcasted_iota(jnp.int32, (NCOEF, LANES), 1)
    gram = jnp.zeros((NCOEF, LANES), F32)
    for j in range(NCOEF):
        gram = jnp.where(lane == j, jnp.sum(basis * basis[j : j + 1, :], axis=1, keepdims=True), gram)
    side = basis
    for i in range(NCOEF):
        scale = np.float32(1.0) / jnp.sqrt(gram[i : i + 1, i : i + 1])
        upper = gram[i : i + 1, :] * scale
        factor = gram[:, i : i + 1] * scale
        solved = side[i : i + 1, :] * scale
        below = row > i
        gram = jnp.where(below, gram - factor * upper, jnp.where(row == i, upper, gram))
        side = jnp.where(order > i, side - factor * solved, jnp.where(order == i, solved, side))
    for i in reversed(range(NCOEF)):
        solved = side[i : i + 1, :] / gram[i : i + 1, i : i + 1]
        side = jnp.where(order < i, side - gram[:, i : i + 1] * solved, jnp.where(order == i, solved, side))
    mine = jnp.sum(jnp.where(place == band, side, 0.0), axis=1, keepdims=True)
    return jnp.sum(basis * mine, axis=0, keepdims=True)


OVER_LANES = (((1,), (1,)), ((), ()))


def accepted(corr, power):
    total = lax.dot_general(
        jnp.ones((SUB, LANES), F32), power, OVER_LANES, precision=lax.Precision.HIGHEST, preferred_element_type=F32
    )
    return jax.nn.sigmoid(corr - np.float32(0.5) * total[0:1, :])


def score_kernel(
    harmonics, blocks, weighted_ref, resid_ref, noise_ref, bins_ref, wave_ref, power_ref, rec_ref, extra_ref,
    cross_ref, cross_extra_ref, accept_ref, new_ref, log_ref,
    prev_ref, prev_power_ref, stage_ref, values_ref, edge_ref, rim_ref,
):
    walkers, own = weighted_ref.shape
    slots = wave_ref.shape[0]
    band_bins = own // 2
    last = blocks - 1
    span = cross_ref.shape[1]
    sources, extra = extra_ref.shape
    place = lax.axis_index("shard")
    first, final = place == 0, place == sources - 1

    below_rec = jnp.where(first, cross_ref[...], rec_ref[:, :span])
    above_rec = jnp.where(final, cross_ref[...], rec_ref[:, span:])
    source = lax.rem(place + 1, sources)
    rows = -(-3 * LANES // cross_extra_ref.shape[1])
    crossed = jnp.concatenate([cross_extra_ref[i : i + 1, :] for i in range(rows)], axis=1)
    above = jnp.where(final, crossed[:, : 3 * LANES], extra_ref[pl.ds(source, 1), : 3 * LANES])
    source = lax.rem(place + sources - 1, sources)
    below = extra_ref[pl.ds(source, 1), 3 * LANES :]
    rows = -(-below.shape[1] // cross_extra_ref.shape[1])
    crossed = jnp.concatenate([cross_extra_ref[i : i + 1, :] for i in range(rows)], axis=1)
    below = jnp.where(first, crossed[:, : below.shape[1]], below)

    bins = jnp.concatenate(
        [below[:, 3 * LANES + i * slots : 3 * LANES + (i + 1) * slots] for i in range(5)] + [jnp.zeros((3, slots), F32)],
        axis=0,
    )
    passes = (bins[4:5] > np.float32(band_bins - Q)) & (bins[0:1] != 0.0)
    flags = jnp.broadcast_to(jnp.where(passes, 1.0, 0.0), (2 * SUB, slots)).astype(BF16)
    row, column = (lax.broadcasted_iota(jnp.int32, (LANES, LANES), i) for i in range(2))
    upto = jnp.where(row <= column, 1.0, 0.0).astype(BF16)
    ranks = []
    for start in range(0, slots, LANES):
        rank = jnp.dot(flags[:, start : start + LANES], upto, preferred_element_type=F32)[0:1]
        ranks.append(rank + ranks[-1][:, LANES - 1 :] if ranks else rank)
    passing = jnp.max(ranks[-1]).astype(jnp.int32)
    rank = jnp.where(passes, jnp.concatenate(ranks, axis=1), 0.0)
    bin_pieces = [x.astype(BF16) for x in pieces(bins)]

    pairs = []
    for k, rec in ((last, below_rec), (0, above_rec)):
        amps, linear, reduced = coefficients(rec, harmonics * 2 * SUB, band_bins)
        pairs.append((phase_terms(k, band_bins, linear, reduced), amp_terms(k, band_bins, amps)))
    evaluate = evaluator(pairs, stage_ref, values_ref)

    def edge_block(q):
        halves = []
        for s in range(2):
            total = None
            for h in range(harmonics):
                at = pl.ds(q * LANES + (2 * h + s) * SUB, SUB)
                terms = []
                for i in range(2):
                    a = values_ref[i, at, LANES:]
                    terms += [a * x for x in cis_turns(frac(values_ref[i, at, :LANES]))]
                total = terms if h == 0 else [x + y for x, y in zip(total, terms, strict=True)]
            halves.append(total)
        for i, template in enumerate(summed(halves)):
            part = (below, above)[i // 2][:, i % 2 * LANES : (i % 2 + 1) * LANES]
            edge_ref[q * SUB : (q + 1) * SUB, i * LANES : (i + 1) * LANES] = part - template

    by_walkers(walkers // SUB, evaluate, edge_block)
    below_noise, above_noise = below[:, 2 * LANES : 3 * LANES], above[:, 2 * LANES : 3 * LANES]
    noise = jnp.concatenate([below_noise, below_noise, above_noise, above_noise], axis=1)
    rim_ref[...] = (edge_ref[...] * noise).astype(BF16)

    mine = jnp.concatenate([weighted_ref[:, :LANES], weighted_ref[:, band_bins : band_bins + LANES]], axis=1)
    tail = jnp.concatenate([rim_ref[:, : 2 * LANES], mine], axis=1)
    group = 2 * SUB
    lane = lane_iota(group).astype(F32)
    first_noise = noise_ref[0:1, :LANES]
    chunk = prev_ref.shape[0]

    def spill(index):
        place = lax.broadcasted_iota(jnp.int32, (chunk, slots), 0) + (index * chunk + 1)
        chosen = jnp.where(rank == place.astype(F32), 1.0, 0.0).astype(BF16)
        cols = [lax.dot_general(chosen, x, OVER_LANES, preferred_element_type=F32) for x in bin_pieces]
        cols = cols[0] + cols[1] + cols[2]
        for start in range(0, chunk, group):
            at = slice(start, start + group)
            re, im, wrapped, _ = slot_wave(cols[at, :], lane)
            re, im = re.astype(BF16).astype(F32), im.astype(BF16).astype(F32)
            prev_power_ref[at, :] = (re * re + im * im) * jnp.where(wrapped, first_noise, below_noise)
            prev_ref[at, :LANES] = jnp.where(wrapped, 0.0, re).astype(BF16)
            prev_ref[at, LANES : 2 * LANES] = jnp.where(wrapped, 0.0, im).astype(BF16)
            prev_ref[at, 2 * LANES : 3 * LANES] = jnp.where(wrapped, re, 0.0).astype(BF16)
            prev_ref[at, 3 * LANES :] = jnp.where(wrapped, im, 0.0).astype(BF16)
        corr = lax.dot_general(tail, prev_ref[...], OVER_LANES, preferred_element_type=F32)
        half = accepted(corr, prev_power_ref[...]).astype(BF16)
        return jnp.dot(half, prev_ref[:, 2 * LANES :], preferred_element_type=F32)

    carried = spill(0)
    corr = lax.dot_general(weighted_ref[...], wave_ref[:, :own], OVER_LANES, preferred_element_type=F32)
    corr += lax.dot_general(rim_ref[:, 2 * LANES :], wave_ref[:, own:], OVER_LANES, preferred_element_type=F32)
    rim = wave_ref[:, own:].astype(F32)
    re, im = rim[:, :LANES], rim[:, LANES:]
    accept = accepted(corr, power_ref[...] + (re * re + im * im) * above_noise)
    accept = jnp.where(bins_ref[5:6, :] > 0.0, accept, 0.0)
    accept_ref[...] = accept
    half = accept.astype(BF16)
    carried = lax.fori_loop(1, (passing + chunk - 1) // chunk, lambda i, total: total + spill(i), carried)
    squares = jnp.zeros((walkers, LANES), F32)
    width = 2 * LANES
    for start in range(0, own, width):
        lanes = slice(start, start + width)
        new = resid_ref[:, lanes] - jnp.dot(half, wave_ref[:, lanes], preferred_element_type=F32)
        parts = [new[:, i : i + LANES] for i in range(0, width, LANES)]
        if start % band_bins == 0:
            part = start // band_bins
            parts[0] -= carried[:, part * LANES : (part + 1) * LANES]
        for i, piece in enumerate(parts):
            new_ref[:, start + i * LANES : start + (i + 1) * LANES] = piece
            squares += piece * piece
    total = jnp.sum(jnp.sum(squares, axis=0, keepdims=True), axis=1, keepdims=True)
    log_power = jnp.log(total * np.float32(1.0 / (walkers * own)) + np.float32(1e-6))
    log_ref[:, 0, :] = jnp.broadcast_to(log_power, (log_ref.shape[0], log_ref.shape[2]))


def output_kernel(bands, accept_ref, new_ref, prob_ref, out_ref, fit_ref):
    _, own = new_ref.shape
    half = own // 2
    prob_ref[...] = accept_ref[...]
    for part in range(2):
        out_ref[:, part, :] = new_ref[:, part * half : (part + 1) * half]
    fit = fit_rows(lax.axis_index(BOTH), bands)
    fit = jnp.broadcast_to(fit, (SUB, fit.shape[1])).T
    fit_ref[...] = jnp.broadcast_to(fit[:bands, 0:1], (bands, LANES))


def call(kernel, outs, args, scratch=(), smem=0, flops=0, name=None, hbm=False, last_any=False, alias=None):
    vmem = pl.BlockSpec(memory_space=pltpu.VMEM)
    rest = vmem
    if hbm:
        rest = pl.BlockSpec(memory_space=pl.ANY)
        args = [pltpu.with_memory_space_constraint(x, pltpu.HBM) if x.dtype != jnp.int32 or x.ndim > 1 else x for x in args]
    specs = [pl.BlockSpec(memory_space=pltpu.SMEM)] * smem + [rest] * (len(args) - smem)
    if last_any:
        specs[-1] = pl.BlockSpec(memory_space=pl.ANY)
    return pl.pallas_call(
        kernel,
        out_shape=outs,
        in_specs=specs,
        out_specs=[vmem] * len(outs),
        scratch_shapes=scratch,
        compiler_params=pltpu.CompilerParams(vmem_limit_bytes=16 * 2**20),
        cost_estimate=pl.CostEstimate(flops=flops, bytes_accessed=2**20, transcendentals=0),
        name=name,
        input_output_aliases=alias or {},
    )(*args)


def shape(dims, dtype):
    return jax.ShapeDtypeStruct(dims, dtype)


def local(
    data,
    inv_noise,
    mbh_amp,
    mbh_phase,
    bin_amp,
    bin_phase,
    bin_slope,
    bin_curve,
    bin_start,
    bin_count,
):
    band_bins = data.shape[1]
    slots = bin_amp.shape[1]
    rows, harmonics, powers, peers = mbh_amp.shape
    groups = lax.axis_size("group")
    walkers = rows * peers // 2
    bands = lax.axis_size(BOTH)
    own = 2 * band_bins

    span = padded(2 * powers * harmonics * rows)
    extra = 6 * LANES + 5 * slots
    cross_rows = -(-(extra - 3 * LANES) // span // SUB) * SUB
    packed, bins, data, noise = call(
        pack_kernel,
        [
            shape((peers, 1, 3 * span + extra), F32),
            shape((SUB, slots), F32),
            shape((2, band_bins), F32),
            shape((1, band_bins), F32),
        ],
        [
            mbh_amp.transpose(1, 2, 3, 0), mbh_phase.transpose(1, 2, 3, 0), data, inv_noise.reshape(-1, LANES),
            bin_amp, bin_phase, bin_slope, bin_curve, bin_start, bin_count,
        ],
        scratch=[
            pltpu.VMEM((harmonics, powers, peers, rows), F32),
            pltpu.VMEM((harmonics, powers, peers, rows), F32),
            pltpu.VMEM((4, 1, slots), F32),
            pltpu.VMEM((1, slots), jnp.int32),
            pltpu.VMEM((band_bins // LANES, LANES), BF16),
            pltpu.SMEM((1,), jnp.int32),
            pltpu.SemaphoreType.DMA((10,)),
        ],
        hbm=True,
        name="pack",
    )
    received = lax.all_to_all(packed, "shard", split_axis=0, concat_axis=0, tiled=True)
    received = received.reshape(peers, -1)
    wave, slot_power = call(
        wave_kernel,
        [shape((slots, own + 2 * LANES), BF16), shape((slots, LANES), F32)],
        [bins, noise],
        scratch=[pltpu.VMEM((slots, LANES), F32)],
        flops=10**9,
        name="waves",
    )
    (to_cross,) = call(
        cross_kernel,
        [shape((peers + cross_rows, span), F32)],
        [received, slot_power],
        last_any=True,
        name="cross",
    )
    pairs = [(g * peers, (g + 1) * peers) for g in range(groups - 1)]
    pairs += [(g * peers + peers - 1, (g - 1) * peers + peers - 1) for g in range(1, groups)]
    crossed = lax.ppermute(to_cross, BOTH, pairs)

    extras = received[:, 3 * span :]
    parts = [received[:, i * span : (i + 1) * span] for i in range(3)] + [crossed[:peers]]
    crossed_extra = crossed[peers:]
    if rows != 2 * SUB:

        def by_eight(x):
            x = x[:, : 2 * powers * harmonics * rows].reshape(peers, 2 * powers, harmonics, rows)
            x = x.transpose(1, 2, 0, 3).reshape(2 * powers, harmonics, walkers // SUB, SUB, 2)
            x = x.transpose(2, 0, 1, 4, 3).reshape(walkers // SUB, 2 * powers * harmonics * 2 * SUB)
            return jnp.pad(x, ((0, 0), (0, padded(x.shape[1]) - x.shape[1])))

        parts = [by_eight(x) for x in parts]

    resid, weighted = call(
        functools.partial(template_kernel, harmonics),
        [shape((walkers, own), F32), shape((walkers, own), BF16)],
        [parts[0], data, noise],
        scratch=[
            pltpu.VMEM((4, 2 * QUAD, walkers // SUB, LANES), F32),
            pltpu.VMEM((4, walkers // SUB * LANES, 2 * LANES), F32),
        ],
        flops=10**9,
        name="template",
    )
    accept, updated, log_power = call(
        functools.partial(score_kernel, harmonics, band_bins // LANES),
        [shape((walkers, slots), F32), shape((walkers, own), F32), shape((bands, 1, LANES), F32)],
        [
            weighted, resid, noise, bins, wave, slot_power, jnp.concatenate(parts[1:3], axis=1), extras,
            parts[3], crossed_extra,
        ],
        scratch=[
            pltpu.VMEM((min(slots, LANES), 4 * LANES), BF16),
            pltpu.VMEM((min(slots, LANES), LANES), F32),
            pltpu.VMEM((2, 2 * QUAD, walkers // SUB, LANES), F32),
            pltpu.VMEM((2, walkers // SUB * LANES, 2 * LANES), F32),
            pltpu.VMEM((walkers, 4 * LANES), F32),
            pltpu.VMEM((walkers, 4 * LANES), BF16),
        ],
        name="scores",
    )
    log_powers = lax.all_to_all(log_power, BOTH, split_axis=0, concat_axis=0, tiled=True)
    accept_prob, residual_new, fit = call(
        functools.partial(output_kernel, bands),
        [shape((walkers, slots), F32), shape((walkers, 2, band_bins), F32), shape((bands, LANES), F32)],
        [accept, updated],
        name="outputs",
    )
    noise_fit = jnp.sum(fit * log_powers[:, 0, :], axis=0)[:1]
    return (accept_prob, residual_new, noise_fit)


def solution(mesh):
    in_specs = (
        P(None, BOTH),
        P(BOTH),
        P("shard", None, None, "group"),
        P("shard", None, None, "group"),
        P(BOTH, None),
        P(BOTH, None),
        P(BOTH, None),
        P(BOTH, None),
        P(BOTH, None),
        P(BOTH),
    )
    out_specs = (P(None, BOTH), P(None, None, BOTH), P(BOTH))
    return jax.shard_map(local, mesh=mesh, in_specs=in_specs, out_specs=out_specs, check_vma=False)
```

time: 41.6 us -> 38.1 us (0.916)
  Pallas kernels: 16.3 us -> 12.7 us
    pallas_call x6, Pallas kernels: 16.3 us -> 12.7 us  [call(): pl.pallas_call(kernel, out_shape=outs, in_specs=specs, out_specs=[vmem] *...]
where the time goes in v3:
time: 38.1 us; the launch traced here: 37.8 us
  Pallas kernels  12.7 us (33%)
  starting transfers between devices  12.2 us (32%)
  waiting for transfers between devices  10.9 us (29%)
  between operations  1.37 us (4%)
  other arithmetic  0.53 us (1%)
    pallas_call x6, Pallas kernels, call(): pl.pallas_call(kernel, out_shape=outs, in_specs=specs, out_specs=[vmem] *...  12.7 us
    all_to_all x1, starting transfers between devices, local(): lax.all_to_all(packed, 'shard', split_axis=0, concat_axis=0, tiled=True)  7.29 us
    all_to_all x1, waiting for transfers between devices, local(): lax.all_to_all(packed, 'shard', split_axis=0, concat_axis=0, tiled=True)  5.7 us
    all_to_all x1, waiting for transfers between devices, local(): lax.all_to_all(log_power, BOTH, split_axis=0, concat_axis=0, tiled=True)  5.2 us
    all_to_all x1, starting transfers between devices, local(): lax.all_to_all(log_power, BOTH, split_axis=0, concat_axis=0, tiled=True)  3.64 us
    ppermute x1, starting transfers between devices, local(): crossed = lax.ppermute(to_cross, BOTH, pairs)  1.29 us
  transfers between devices with their start and end apart: 3, of which 2 were waited for; matrix products, arithmetic and copies ran while one was open for 0% of the time, Pallas kernels for 18%

profile of v3, /device:TPU:0, one launch (start us, length us, event | category | flops | bytes accessed | tf_op | source)
XLA Modules:
  0.0 37.8 jit_solution(8152486816490709435)
XLA Ops:
  1.3 1.9 %pack.1 = (f32[8,1,5248]{2,1,0:T(1,128)}, f32[8,512]{1,0:T(8,128)S(1)}, f32[2,1024]{1,0:T(2,128)S(1)}, f32[1,1024]{1,0:T(1,128)S(1)}) custom-call(f32[6,3,8,16]{3,2,1,0:T(8,128)} %bitcast.12, f32[6,3,8,16]{3,2,1,0:T(8,128)} %bitcast.13, f32[2,1024]{1,0:T(2,128)} %data_hbm.1, bf16[8,128]{1,0:T(8,128)(2,1)} %bitcast.15, f32[1,512]{1,0:T(1,128)} %bin_amp_hbm.1, ...), custom_call_target="tpu_custom_call" | custom-call | bytes 1048576 | tf_op jit(solution)/shard_map/pack/pallas_call | solution.py:514
  3.2 7.3 %all-to-all-start = ((f32[8,1,5248]{2,1,0:T(1,128)}), f32[8,1,5248]{2,1,0:T(1,128)S(1)}, u32[]{:S(2)}, u32[]{:S(2)}) async-start(f32[8,1,5248]{2,1,0:T(1,128)} %get-tuple-element.17), calls=%async_computation | async-start | bytes 335872 | tf_op jit(solution)/shard_map/all_to_all | solution.py:578
  10.4 1.9 %waves.1 = (bf16[512,2304]{1,0:T(8,128)(2,1)S(1)}, f32[512,128]{1,0:T(8,128)S(1)}) custom-call(f32[8,512]{1,0:T(8,128)S(1)} %get-tuple-element.22.bins_ref, f32[1,1024]{1,0:T(1,128)S(1)} %get-tuple-element.19.noise_ref), custom_call_target="tpu_custom_call" | custom-call | flops 1000000000 | bytes 1048576 | tf_op jit(solution)/shard_map/waves/pallas_call | solution.py:514
  12.3 5.7 %all-to-all-done = f32[8,1,5248]{2,1,0:T(1,128)S(1)} async-done(((f32[8,1,5248]{2,1,0:T(1,128)}), f32[8,1,5248]{2,1,0:T(1,128)S(1)}, u32[]{:S(2)}, u32[]{:S(2)}) %all-to-all-start) | async-done | bytes 167968 | tf_op jit(solution)/shard_map/all_to_all | solution.py:578
  18.1 1.3 %collective-permute-start = (f32[16,640]{1,0:T(8,128)S(1)}, f32[16,640]{1,0:T(8,128)S(1)}, u32[]{:S(2)}, u32[]{:S(2)}) collective-permute-start(f32[16,640]{1,0:T(8,128)S(1)} %cross.1), channel_id=1, source_target_pairs={{0,8},{8,16},{16,24},{15,7},{23,15},{31,23}} | collective-permute-start | bytes 122888 | tf_op jit(solution)/shard_map/ppermute | solution.py:597
  19.4 3.0 %template.1 = (f32[64,2048]{1,0:T(8,128)S(1)}, bf16[64,2048]{1,0:T(8,128)(2,1)S(1)}) custom-call(f32[8,640]{1,0:T(8,128)S(1)} %slice.23.rec_ref, f32[2,1024]{1,0:T(2,128)S(1)} %get-tuple-element.18.data_ref, f32[1,1024]{1,0:T(1,128)S(1)} %get-tuple-element.19.noise_ref), custom_call_target="tpu_custom_call" | custom-call | flops 1000000000 | bytes 1048576 | tf_op jit(solution)/shard_map/template/pallas_call | solution.py:514
  22.4 0.0 collective-permute-done
  22.4 4.1 %scores.1 = (f32[64,512]{1,0:T(8,128)S(1)}, f32[64,2048]{1,0:T(8,128)S(1)}, f32[32,1,128]{2,1,0:T(1,128)}) custom-call(bf16[64,2048]{1,0:T(8,128)(2,1)S(1)} %get-tuple-element.20.weighted_ref, f32[64,2048]{1,0:T(8,128)S(1)} %get-tuple-element.21.resid_ref, f32[1,1024]{1,0:T(1,128)S(1)} %get-tuple-element.19.noise_ref, ...), custom_call_target="tpu_custom_call" | custom-call | bytes 1048576 | tf_op jit(solution)/shard_map/scores/pallas_call | solution.py:514
  26.5 3.6 %all-to-all-start.1 = ((f32[32,1,128]{2,1,0:T(1,128)}), f32[32,1,128]{2,1,0:T(1,128)S(1)}, u32[]{:S(2)}, u32[]{:S(2)}) async-start(f32[32,1,128]{2,1,0:T(1,128)} %get-tuple-element.30), calls=%async_computation.1 | async-start | bytes 32768 | tf_op jit(solution)/shard_map/all_to_all | solution.py:640
  30.1 1.9 %outputs.1 = (f32[64,512]{1,0:T(8,128)}, f32[64,2,1024]{2,1,0:T(2,128)}, f32[32,128]{1,0:T(8,128)S(1)}) custom-call(f32[64,512]{1,0:T(8,128)S(1)} %get-tuple-element.25.accept_ref, f32[64,2048]{1,0:T(8,128)S(1)} %get-tuple-element.26.new_ref), custom_call_target="tpu_custom_call" | custom-call | bytes 1048576 | tf_op jit(solution)/shard_map/outputs/pallas_call | solution.py:514
  32.0 5.2 %all-to-all-done.1 = f32[32,1,128]{2,1,0:T(1,128)S(1)} async-done(((f32[32,1,128]{2,1,0:T(1,128)}), f32[32,1,128]{2,1,0:T(1,128)S(1)}, u32[]{:S(2)}, u32[]{:S(2)}) %all-to-all-start.1) | async-done | bytes 16416 | tf_op jit(solution)/shard_map/all_to_all | solution.py:640
  37.2 0.5 %multiply_reduce_fusion = f32[128]{0:T(128)} fusion(f32[32,128]{1,0:T(8,128)S(1)} %get-tuple-element.29, f32[32,128]{1,0:T(8,128)S(1)} %bitcast.14), kind=kLoop, calls=%fused_computation.1 | loop fusion | flops 8064 | bytes 33280 | tf_op jit(solution)/shard_map/reduce_sum | solution.py:647
  (6 shorter events, 0.1 us)
Async XLA Ops:
  3.2 14.9 %all-to-all-start = ((f32[8,1,5248]{2,1,0:T(1,128)}), f32[8,1,5248]{2,1,0:T(1,128)S(1)}, u32[]{:S(2)}, u32[]{:S(2)}) async-start(f32[8,1,5248]{2,1,0:T(1,128)} %get-tuple-element.17), calls=%async_computation | async-start | bytes 335872 | tf_op jit(solution)/shard_map/all_to_all | solution.py:578
  18.1 4.3 %collective-permute-start = (f32[16,640]{1,0:T(8,128)S(1)}, f32[16,640]{1,0:T(8,128)S(1)}, u32[]{:S(2)}, u32[]{:S(2)}) collective-permute-start(f32[16,640]{1,0:T(8,128)S(1)} %cross.1), channel_id=1, source_target_pairs={{0,8},{8,16},{16,24},{15,7},{23,15},{31,23}} | collective-permute-start | bytes 122888 | tf_op jit(solution)/shard_map/ppermute | solution.py:597
  26.5 10.8 %all-to-all-start.1 = ((f32[32,1,128]{2,1,0:T(1,128)}), f32[32,1,128]{2,1,0:T(1,128)S(1)}, u32[]{:S(2)}, u32[]{:S(2)}) async-start(f32[32,1,128]{2,1,0:T(1,128)} %get-tuple-element.30), calls=%async_computation.1 | async-start | bytes 32768 | tf_op jit(solution)/shard_map/all_to_all | solution.py:640

commit v4 on v3

--- a/solution.py
+++ b/solution.py
@@ -16,6 +16,7 @@
 F32 = jnp.float32
 BF16 = jnp.bfloat16
 BOTH = ("group", "shard")
+OVER_LANES = (((1,), (1,)), ((), ()))
 
 INV_TAU = np.float32(1.0 / (2.0 * math.pi))
 TAU_A = np.float32(round(2.0 * math.pi * 512) / 512)
@@ -299,7 +300,7 @@
     return scale * c, scale * s, wrapped, high
 
 
-def wave_kernel(bins_ref, noise_ref, wave_ref, power_ref, cols_ref):
+def wave_kernel(bins_ref, noise_ref, wave_ref, total_ref, rim_ref, cols_ref, power_ref):
     slots = bins_ref.shape[1]
     band_bins = noise_ref.shape[1]
     blocks = band_bins // LANES
@@ -322,10 +323,14 @@
             wave_ref[at, start : start + LANES] = jnp.where(inside, re, 0.0).astype(BF16)
             start += band_bins if k < blocks else LANES
             wave_ref[at, start : start + LANES] = jnp.where(inside, im, 0.0).astype(BF16)
-        power_ref[at, :] = (re * re + im * im) * noise
+        squares = re * re + im * im
+        power_ref[at, :] = squares * noise
+        for i, piece in enumerate(pieces(jnp.where(home == np.float32(blocks), squares, 0.0))):
+            rim_ref[at, i * LANES : (i + 1) * LANES] = piece.astype(BF16)
         return 0
 
     lax.fori_loop(0, slots // rows, block, 0, unroll=4)
+    total_ref[...] = row_sums(power_ref[...])
 
 
 def fit_rows(band, bands):
@@ -360,18 +365,17 @@
     return jnp.sum(basis * mine, axis=0, keepdims=True)
 
 
-OVER_LANES = (((1,), (1,)), ((), ()))
-
-
-def accepted(corr, power):
-    total = lax.dot_general(
-        jnp.ones((SUB, LANES), F32), power, OVER_LANES, precision=lax.Precision.HIGHEST, preferred_element_type=F32
-    )
-    return jax.nn.sigmoid(corr - np.float32(0.5) * total[0:1, :])
+def row_sums(x):
+    ones = jnp.ones((SUB, LANES), F32)
+    return lax.dot_general(ones, x, OVER_LANES, precision=lax.Precision.HIGHEST, preferred_element_type=F32)
+
+
+def accepted(corr, total):
+    return jax.nn.sigmoid(corr - np.float32(0.5) * total)
 
 
 def score_kernel(
-    harmonics, blocks, weighted_ref, resid_ref, noise_ref, bins_ref, wave_ref, power_ref, rec_ref, extra_ref,
+    harmonics, blocks, weighted_ref, resid_ref, noise_ref, bins_ref, wave_ref, total_ref, rim_squares_ref, rec_ref, extra_ref,
     cross_ref, cross_extra_ref, accept_ref, new_ref, log_ref,
     prev_ref, prev_power_ref, stage_ref, values_ref, edge_ref, rim_ref,
 ):
@@ -418,7 +422,12 @@
         pairs.append((phase_terms(k, band_bins, linear, reduced), amp_terms(k, band_bins, amps)))
     evaluate = evaluator(pairs, stage_ref, values_ref)
 
+    step = own // (walkers // SUB)
+    corr = [jnp.zeros((walkers, slots), F32)]
+
     def edge_block(q):
+        lanes = slice(q * step, (q + 1) * step)
+        corr[0] += lax.dot_general(weighted_ref[:, lanes], wave_ref[:, lanes], OVER_LANES, preferred_element_type=F32)
         halves = []
         for s in range(2):
             total = None
@@ -439,6 +448,14 @@
     noise = jnp.concatenate([below_noise, below_noise, above_noise, above_noise], axis=1)
     rim_ref[...] = (edge_ref[...] * noise).astype(BF16)
 
+    corr = corr[0] + lax.dot_general(rim_ref[:, 2 * LANES :], wave_ref[:, own:], OVER_LANES, preferred_element_type=F32)
+    noise = jnp.broadcast_to(jnp.concatenate([above_noise] * 3, axis=1), (2 * SUB, 3 * LANES)).astype(BF16)
+    total = lax.dot_general(noise, rim_squares_ref[...], OVER_LANES, preferred_element_type=F32)
+    accept = accepted(corr, total_ref[0:1, :] + total[0:1, :])
+    accept = jnp.where(bins_ref[5:6, :] > 0.0, accept, 0.0)
+    accept_ref[...] = accept
+    half = accept.astype(BF16)
+
     mine = jnp.concatenate([weighted_ref[:, :LANES], weighted_ref[:, band_bins : band_bins + LANES]], axis=1)
     tail = jnp.concatenate([rim_ref[:, : 2 * LANES], mine], axis=1)
     group = 2 * SUB
@@ -446,46 +463,59 @@
     first_noise = noise_ref[0:1, :LANES]
     chunk = prev_ref.shape[0]
 
-    def spill(index):
+    def chosen_slots(index):
         place = lax.broadcasted_iota(jnp.int32, (chunk, slots), 0) + (index * chunk + 1)
         chosen = jnp.where(rank == place.astype(F32), 1.0, 0.0).astype(BF16)
         cols = [lax.dot_general(chosen, x, OVER_LANES, preferred_element_type=F32) for x in bin_pieces]
-        cols = cols[0] + cols[1] + cols[2]
+        return cols[0] + cols[1] + cols[2]
+
+    def fill(cols, start):
+        at = slice(start, start + group)
+        re, im, wrapped, _ = slot_wave(cols[at, :], lane)
+        re, im = re.astype(BF16).astype(F32), im.astype(BF16).astype(F32)
+        prev_power_ref[at, :] = (re * re + im * im) * jnp.where(wrapped, first_noise, below_noise)
+        prev_ref[at, :LANES] = jnp.where(wrapped, 0.0, re).astype(BF16)
+        prev_ref[at, LANES : 2 * LANES] = jnp.where(wrapped, 0.0, im).astype(BF16)
+        prev_ref[at, 2 * LANES : 3 * LANES] = jnp.where(wrapped, re, 0.0).astype(BF16)
+        prev_ref[at, 3 * LANES :] = jnp.where(wrapped, im, 0.0).astype(BF16)
+
+    def spilled():
+        corr = lax.dot_general(tail, prev_ref[...], OVER_LANES, preferred_element_type=F32)
+        half = accepted(corr, row_sums(prev_power_ref[...])[0:1, :]).astype(BF16)
+        return jnp.dot(half, prev_ref[:, 2 * LANES :], preferred_element_type=F32)
+
+    def spill(index, carried):
+        cols = chosen_slots(index)
         for start in range(0, chunk, group):
-            at = slice(start, start + group)
-            re, im, wrapped, _ = slot_wave(cols[at, :], lane)
-            re, im = re.astype(BF16).astype(F32), im.astype(BF16).astype(F32)
-            prev_power_ref[at, :] = (re * re + im * im) * jnp.where(wrapped, first_noise, below_noise)
-            prev_ref[at, :LANES] = jnp.where(wrapped, 0.0, re).astype(BF16)
-            prev_ref[at, LANES : 2 * LANES] = jnp.where(wrapped, 0.0, im).astype(BF16)
-            prev_ref[at, 2 * LANES : 3 * LANES] = jnp.where(wrapped, re, 0.0).astype(BF16)
-            prev_ref[at, 3 * LANES :] = jnp.where(wrapped, im, 0.0).astype(BF16)
-        corr = lax.dot_general(tail, prev_ref[...], OVER_LANES, preferred_element_type=F32)
-        half = accepted(corr, prev_power_ref[...]).astype(BF16)
-        return jnp.dot(half, prev_ref[:, 2 * LANES :], preferred_element_type=F32)
-
-    carried = spill(0)
-    corr = lax.dot_general(weighted_ref[...], wave_ref[:, :own], OVER_LANES, preferred_element_type=F32)
-    corr += lax.dot_general(rim_ref[:, 2 * LANES :], wave_ref[:, own:], OVER_LANES, preferred_element_type=F32)
-    rim = wave_ref[:, own:].astype(F32)
-    re, im = rim[:, :LANES], rim[:, LANES:]
-    accept = accepted(corr, power_ref[...] + (re * re + im * im) * above_noise)
-    accept = jnp.where(bins_ref[5:6, :] > 0.0, accept, 0.0)
-    accept_ref[...] = accept
-    half = accept.astype(BF16)
-    carried = lax.fori_loop(1, (passing + chunk - 1) // chunk, lambda i, total: total + spill(i), carried)
-    squares = jnp.zeros((walkers, LANES), F32)
+            fill(cols, start)
+        return carried + spilled()
+
+    squares = [jnp.zeros((walkers, LANES), F32)]
     width = 2 * LANES
-    for start in range(0, own, width):
+
+    def update(start, carried=None):
         lanes = slice(start, start + width)
         new = resid_ref[:, lanes] - jnp.dot(half, wave_ref[:, lanes], preferred_element_type=F32)
         parts = [new[:, i : i + LANES] for i in range(0, width, LANES)]
-        if start % band_bins == 0:
+        if carried is not None:
             part = start // band_bins
             parts[0] -= carried[:, part * LANES : (part + 1) * LANES]
         for i, piece in enumerate(parts):
             new_ref[:, start + i * LANES : start + (i + 1) * LANES] = piece
-            squares += piece * piece
+            squares[0] += piece * piece
+
+    cols = chosen_slots(0)
+    fills = list(range(0, chunk, group))
+    starts = [start for start in range(0, own, width) if start % band_bins]
+    for i in range(max(len(fills), len(starts))):
+        if i < len(starts):
+            update(starts[i])
+        if i < len(fills):
+            fill(cols, fills[i])
+    carried = lax.fori_loop(1, (passing + chunk - 1) // chunk, spill, spilled())
+    update(0, carried)
+    update(band_bins, carried)
+    squares = squares[0]
     total = jnp.sum(jnp.sum(squares, axis=0, keepdims=True), axis=1, keepdims=True)
     log_power = jnp.log(total * np.float32(1.0 / (walkers * own)) + np.float32(1e-6))
     log_ref[:, 0, :] = jnp.broadcast_to(log_power, (log_ref.shape[0], log_ref.shape[2]))
@@ -577,11 +607,11 @@
     )
     received = lax.all_to_all(packed, "shard", split_axis=0, concat_axis=0, tiled=True)
     received = received.reshape(peers, -1)
-    wave, slot_power = call(
+    wave, slot_power, rim_squares = call(
         wave_kernel,
-        [shape((slots, own + 2 * LANES), BF16), shape((slots, LANES), F32)],
+        [shape((slots, own + 2 * LANES), BF16), shape((SUB, slots), F32), shape((slots, 3 * LANES), BF16)],
         [bins, noise],
-        scratch=[pltpu.VMEM((slots, LANES), F32)],
+        scratch=[pltpu.VMEM((slots, LANES), F32), pltpu.VMEM((slots, LANES), F32)],
         flops=10**9,
         name="waves",
     )
@@ -624,7 +654,7 @@
         functools.partial(score_kernel, harmonics, band_bins // LANES),
         [shape((walkers, slots), F32), shape((walkers, own), F32), shape((bands, 1, LANES), F32)],
         [
-            weighted, resid, noise, bins, wave, slot_power, jnp.concatenate(parts[1:3], axis=1), extras,
+            weighted, resid, noise, bins, wave, slot_power, rim_squares, jnp.concatenate(parts[1:3], axis=1), extras,
             parts[3], crossed_extra,
         ],
         scratch=[

time: 38.1 us -> 37.3 us (0.979)
  waiting for transfers between devices: 10.9 us -> 10.5 us
  Pallas kernels: 12.7 us -> 12.3 us
    all_to_all x1, waiting for transfers between devices: 5.7 us -> 5.31 us  [local(): lax.all_to_all(packed, 'shard', split_axis=0, concat_axis=0, tiled=True)]
  transfers between devices with their start and end apart: 3 -> 3, of which waited for: 2 -> 2; matrix products, arithmetic and copies ran while one was open for 0% -> 0% of each run, Pallas kernels for 18% -> 19%
where the time goes in v4:
time: 37.3 us; the launch traced here: 37 us
  Pallas kernels  12.3 us (33%)
  starting transfers between devices  12.2 us (33%)
  waiting for transfers between devices  10.5 us (28%)
  between operations  1.36 us (4%)
  other arithmetic  0.53 us (1%)
    pallas_call x6, Pallas kernels, call(): pl.pallas_call(kernel, out_shape=outs, in_specs=specs, out_specs=[vmem] *...  12.3 us
    all_to_all x1, starting transfers between devices, local(): lax.all_to_all(packed, 'shard', split_axis=0, concat_axis=0, tiled=True)  7.29 us
    all_to_all x1, waiting for transfers between devices, local(): lax.all_to_all(packed, 'shard', split_axis=0, concat_axis=0, tiled=True)  5.31 us
    all_to_all x1, waiting for transfers between devices, local(): lax.all_to_all(log_power, BOTH, split_axis=0, concat_axis=0, tiled=True)  5.2 us
    all_to_all x1, starting transfers between devices, local(): lax.all_to_all(log_power, BOTH, split_axis=0, concat_axis=0, tiled=True)  3.64 us
    ppermute x1, starting transfers between devices, local(): crossed = lax.ppermute(to_cross, BOTH, pairs)  1.29 us
  transfers between devices with their start and end apart: 3, of which 2 were waited for; matrix products, arithmetic and copies ran while one was open for 0% of the time, Pallas kernels for 19%

profile of v4, /device:TPU:0, one launch (start us, length us, event | category | flops | bytes accessed | tf_op | source)
XLA Modules:
  0.0 37.0 jit_solution(11477892671783163393)
XLA Ops:
  1.3 1.9 %pack.1 = (f32[8,1,5248]{2,1,0:T(1,128)}, f32[8,512]{1,0:T(8,128)S(1)}, f32[2,1024]{1,0:T(2,128)S(1)}, f32[1,1024]{1,0:T(1,128)S(1)}) custom-call(f32[6,3,8,16]{3,2,1,0:T(8,128)} %bitcast.12, f32[6,3,8,16]{3,2,1,0:T(8,128)} %bitcast.13, f32[2,1024]{1,0:T(2,128)} %data_hbm.1, bf16[8,128]{1,0:T(8,128)(2,1)} %bitcast.15, f32[1,512]{1,0:T(1,128)} %bin_amp_hbm.1, ...), custom_call_target="tpu_custom_call" | custom-call | bytes 1048576 | tf_op jit(solution)/shard_map/pack/pallas_call | solution.py:544
  3.2 7.3 %all-to-all-start = ((f32[8,1,5248]{2,1,0:T(1,128)}), f32[8,1,5248]{2,1,0:T(1,128)S(1)}, u32[]{:S(2)}, u32[]{:S(2)}) async-start(f32[8,1,5248]{2,1,0:T(1,128)} %get-tuple-element.18), calls=%async_computation | async-start | bytes 335872 | tf_op jit(solution)/shard_map/all_to_all | solution.py:608
  10.4 2.3 %waves.1 = (bf16[512,2304]{1,0:T(8,128)(2,1)S(1)}, f32[8,512]{1,0:T(8,128)S(1)}, bf16[512,384]{1,0:T(8,128)(2,1)S(1)}) custom-call(f32[8,512]{1,0:T(8,128)S(1)} %get-tuple-element.23.bins_ref, f32[1,1024]{1,0:T(1,128)S(1)} %get-tuple-element.20.noise_ref), custom_call_target="tpu_custom_call" | custom-call | flops 1000000000 | bytes 1048576 | tf_op jit(solution)/shard_map/waves/pallas_call | solution.py:544
  12.7 5.3 %all-to-all-done = f32[8,1,5248]{2,1,0:T(1,128)S(1)} async-done(((f32[8,1,5248]{2,1,0:T(1,128)}), f32[8,1,5248]{2,1,0:T(1,128)S(1)}, u32[]{:S(2)}, u32[]{:S(2)}) %all-to-all-start) | async-done | bytes 167968 | tf_op jit(solution)/shard_map/all_to_all | solution.py:608
  18.1 1.3 %collective-permute-start = (f32[16,640]{1,0:T(8,128)S(1)}, f32[16,640]{1,0:T(8,128)S(1)}, u32[]{:S(2)}, u32[]{:S(2)}) collective-permute-start(f32[16,640]{1,0:T(8,128)S(1)} %cross.1), channel_id=1, source_target_pairs={{0,8},{8,16},{16,24},{15,7},{23,15},{31,23}} | collective-permute-start | bytes 122888 | tf_op jit(solution)/shard_map/ppermute | solution.py:627
  19.4 3.0 %template.1 = (f32[64,2048]{1,0:T(8,128)S(1)}, bf16[64,2048]{1,0:T(8,128)(2,1)S(1)}) custom-call(f32[8,640]{1,0:T(8,128)S(1)} %slice.23.rec_ref, f32[2,1024]{1,0:T(2,128)S(1)} %get-tuple-element.19.data_ref, f32[1,1024]{1,0:T(1,128)S(1)} %get-tuple-element.20.noise_ref), custom_call_target="tpu_custom_call" | custom-call | flops 1000000000 | bytes 1048576 | tf_op jit(solution)/shard_map/template/pallas_call | solution.py:544
  22.4 0.0 collective-permute-done
  22.4 3.3 %scores.1 = (f32[64,512]{1,0:T(8,128)S(1)}, f32[64,2048]{1,0:T(8,128)S(1)}, f32[32,1,128]{2,1,0:T(1,128)}) custom-call(bf16[64,2048]{1,0:T(8,128)(2,1)S(1)} %get-tuple-element.21.weighted_ref, f32[64,2048]{1,0:T(8,128)S(1)} %get-tuple-element.22.resid_ref, f32[1,1024]{1,0:T(1,128)S(1)} %get-tuple-element.20.noise_ref, ...), custom_call_target="tpu_custom_call" | custom-call | bytes 1048576 | tf_op jit(solution)/shard_map/scores/pallas_call | solution.py:544
  25.7 3.6 %all-to-all-start.1 = ((f32[32,1,128]{2,1,0:T(1,128)}), f32[32,1,128]{2,1,0:T(1,128)S(1)}, u32[]{:S(2)}, u32[]{:S(2)}) async-start(f32[32,1,128]{2,1,0:T(1,128)} %get-tuple-element.32), calls=%async_computation.1 | async-start | bytes 32768 | tf_op jit(solution)/shard_map/all_to_all | solution.py:670
  29.4 1.9 %outputs.1 = (f32[64,512]{1,0:T(8,128)}, f32[64,2,1024]{2,1,0:T(2,128)}, f32[32,128]{1,0:T(8,128)S(1)}) custom-call(f32[64,512]{1,0:T(8,128)S(1)} %get-tuple-element.27.accept_ref, f32[64,2048]{1,0:T(8,128)S(1)} %get-tuple-element.28.new_ref), custom_call_target="tpu_custom_call" | custom-call | bytes 1048576 | tf_op jit(solution)/shard_map/outputs/pallas_call | solution.py:544
  31.3 5.2 %all-to-all-done.1 = f32[32,1,128]{2,1,0:T(1,128)S(1)} async-done(((f32[32,1,128]{2,1,0:T(1,128)}), f32[32,1,128]{2,1,0:T(1,128)S(1)}, u32[]{:S(2)}, u32[]{:S(2)}) %all-to-all-start.1) | async-done | bytes 16416 | tf_op jit(solution)/shard_map/all_to_all | solution.py:670
  36.5 0.5 %multiply_reduce_fusion = f32[128]{0:T(128)} fusion(f32[32,128]{1,0:T(8,128)S(1)} %get-tuple-element.31, f32[32,128]{1,0:T(8,128)S(1)} %bitcast.14), kind=kLoop, calls=%fused_computation.1 | loop fusion | flops 8064 | bytes 33280 | tf_op jit(solution)/shard_map/reduce_sum | solution.py:677
  (6 shorter events, 0.1 us)
Async XLA Ops:
  3.2 14.9 %all-to-all-start = ((f32[8,1,5248]{2,1,0:T(1,128)}), f32[8,1,5248]{2,1,0:T(1,128)S(1)}, u32[]{:S(2)}, u32[]{:S(2)}) async-start(f32[8,1,5248]{2,1,0:T(1,128)} %get-tuple-element.18), calls=%async_computation | async-start | bytes 335872 | tf_op jit(solution)/shard_map/all_to_all | solution.py:608
  18.1 4.3 %collective-permute-start = (f32[16,640]{1,0:T(8,128)S(1)}, f32[16,640]{1,0:T(8,128)S(1)}, u32[]{:S(2)}, u32[]{:S(2)}) collective-permute-start(f32[16,640]{1,0:T(8,128)S(1)} %cross.1), channel_id=1, source_target_pairs={{0,8},{8,16},{16,24},{15,7},{23,15},{31,23}} | collective-permute-start | bytes 122888 | tf_op jit(solution)/shard_map/ppermute | solution.py:627
  25.7 10.8 %all-to-all-start.1 = ((f32[32,1,128]{2,1,0:T(1,128)}), f32[32,1,128]{2,1,0:T(1,128)S(1)}, u32[]{:S(2)}, u32[]{:S(2)}) async-start(f32[32,1,128]{2,1,0:T(1,128)} %get-tuple-element.32), calls=%async_computation.1 | async-start | bytes 32768 | tf_op jit(solution)/shard_map/all_to_all | solution.py:670

commit v5 on v4

--- a/solution.py
+++ b/solution.py
@@ -68,7 +68,7 @@
 
 def pack_kernel(
     amp_hbm, phase_hbm, data_hbm, noise_hbm, bin_amp_hbm, bin_phase_hbm, bin_slope_hbm, bin_curve_hbm,
-    bin_start_hbm, count_hbm, packed_ref, bins_ref, data_ref, noise_ref,
+    bin_start_hbm, count_hbm, packed_ref, bins_ref, data_ref, noise_ref, own_ref,
     amp_ref, phase_ref, rows_ref, start_ref, raw_noise_ref, count_ref, sems,
 ):
     copies = [
@@ -104,10 +104,11 @@
     noise = jnp.concatenate([raw_noise[i : i + 1] for i in range(raw_noise.shape[0])], axis=1)
     noise_ref[...] = noise
     start = 3 * span
-    for lanes in (slice(0, LANES), slice(band_bins - LANES, band_bins)):
-        for row in (data_ref[0:1, lanes], data_ref[1:2, lanes], noise[:, lanes]):
-            packed_ref[:, 0, start : start + LANES] = jnp.broadcast_to(row, (peers, LANES))
-            start += LANES
+    before = lax.rem(lax.axis_index("shard") + peers - 1, peers)
+    for i, row in enumerate((data_ref[0:1, :], data_ref[1:2, :], noise)):
+        packed_ref[:, 0, start : start + LANES] = jnp.broadcast_to(row[:, band_bins - LANES :], (peers, LANES))
+        packed_ref[pl.ds(before, 1), 0, start : start + LANES] = row[:, :LANES]
+        start += LANES
     for row in slot_rows:
         packed_ref[:, 0, start : start + slots] = jnp.broadcast_to(row, (peers, slots))
         start += slots
@@ -123,20 +124,20 @@
         blocks = [packed[:, i : i + LANES] for i in range(0, span, LANES)]
         blocks = [jnp.take_along_axis(x, order, axis=1, mode="promise_in_bounds") for x in blocks]
         packed = jnp.concatenate(blocks, axis=1)
+    own_ref[...] = packed
     packed_ref[:, 0, :span] = packed
     packed_ref[:, 0, span : 2 * span] = jnp.concatenate([packed[-1:], packed[:-1]], axis=0)
     packed_ref[:, 0, 2 * span : 3 * span] = jnp.concatenate([packed[1:], packed[:1]], axis=0)
 
 
-def cross_kernel(rec_ref, _, out_ref):
+def cross_kernel(rec_ref, *refs):
+    out_ref = refs[-1]
     peers = rec_ref.shape[0]
     span = out_ref.shape[1]
     first = lax.axis_index("shard") == 0
     out_ref[:peers, :] = jnp.where(first, rec_ref[:, span : 2 * span], rec_ref[:, 2 * span : 3 * span])
-    start = 3 * span
-    rim = rec_ref[0:1, start : start + 3 * LANES]
-    start += 3 * LANES
-    row = rec_ref[peers - 1 : peers, start:]
+    row = rec_ref[peers - 1 : peers, 3 * span :]
+    rim = rec_ref[0:1, 3 * span : 3 * span + 3 * LANES]
     row = jnp.concatenate([jnp.where(first, row[:, : 3 * LANES], rim), row[:, 3 * LANES :]], axis=1)
     for i, at in enumerate(range(0, row.shape[1], span)):
         lanes = min(span, row.shape[1] - at)
@@ -174,39 +175,43 @@
     return [high, middle, (rest - middle).astype(BF16).astype(F32)]
 
 
-QUAD = 16
-
-
-def quad_rows(terms):
-    terms = [pieces(x) for x in terms]
-    rows = [*terms[0], *terms[1], *terms[2], *terms[2]]
-    return rows + [jnp.zeros_like(rows[0])] * (QUAD - len(rows))
-
-
-def lane_powers():
-    row = lax.broadcasted_iota(jnp.int32, (QUAD, LANES), 0)
-    lane = lax.broadcasted_iota(jnp.int32, (QUAD, LANES), 1)
+def piece_rows(terms):
+    rows = []
+    for kind, term in zip(((0,), (1,), (2, 3)), terms):
+        parts = pieces(term)
+        rows += [(part, power) for power in kind for part in parts]
+    return rows
+
+
+def evaluator(quantities, stage_ref, values_ref):
+    lane = lax.broadcasted_iota(jnp.int32, (1, LANES), 1)
     low = lane * lane % LANES
-    table = jnp.where(row < 3, 1, jnp.where(row < 6, lane, jnp.where(row < 9, lane * lane - low, low)))
-    table = jnp.where(row < 12, table, 0).astype(F32)
-    zero = jnp.zeros((QUAD, LANES), F32)
-    upper = jnp.concatenate([table, zero], axis=1)
-    lower = jnp.concatenate([zero, table], axis=1)
-    return jnp.concatenate([upper, lower], axis=0).astype(BF16)
-
-
-def evaluator(pairs, stage_ref, values_ref):
-    table = lane_powers()
-    for pair, (first, second) in enumerate(pairs):
-        for i, row in enumerate(quad_rows(first) + quad_rows(second)):
-            stage_ref[pair, i] = row
+    powers = [x.astype(F32) for x in (jnp.ones_like(lane), lane, lane * lane - low, low)]
+    count = stage_ref.shape[0]
+    table, spans = [], []
+    for terms in quantities:
+        start = len(table)
+        for part, power in piece_rows(terms):
+            stage_ref[len(table)] = part
+            table.append(powers[power])
+        spans.append((start, len(table)))
+    for i in range(len(table), count):
+        stage_ref[i] = jnp.zeros(stage_ref.shape[1:], F32)
+        table.append(jnp.zeros((1, LANES), F32))
+    table = jnp.concatenate(table, axis=0)
+    row = lax.broadcasted_iota(jnp.int32, (count, LANES), 0)
+    blocks = [jnp.where((row >= start) & (row < stop), table, 0.0) for start, stop in spans]
+    table = jnp.concatenate(blocks, axis=1).astype(BF16)
 
     def evaluate(q):
-        for pair in range(len(pairs)):
-            rows = stage_ref[pair, :, q, :].T.astype(BF16)
-            values_ref[pair, q * LANES : (q + 1) * LANES, :] = jnp.dot(rows, table, preferred_element_type=F32)
+        rows = stage_ref[:, q, :].T.astype(BF16)
+        values_ref[q * LANES : (q + 1) * LANES, :] = jnp.dot(rows, table, preferred_element_type=F32)
 
     return evaluate
+
+
+def stage_rows(count):
+    return -(-count // (2 * SUB)) * 2 * SUB
 
 
 def by_walkers(count, evaluate, block):
@@ -221,23 +226,23 @@
     return [a.astype(BF16).astype(F32) + b.astype(BF16).astype(F32) for a, b in zip(*halves, strict=True)]
 
 
-def template_kernel(harmonics, rec_ref, data_ref, noise_ref, resid_ref, weighted_ref, stage_ref, values_ref):
+def template_blocks(harmonics, rec, rows, data_ref, stage_ref, values_ref, emit):
     band_bins = data_ref.shape[1]
     blocks = band_bins // LANES
     share = LANES / band_bins
-    amps, linear, reduced = coefficients(rec_ref, harmonics * 2 * SUB, band_bins)
+    amps, linear, reduced = coefficients(rec, harmonics * 2 * SUB, band_bins)
     _, f1, f2 = reduced
-    zero = jnp.zeros_like(f1)
     twist_re, twist_im = cis_turns(frac(np.float32(2.0) * f2))
-    step = [frac(f1 + f2), linear[1] * np.float32(2 * share / band_bins) * INV_TAU, zero]
     now, then = amp_terms(0, band_bins, amps), amp_terms(1, band_bins, amps)
-    grow = [then[0] - now[0], amps[2] * np.float32(2 * share / band_bins), zero]
     evaluate = evaluator(
         [
-            (phase_terms(0, band_bins, linear, reduced), now),
-            (step, grow),
-            ([twist_re, zero, zero], [twist_im, zero, zero]),
-            ([amps[2] * np.float32(2 * share * share), zero, zero], [zero] * 3),
+            phase_terms(0, band_bins, linear, reduced),
+            now,
+            [frac(f1 + f2), linear[1] * np.float32(2 * share / band_bins) * INV_TAU],
+            [then[0] - now[0], amps[2] * np.float32(2 * share / band_bins)],
+            [twist_re],
+            [twist_im],
+            [amps[2] * np.float32(2 * share * share)],
         ],
         stage_ref,
         values_ref,
@@ -249,10 +254,8 @@
             total = [None] * (2 * blocks)
             for h in range(harmonics):
                 at = pl.ds(q * LANES + (2 * h + s) * SUB, SUB)
-                phase, a = values_ref[0, at, :LANES], values_ref[0, at, LANES:]
-                w_phase, da = values_ref[1, at, :LANES], values_ref[1, at, LANES:]
-                twist_re, twist_im = values_ref[2, at, :LANES], values_ref[2, at, LANES:]
-                dda = values_ref[3, at, :LANES]
+                values = [values_ref[at, i * LANES : (i + 1) * LANES] for i in range(7)]
+                phase, a, w_phase, da, twist_re, twist_im, dda = values
                 z_re, z_im = cis_turns(frac(phase))
                 w_re, w_im = cis_turns(frac(w_phase))
                 for k in range(blocks):
@@ -266,14 +269,44 @@
                         w_re, w_im = w_re * twist_re - w_im * twist_im, w_re * twist_im + w_im * twist_re
                         da = da + dda
             halves.append(total)
-        row = q * SUB
         for i, template in enumerate(summed(halves)):
             here = i // 2 * LANES
             there = i % 2 * band_bins + here
-            part = data_ref[i % 2 : i % 2 + 1, here : here + LANES]
-            resid_ref[pl.ds(row, SUB), there : there + LANES] = part - template
-
-    by_walkers(rec_ref.shape[0], evaluate, block)
+            emit(q, slice(there, there + LANES), data_ref[i % 2 : i % 2 + 1, here : here + LANES] - template)
+
+    by_walkers(rows, evaluate, block)
+
+
+def own_kernel(harmonics, rec_ref, data_ref, resid_ref, stage_ref, values_ref):
+    def emit(_, lanes, residual):
+        resid_ref[:, lanes] = residual
+
+    rec = rec_ref[pl.ds(lax.axis_index("shard"), 1), :]
+    template_blocks(harmonics, rec, 1, data_ref, stage_ref, values_ref, emit)
+
+
+def template_kernel(harmonics, own_done, *refs):
+    if own_done:
+        rec_ref, data_ref, noise_ref, own_ref, resid_ref, weighted_ref, stage_ref, values_ref = refs
+    else:
+        rec_ref, data_ref, noise_ref, resid_ref, weighted_ref, stage_ref, values_ref = refs
+    band_bins = data_ref.shape[1]
+    count = rec_ref.shape[0]
+    rec = rec_ref[...]
+    skip = 0
+    if own_done:
+        place = lax.axis_index("shard")
+        rec = pltpu.roll(rec, lax.rem(2 * count - 1 - place, count), 0)
+        resid_ref[pl.ds(pl.multiple_of(place * SUB, SUB), SUB), :] = own_ref[...]
+        skip = 1
+
+    def emit(q, lanes, residual):
+        row = q * SUB
+        if own_done:
+            row = pl.multiple_of(lax.rem(place + 1 + q, count) * SUB, SUB)
+        resid_ref[pl.ds(row, SUB), lanes] = residual
+
+    template_blocks(harmonics, rec, count - skip, data_ref, stage_ref, values_ref, emit)
     for part in range(2):
         lanes = slice(part * band_bins, (part + 1) * band_bins)
         weighted_ref[:, lanes] = (resid_ref[:, lanes] * noise_ref[0:1, :]).astype(BF16)
@@ -395,7 +428,7 @@
     crossed = jnp.concatenate([cross_extra_ref[i : i + 1, :] for i in range(rows)], axis=1)
     above = jnp.where(final, crossed[:, : 3 * LANES], extra_ref[pl.ds(source, 1), : 3 * LANES])
     source = lax.rem(place + sources - 1, sources)
-    below = extra_ref[pl.ds(source, 1), 3 * LANES :]
+    below = extra_ref[pl.ds(source, 1), :]
     rows = -(-below.shape[1] // cross_extra_ref.shape[1])
     crossed = jnp.concatenate([cross_extra_ref[i : i + 1, :] for i in range(rows)], axis=1)
     below = jnp.where(first, crossed[:, : below.shape[1]], below)
@@ -416,14 +449,55 @@
     rank = jnp.where(passes, jnp.concatenate(ranks, axis=1), 0.0)
     bin_pieces = [x.astype(BF16) for x in pieces(bins)]
 
-    pairs = []
+    below_noise, above_noise = below[:, 2 * LANES : 3 * LANES], above[:, 2 * LANES : 3 * LANES]
+    group = 2 * SUB
+    lane = lane_iota(group).astype(F32)
+    first_noise = noise_ref[0:1, :LANES]
+    chunk = prev_ref.shape[0]
+    tail = []
+
+    def chosen_slots(index):
+        place = lax.broadcasted_iota(jnp.int32, (chunk, slots), 0) + (index * chunk + 1)
+        chosen = jnp.where(rank == place.astype(F32), 1.0, 0.0).astype(BF16)
+        cols = [lax.dot_general(chosen, x, OVER_LANES, preferred_element_type=F32) for x in bin_pieces]
+        return cols[0] + cols[1] + cols[2]
+
+    def fill(cols, start):
+        at = slice(start, start + group)
+        re, im, wrapped, _ = slot_wave(cols[at, :], lane)
+        re, im = re.astype(BF16).astype(F32), im.astype(BF16).astype(F32)
+        power = (re * re + im * im) * jnp.where(wrapped, first_noise, below_noise)
+        for i, piece in enumerate(pieces(power)):
+            prev_power_ref[at, i * LANES : (i + 1) * LANES] = piece.astype(BF16)
+        prev_ref[at, :LANES] = jnp.where(wrapped, 0.0, re).astype(BF16)
+        prev_ref[at, LANES : 2 * LANES] = jnp.where(wrapped, 0.0, im).astype(BF16)
+        prev_ref[at, 2 * LANES : 3 * LANES] = jnp.where(wrapped, re, 0.0).astype(BF16)
+        prev_ref[at, 3 * LANES :] = jnp.where(wrapped, im, 0.0).astype(BF16)
+
+    def spilled():
+        corr = lax.dot_general(tail[0], prev_ref[...], OVER_LANES, preferred_element_type=F32)
+        ones = jnp.ones((2 * SUB, prev_power_ref.shape[1]), BF16)
+        total = lax.dot_general(ones, prev_power_ref[...], OVER_LANES, preferred_element_type=F32)
+        half = accepted(corr, total[0:1, :]).astype(BF16)
+        return jnp.dot(half, prev_ref[:, 2 * LANES :], preferred_element_type=F32)
+
+    def spill(index, carried):
+        cols = chosen_slots(index)
+        for start in range(0, chunk, group):
+            fill(cols, start)
+        return carried + spilled()
+
+    quantities = []
     for k, rec in ((last, below_rec), (0, above_rec)):
         amps, linear, reduced = coefficients(rec, harmonics * 2 * SUB, band_bins)
-        pairs.append((phase_terms(k, band_bins, linear, reduced), amp_terms(k, band_bins, amps)))
-    evaluate = evaluator(pairs, stage_ref, values_ref)
+        quantities += [phase_terms(k, band_bins, linear, reduced), amp_terms(k, band_bins, amps)]
+    evaluate = evaluator(quantities, stage_ref, values_ref)
 
     step = own // (walkers // SUB)
     corr = [jnp.zeros((walkers, slots), F32)]
+
+    cols = chosen_slots(0)
+    fills = list(range(0, chunk, group))
 
     def edge_block(q):
         lanes = slice(q * step, (q + 1) * step)
@@ -435,18 +509,21 @@
                 at = pl.ds(q * LANES + (2 * h + s) * SUB, SUB)
                 terms = []
                 for i in range(2):
-                    a = values_ref[i, at, LANES:]
-                    terms += [a * x for x in cis_turns(frac(values_ref[i, at, :LANES]))]
+                    phase, a = (values_ref[at, (2 * i + j) * LANES : (2 * i + j + 1) * LANES] for j in range(2))
+                    terms += [a * x for x in cis_turns(frac(phase))]
                 total = terms if h == 0 else [x + y for x, y in zip(total, terms, strict=True)]
             halves.append(total)
         for i, template in enumerate(summed(halves)):
             part = (below, above)[i // 2][:, i % 2 * LANES : (i % 2 + 1) * LANES]
             edge_ref[q * SUB : (q + 1) * SUB, i * LANES : (i + 1) * LANES] = part - template
+        for start in fills[q :: walkers // SUB]:
+            fill(cols, start)
 
     by_walkers(walkers // SUB, evaluate, edge_block)
-    below_noise, above_noise = below[:, 2 * LANES : 3 * LANES], above[:, 2 * LANES : 3 * LANES]
     noise = jnp.concatenate([below_noise, below_noise, above_noise, above_noise], axis=1)
     rim_ref[...] = (edge_ref[...] * noise).astype(BF16)
+    mine = jnp.concatenate([weighted_ref[:, :LANES], weighted_ref[:, band_bins : band_bins + LANES]], axis=1)
+    tail.append(jnp.concatenate([rim_ref[:, : 2 * LANES], mine], axis=1))
 
     corr = corr[0] + lax.dot_general(rim_ref[:, 2 * LANES :], wave_ref[:, own:], OVER_LANES, preferred_element_type=F32)
     noise = jnp.broadcast_to(jnp.concatenate([above_noise] * 3, axis=1), (2 * SUB, 3 * LANES)).astype(BF16)
@@ -455,40 +532,6 @@
     accept = jnp.where(bins_ref[5:6, :] > 0.0, accept, 0.0)
     accept_ref[...] = accept
     half = accept.astype(BF16)
-
-    mine = jnp.concatenate([weighted_ref[:, :LANES], weighted_ref[:, band_bins : band_bins + LANES]], axis=1)
-    tail = jnp.concatenate([rim_ref[:, : 2 * LANES], mine], axis=1)
-    group = 2 * SUB
-    lane = lane_iota(group).astype(F32)
-    first_noise = noise_ref[0:1, :LANES]
-    chunk = prev_ref.shape[0]
-
-    def chosen_slots(index):
-        place = lax.broadcasted_iota(jnp.int32, (chunk, slots), 0) + (index * chunk + 1)
-        chosen = jnp.where(rank == place.astype(F32), 1.0, 0.0).astype(BF16)
-        cols = [lax.dot_general(chosen, x, OVER_LANES, preferred_element_type=F32) for x in bin_pieces]
-        return cols[0] + cols[1] + cols[2]
-
-    def fill(cols, start):
-        at = slice(start, start + group)
-        re, im, wrapped, _ = slot_wave(cols[at, :], lane)
-        re, im = re.astype(BF16).astype(F32), im.astype(BF16).astype(F32)
-        prev_power_ref[at, :] = (re * re + im * im) * jnp.where(wrapped, first_noise, below_noise)
-        prev_ref[at, :LANES] = jnp.where(wrapped, 0.0, re).astype(BF16)
-        prev_ref[at, LANES : 2 * LANES] = jnp.where(wrapped, 0.0, im).astype(BF16)
-        prev_ref[at, 2 * LANES : 3 * LANES] = jnp.where(wrapped, re, 0.0).astype(BF16)
-        prev_ref[at, 3 * LANES :] = jnp.where(wrapped, im, 0.0).astype(BF16)
-
-    def spilled():
-        corr = lax.dot_general(tail, prev_ref[...], OVER_LANES, preferred_element_type=F32)
-        half = accepted(corr, row_sums(prev_power_ref[...])[0:1, :]).astype(BF16)
-        return jnp.dot(half, prev_ref[:, 2 * LANES :], preferred_element_type=F32)
-
-    def spill(index, carried):
-        cols = chosen_slots(index)
-        for start in range(0, chunk, group):
-            fill(cols, start)
-        return carried + spilled()
 
     squares = [jnp.zeros((walkers, LANES), F32)]
     width = 2 * LANES
@@ -504,15 +547,11 @@
             new_ref[:, start + i * LANES : start + (i + 1) * LANES] = piece
             squares[0] += piece * piece
 
-    cols = chosen_slots(0)
-    fills = list(range(0, chunk, group))
-    starts = [start for start in range(0, own, width) if start % band_bins]
-    for i in range(max(len(fills), len(starts))):
-        if i < len(starts):
-            update(starts[i])
-        if i < len(fills):
-            fill(cols, fills[i])
-    carried = lax.fori_loop(1, (passing + chunk - 1) // chunk, spill, spilled())
+    carried = spilled()
+    for start in range(0, own, width):
+        if start % band_bins:
+            update(start)
+    carried = lax.fori_loop(1, (passing + chunk - 1) // chunk, spill, carried)
     update(0, carried)
     update(band_bins, carried)
     squares = squares[0]
@@ -532,15 +571,15 @@
     fit_ref[...] = jnp.broadcast_to(fit[:bands, 0:1], (bands, LANES))
 
 
-def call(kernel, outs, args, scratch=(), smem=0, flops=0, name=None, hbm=False, last_any=False, alias=None):
+def call(kernel, outs, args, scratch=(), smem=0, flops=0, name=None, hbm=False, unread=0, alias=None):
     vmem = pl.BlockSpec(memory_space=pltpu.VMEM)
     rest = vmem
     if hbm:
         rest = pl.BlockSpec(memory_space=pl.ANY)
         args = [pltpu.with_memory_space_constraint(x, pltpu.HBM) if x.dtype != jnp.int32 or x.ndim > 1 else x for x in args]
     specs = [pl.BlockSpec(memory_space=pltpu.SMEM)] * smem + [rest] * (len(args) - smem)
-    if last_any:
-        specs[-1] = pl.BlockSpec(memory_space=pl.ANY)
+    if unread:
+        specs[-unread:] = [pl.BlockSpec(memory_space=pl.ANY)] * unread
     return pl.pallas_call(
         kernel,
         out_shape=outs,
@@ -579,15 +618,16 @@
     own = 2 * band_bins
 
     span = padded(2 * powers * harmonics * rows)
-    extra = 6 * LANES + 5 * slots
-    cross_rows = -(-(extra - 3 * LANES) // span // SUB) * SUB
-    packed, bins, data, noise = call(
+    extra = 3 * LANES + 5 * slots
+    cross_rows = -(-extra // span // SUB) * SUB
+    packed, bins, data, noise, own_rows = call(
         pack_kernel,
         [
             shape((peers, 1, 3 * span + extra), F32),
             shape((SUB, slots), F32),
             shape((2, band_bins), F32),
             shape((1, band_bins), F32),
+            shape((peers, span), F32),
         ],
         [
             mbh_amp.transpose(1, 2, 3, 0), mbh_phase.transpose(1, 2, 3, 0), data, inv_noise.reshape(-1, LANES),
@@ -615,11 +655,24 @@
         flops=10**9,
         name="waves",
     )
+    direct = rows == 2 * SUB
+    before = [slot_power]
+    scratch = [pltpu.VMEM((stage_rows(45), walkers // SUB, LANES), F32), pltpu.VMEM((walkers // SUB * LANES, 7 * LANES), F32)]
+    if direct:
+        (own_resid,) = call(
+            functools.partial(own_kernel, harmonics),
+            [shape((SUB, own), F32)],
+            [own_rows, data],
+            scratch=[pltpu.VMEM((stage_rows(45), 1, LANES), F32), pltpu.VMEM((LANES, 7 * LANES), F32)],
+            flops=10**9,
+            name="own_template",
+        )
+        before.append(own_resid)
     (to_cross,) = call(
         cross_kernel,
         [shape((peers + cross_rows, span), F32)],
-        [received, slot_power],
-        last_any=True,
+        [received, *before],
+        unread=len(before),
         name="cross",
     )
     pairs = [(g * peers, (g + 1) * peers) for g in range(groups - 1)]
@@ -629,7 +682,7 @@
     extras = received[:, 3 * span :]
     parts = [received[:, i * span : (i + 1) * span] for i in range(3)] + [crossed[:peers]]
     crossed_extra = crossed[peers:]
-    if rows != 2 * SUB:
+    if not direct:
 
         def by_eight(x):
             x = x[:, : 2 * powers * harmonics * rows].reshape(peers, 2 * powers, harmonics, rows)
@@ -640,13 +693,10 @@
         parts = [by_eight(x) for x in parts]
 
     resid, weighted = call(
-        functools.partial(template_kernel, harmonics),
+        functools.partial(template_kernel, harmonics, direct),
         [shape((walkers, own), F32), shape((walkers, own), BF16)],
-        [parts[0], data, noise],
-        scratch=[
-            pltpu.VMEM((4, 2 * QUAD, walkers // SUB, LANES), F32),
-            pltpu.VMEM((4, walkers // SUB * LANES, 2 * LANES), F32),
-        ],
+        [parts[0], data, noise, *before[1:]],
+        scratch=scratch,
         flops=10**9,
         name="template",
     )
@@ -659,9 +709,9 @@
         ],
         scratch=[
             pltpu.VMEM((min(slots, LANES), 4 * LANES), BF16),
-            pltpu.VMEM((min(slots, LANES), LANES), F32),
-            pltpu.VMEM((2, 2 * QUAD, walkers // SUB, LANES), F32),
-            pltpu.VMEM((2, walkers // SUB * LANES, 2 * LANES), F32),
+            pltpu.VMEM((min(slots, LANES), 3 * LANES), BF16),
+            pltpu.VMEM((stage_rows(48), walkers // SUB, LANES), F32),
+            pltpu.VMEM((walkers // SUB * LANES, 4 * LANES), F32),
             pltpu.VMEM((walkers, 4 * LANES), F32),
             pltpu.VMEM((walkers, 4 * LANES), BF16),
         ],

time: 37.3 us -> 36.4 us (0.976)
  waiting for transfers between devices: 10.5 us -> 9.81 us
    all_to_all x1, waiting for transfers between devices: 5.31 us -> 4.61 us  [local(): lax.all_to_all(packed, 'shard', split_axis=0, concat_axis=0, tiled=True)]
    pallas_call x6 -> x7, Pallas kernels: 12.3 us -> 12.3 us  [call(): pl.pallas_call(kernel, out_shape=outs, in_specs=specs, out_specs=[vmem] *...]
  transfers between devices with their start and end apart: 3 -> 3, of which waited for: 2 -> 2; matrix products, arithmetic and copies ran while one was open for 0% -> 0% of each run, Pallas kernels for 19% -> 20%
where the time goes in v5:
time: 36.4 us; the launch traced here: 36.1 us
  Pallas kernels  12.3 us (34%)
  starting transfers between devices  12 us (33%)
  waiting for transfers between devices  9.81 us (27%)
  between operations  1.37 us (4%)
  other arithmetic  0.53 us (1%)
    pallas_call x7, Pallas kernels, call(): pl.pallas_call(kernel, out_shape=outs, in_specs=specs, out_specs=[vmem] *...  12.3 us
    all_to_all x1, starting transfers between devices, local(): lax.all_to_all(packed, 'shard', split_axis=0, concat_axis=0, tiled=True)  7.29 us
    all_to_all x1, waiting for transfers between devices, local(): lax.all_to_all(log_power, BOTH, split_axis=0, concat_axis=0, tiled=True)  5.2 us
    all_to_all x1, waiting for transfers between devices, local(): lax.all_to_all(packed, 'shard', split_axis=0, concat_axis=0, tiled=True)  4.61 us
    all_to_all x1, starting transfers between devices, local(): lax.all_to_all(log_power, BOTH, split_axis=0, concat_axis=0, tiled=True)  3.45 us
    ppermute x1, starting transfers between devices, local(): crossed = lax.ppermute(to_cross, BOTH, pairs)  1.29 us
  transfers between devices with their start and end apart: 3, of which 2 were waited for; matrix products, arithmetic and copies ran while one was open for 0% of the time, Pallas kernels for 20%

profile of v5, /device:TPU:0, one launch (start us, length us, event | category | flops | bytes accessed | tf_op | source)
XLA Modules:
  0.0 36.1 jit_solution(156993159026905525)
XLA Ops:
  1.3 1.9 %pack.1 = (f32[8,1,4864]{2,1,0:T(1,128)}, f32[8,512]{1,0:T(8,128)S(1)}, f32[2,1024]{1,0:T(2,128)S(1)}, f32[1,1024]{1,0:T(1,128)S(1)}, f32[8,640]{1,0:T(8,128)S(1)}) custom-call(f32[6,3,8,16]{3,2,1,0:T(8,128)} %bitcast.12, f32[6,3,8,16]{3,2,1,0:T(8,128)} %bitcast.13, f32[2,1024]{1,0:T(2,128)} %data_hbm.1, bf16[8,128]{1,0:T(8,128)(2,1)} %bitcast.15, ...), custom_call_target="tpu_custom_call" | custom-call | bytes 1048576 | tf_op jit(solution)/shard_map/pack/pallas_call | solution.py:583
  3.1 7.3 %all-to-all-start = ((f32[8,1,4864]{2,1,0:T(1,128)}), f32[8,1,4864]{2,1,0:T(1,128)S(1)}, u32[]{:S(2)}, u32[]{:S(2)}) async-start(f32[8,1,4864]{2,1,0:T(1,128)} %get-tuple-element.19), calls=%async_computation | async-start | bytes 311296 | tf_op jit(solution)/shard_map/all_to_all | solution.py:648
  10.4 0.6 %own_template.1.refs_3_.refs_1_ = f32[8,2048]{1,0:T(8,128)S(1)} custom-call(f32[8,640]{1,0:T(8,128)S(1)} %get-tuple-element.22.rec_ref, f32[2,1024]{1,0:T(2,128)S(1)} %get-tuple-element.20.data_ref.refs_1_), custom_call_target="tpu_custom_call" | custom-call | flops 1000000000 | bytes 1048576 | tf_op jit(solution)/shard_map/own_template/pallas_call | solution.py:583
  11.1 2.3 %waves.1 = (bf16[512,2304]{1,0:T(8,128)(2,1)S(1)}, f32[8,512]{1,0:T(8,128)S(1)}, bf16[512,384]{1,0:T(8,128)(2,1)S(1)}) custom-call(f32[8,512]{1,0:T(8,128)S(1)} %get-tuple-element.25.bins_ref, f32[1,1024]{1,0:T(1,128)S(1)} %get-tuple-element.21.refs_2_.noise_ref), custom_call_target="tpu_custom_call" | custom-call | flops 1000000000 | bytes 1048576 | tf_op jit(solution)/shard_map/waves/pallas_call | solution.py:583
  13.3 4.6 %all-to-all-done = f32[8,1,4864]{2,1,0:T(1,128)S(1)} async-done(((f32[8,1,4864]{2,1,0:T(1,128)}), f32[8,1,4864]{2,1,0:T(1,128)S(1)}, u32[]{:S(2)}, u32[]{:S(2)}) %all-to-all-start) | async-done | bytes 155680 | tf_op jit(solution)/shard_map/all_to_all | solution.py:648
  18.0 1.3 %collective-permute-start = (f32[16,640]{1,0:T(8,128)S(1)}, f32[16,640]{1,0:T(8,128)S(1)}, u32[]{:S(2)}, u32[]{:S(2)}) collective-permute-start(f32[16,640]{1,0:T(8,128)S(1)} %cross.1), channel_id=1, source_target_pairs={{0,8},{8,16},{16,24},{15,7},{23,15},{31,23}} | collective-permute-start | bytes 122888 | tf_op jit(solution)/shard_map/ppermute | solution.py:680
  19.3 2.4 %template.1 = (f32[64,2048]{1,0:T(8,128)S(1)}, bf16[64,2048]{1,0:T(8,128)(2,1)S(1)}) custom-call(f32[8,640]{1,0:T(8,128)S(1)} %slice.23.refs_0_, f32[2,1024]{1,0:T(2,128)S(1)} %get-tuple-element.20.data_ref.refs_1_, f32[1,1024]{1,0:T(1,128)S(1)} %get-tuple-element.21.refs_2_.noise_ref, f32[8,2048]{1,0:T(8,128)S(1)} %own_template.1.refs_3_.refs_1_), custom_call_target="tpu_custom_call" | custom-call | flops 1000000000 | bytes 1048576 | tf_op jit(solution)/shard_map/template/pallas_call | solution.py:583
  21.8 0.0 collective-permute-done
  21.8 3.2 %scores.1 = (f32[64,512]{1,0:T(8,128)S(1)}, f32[64,2048]{1,0:T(8,128)S(1)}, f32[32,1,128]{2,1,0:T(1,128)}) custom-call(bf16[64,2048]{1,0:T(8,128)(2,1)S(1)} %get-tuple-element.23.weighted_ref, f32[64,2048]{1,0:T(8,128)S(1)} %get-tuple-element.24.resid_ref, f32[1,1024]{1,0:T(1,128)S(1)} %get-tuple-element.21.refs_2_.noise_ref, ...), custom_call_target="tpu_custom_call" | custom-call | bytes 1048576 | tf_op jit(solution)/shard_map/scores/pallas_call | solution.py:583
  25.0 3.5 %all-to-all-start.1 = ((f32[32,1,128]{2,1,0:T(1,128)}), f32[32,1,128]{2,1,0:T(1,128)S(1)}, u32[]{:S(2)}, u32[]{:S(2)}) async-start(f32[32,1,128]{2,1,0:T(1,128)} %get-tuple-element.34), calls=%async_computation.1 | async-start | bytes 32768 | tf_op jit(solution)/shard_map/all_to_all | solution.py:720
  28.5 1.9 %outputs.1 = (f32[64,512]{1,0:T(8,128)}, f32[64,2,1024]{2,1,0:T(2,128)}, f32[32,128]{1,0:T(8,128)S(1)}) custom-call(f32[64,512]{1,0:T(8,128)S(1)} %get-tuple-element.29.accept_ref, f32[64,2048]{1,0:T(8,128)S(1)} %get-tuple-element.30.new_ref), custom_call_target="tpu_custom_call" | custom-call | bytes 1048576 | tf_op jit(solution)/shard_map/outputs/pallas_call | solution.py:583
  30.4 5.2 %all-to-all-done.1 = f32[32,1,128]{2,1,0:T(1,128)S(1)} async-done(((f32[32,1,128]{2,1,0:T(1,128)}), f32[32,1,128]{2,1,0:T(1,128)S(1)}, u32[]{:S(2)}, u32[]{:S(2)}) %all-to-all-start.1) | async-done | bytes 16416 | tf_op jit(solution)/shard_map/all_to_all | solution.py:720
  35.6 0.5 %multiply_reduce_fusion = f32[128]{0:T(128)} fusion(f32[32,128]{1,0:T(8,128)S(1)} %get-tuple-element.33, f32[32,128]{1,0:T(8,128)S(1)} %bitcast.14), kind=kLoop, calls=%fused_computation.1 | loop fusion | flops 8064 | bytes 33280 | tf_op jit(solution)/shard_map/reduce_sum | solution.py:727
  (6 shorter events, 0.1 us)
Async XLA Ops:
  3.1 14.8 %all-to-all-start = ((f32[8,1,4864]{2,1,0:T(1,128)}), f32[8,1,4864]{2,1,0:T(1,128)S(1)}, u32[]{:S(2)}, u32[]{:S(2)}) async-start(f32[8,1,4864]{2,1,0:T(1,128)} %get-tuple-element.19), calls=%async_computation | async-start | bytes 311296 | tf_op jit(solution)/shard_map/all_to_all | solution.py:648
  18.0 3.8 %collective-permute-start = (f32[16,640]{1,0:T(8,128)S(1)}, f32[16,640]{1,0:T(8,128)S(1)}, u32[]{:S(2)}, u32[]{:S(2)}) collective-permute-start(f32[16,640]{1,0:T(8,128)S(1)} %cross.1), channel_id=1, source_target_pairs={{0,8},{8,16},{16,24},{15,7},{23,15},{31,23}} | collective-permute-start | bytes 122888 | tf_op jit(solution)/shard_map/ppermute | solution.py:680
  25.0 10.6 %all-to-all-start.1 = ((f32[32,1,128]{2,1,0:T(1,128)}), f32[32,1,128]{2,1,0:T(1,128)S(1)}, u32[]{:S(2)}, u32[]{:S(2)}) async-start(f32[32,1,128]{2,1,0:T(1,128)} %get-tuple-element.34), calls=%async_computation.1 | async-start | bytes 32768 | tf_op jit(solution)/shard_map/all_to_all | solution.py:720

commit v6 on v5

--- a/solution.py
+++ b/solution.py
@@ -22,13 +22,14 @@
 TAU_A = np.float32(round(2.0 * math.pi * 512) / 512)
 TAU_B = np.float32(round((2.0 * math.pi - float(TAU_A)) * 2**22) / 2**22)
 TAU_C = np.float32(2.0 * math.pi - float(TAU_A) - float(TAU_B))
-MAGIC = np.float32(1.5 * 2**23)
 SIN2 = (6.283185160089475, -10.33541375785372, 5.100062754574036, -1.1960903483123309, 0.15444025802555503)
 COS1 = (0.9999999534666666, -4.934792858675247, 4.058411914166824, -1.3318801612473732, 0.2196967986012024)
+SIN_ROOT2 = tuple(c / math.sqrt(2.0) for c in SIN2)
+COS_ROOT2 = tuple(c * math.sqrt(2.0) for c in COS1)
 
 
 def nearest(x):
-    return (x + MAGIC) - MAGIC
+    return jnp.round(x)
 
 
 def padded(count):
@@ -44,9 +45,9 @@
 
 def cis_turns(r):
     y = r * r
-    s2 = poly(y, SIN2) * r
-    c1 = poly(y, COS1)
-    return np.float32(1.0) - np.float32(0.5) * (s2 * s2), s2 * c1
+    s2 = poly(y, SIN_ROOT2) * r
+    c1 = poly(y, COS_ROOT2)
+    return np.float32(1.0) - s2 * s2, s2 * c1
 
 
 def turns(angle):
@@ -447,7 +448,7 @@
         ranks.append(rank + ranks[-1][:, LANES - 1 :] if ranks else rank)
     passing = jnp.max(ranks[-1]).astype(jnp.int32)
     rank = jnp.where(passes, jnp.concatenate(ranks, axis=1), 0.0)
-    bin_pieces = [x.astype(BF16) for x in pieces(bins)]
+    bin_pieces = jnp.concatenate(pieces(bins), axis=0).astype(BF16)
 
     below_noise, above_noise = below[:, 2 * LANES : 3 * LANES], above[:, 2 * LANES : 3 * LANES]
     group = 2 * SUB
@@ -459,8 +460,8 @@
     def chosen_slots(index):
         place = lax.broadcasted_iota(jnp.int32, (chunk, slots), 0) + (index * chunk + 1)
         chosen = jnp.where(rank == place.astype(F32), 1.0, 0.0).astype(BF16)
-        cols = [lax.dot_general(chosen, x, OVER_LANES, preferred_element_type=F32) for x in bin_pieces]
-        return cols[0] + cols[1] + cols[2]
+        cols = lax.dot_general(chosen, bin_pieces, OVER_LANES, preferred_element_type=F32)
+        return cols[:, :SUB] + cols[:, SUB : 2 * SUB] + cols[:, 2 * SUB : 3 * SUB]
 
     def fill(cols, start):
         at = slice(start, start + group)

time: 36.4 us -> 36.3 us (level)
  no operation moved by 1% of the time
where the time goes in v6:
time: 36.3 us; the launch traced here: 36 us
  Pallas kernels  12.2 us (34%)
  starting transfers between devices  12 us (33%)
  waiting for transfers between devices  9.82 us (27%)
  between operations  1.37 us (4%)
  other arithmetic  0.53 us (1%)
    pallas_call x7, Pallas kernels, call(): pl.pallas_call(kernel, out_shape=outs, in_specs=specs, out_specs=[vmem] *...  12.2 us
    all_to_all x1, starting transfers between devices, local(): lax.all_to_all(packed, 'shard', split_axis=0, concat_axis=0, tiled=True)  7.29 us
    all_to_all x1, waiting for transfers between devices, local(): lax.all_to_all(log_power, BOTH, split_axis=0, concat_axis=0, tiled=True)  5.2 us
    all_to_all x1, waiting for transfers between devices, local(): lax.all_to_all(packed, 'shard', split_axis=0, concat_axis=0, tiled=True)  4.62 us
    all_to_all x1, starting transfers between devices, local(): lax.all_to_all(log_power, BOTH, split_axis=0, concat_axis=0, tiled=True)  3.45 us
    ppermute x1, starting transfers between devices, local(): crossed = lax.ppermute(to_cross, BOTH, pairs)  1.29 us
  transfers between devices with their start and end apart: 3, of which 2 were waited for; matrix products, arithmetic and copies ran while one was open for 0% of the time, Pallas kernels for 20%

profile of v6, /device:TPU:0, one launch (start us, length us, event | category | flops | bytes accessed | tf_op | source)
XLA Modules:
  0.0 36.0 jit_solution(9658700726820815091)
XLA Ops:
  1.3 1.9 %pack.1 = (f32[8,1,4864]{2,1,0:T(1,128)}, f32[8,512]{1,0:T(8,128)S(1)}, f32[2,1024]{1,0:T(2,128)S(1)}, f32[1,1024]{1,0:T(1,128)S(1)}, f32[8,640]{1,0:T(8,128)S(1)}) custom-call(f32[6,3,8,16]{3,2,1,0:T(8,128)} %bitcast.12, f32[6,3,8,16]{3,2,1,0:T(8,128)} %bitcast.13, f32[2,1024]{1,0:T(2,128)} %data_hbm.1, bf16[8,128]{1,0:T(8,128)(2,1)} %bitcast.15, ...), custom_call_target="tpu_custom_call" | custom-call | bytes 1048576 | tf_op jit(solution)/shard_map/pack/pallas_call | solution.py:584
  3.1 7.3 %all-to-all-start = ((f32[8,1,4864]{2,1,0:T(1,128)}), f32[8,1,4864]{2,1,0:T(1,128)S(1)}, u32[]{:S(2)}, u32[]{:S(2)}) async-start(f32[8,1,4864]{2,1,0:T(1,128)} %get-tuple-element.19), calls=%async_computation | async-start | bytes 311296 | tf_op jit(solution)/shard_map/all_to_all | solution.py:649
  10.4 0.6 %own_template.1.refs_3_.refs_1_ = f32[8,2048]{1,0:T(8,128)S(1)} custom-call(f32[8,640]{1,0:T(8,128)S(1)} %get-tuple-element.22.rec_ref, f32[2,1024]{1,0:T(2,128)S(1)} %get-tuple-element.20.data_ref.refs_1_), custom_call_target="tpu_custom_call" | custom-call | flops 1000000000 | bytes 1048576 | tf_op jit(solution)/shard_map/own_template/pallas_call | solution.py:584
  11.1 2.3 %waves.1 = (bf16[512,2304]{1,0:T(8,128)(2,1)S(1)}, f32[8,512]{1,0:T(8,128)S(1)}, bf16[512,384]{1,0:T(8,128)(2,1)S(1)}) custom-call(f32[8,512]{1,0:T(8,128)S(1)} %get-tuple-element.25.bins_ref, f32[1,1024]{1,0:T(1,128)S(1)} %get-tuple-element.21.refs_2_.noise_ref), custom_call_target="tpu_custom_call" | custom-call | flops 1000000000 | bytes 1048576 | tf_op jit(solution)/shard_map/waves/pallas_call | solution.py:584
  13.3 4.6 %all-to-all-done = f32[8,1,4864]{2,1,0:T(1,128)S(1)} async-done(((f32[8,1,4864]{2,1,0:T(1,128)}), f32[8,1,4864]{2,1,0:T(1,128)S(1)}, u32[]{:S(2)}, u32[]{:S(2)}) %all-to-all-start) | async-done | bytes 155680 | tf_op jit(solution)/shard_map/all_to_all | solution.py:649
  18.0 1.3 %collective-permute-start = (f32[16,640]{1,0:T(8,128)S(1)}, f32[16,640]{1,0:T(8,128)S(1)}, u32[]{:S(2)}, u32[]{:S(2)}) collective-permute-start(f32[16,640]{1,0:T(8,128)S(1)} %cross.1), channel_id=1, source_target_pairs={{0,8},{8,16},{16,24},{15,7},{23,15},{31,23}} | collective-permute-start | bytes 122888 | tf_op jit(solution)/shard_map/ppermute | solution.py:681
  19.3 2.4 %template.1 = (f32[64,2048]{1,0:T(8,128)S(1)}, bf16[64,2048]{1,0:T(8,128)(2,1)S(1)}) custom-call(f32[8,640]{1,0:T(8,128)S(1)} %slice.23.refs_0_, f32[2,1024]{1,0:T(2,128)S(1)} %get-tuple-element.20.data_ref.refs_1_, f32[1,1024]{1,0:T(1,128)S(1)} %get-tuple-element.21.refs_2_.noise_ref, f32[8,2048]{1,0:T(8,128)S(1)} %own_template.1.refs_3_.refs_1_), custom_call_target="tpu_custom_call" | custom-call | flops 1000000000 | bytes 1048576 | tf_op jit(solution)/shard_map/template/pallas_call | solution.py:584
  21.7 0.0 collective-permute-done
  21.8 3.1 %scores.1 = (f32[64,512]{1,0:T(8,128)S(1)}, f32[64,2048]{1,0:T(8,128)S(1)}, f32[32,1,128]{2,1,0:T(1,128)}) custom-call(bf16[64,2048]{1,0:T(8,128)(2,1)S(1)} %get-tuple-element.23.weighted_ref, f32[64,2048]{1,0:T(8,128)S(1)} %get-tuple-element.24.resid_ref, f32[1,1024]{1,0:T(1,128)S(1)} %get-tuple-element.21.refs_2_.noise_ref, ...), custom_call_target="tpu_custom_call" | custom-call | bytes 1048576 | tf_op jit(solution)/shard_map/scores/pallas_call | solution.py:584
  24.9 3.4 %all-to-all-start.1 = ((f32[32,1,128]{2,1,0:T(1,128)}), f32[32,1,128]{2,1,0:T(1,128)S(1)}, u32[]{:S(2)}, u32[]{:S(2)}) async-start(f32[32,1,128]{2,1,0:T(1,128)} %get-tuple-element.34), calls=%async_computation.1 | async-start | bytes 32768 | tf_op jit(solution)/shard_map/all_to_all | solution.py:721
  28.4 1.9 %outputs.1 = (f32[64,512]{1,0:T(8,128)}, f32[64,2,1024]{2,1,0:T(2,128)}, f32[32,128]{1,0:T(8,128)S(1)}) custom-call(f32[64,512]{1,0:T(8,128)S(1)} %get-tuple-element.29.accept_ref, f32[64,2048]{1,0:T(8,128)S(1)} %get-tuple-element.30.new_ref), custom_call_target="tpu_custom_call" | custom-call | bytes 1048576 | tf_op jit(solution)/shard_map/outputs/pallas_call | solution.py:584
  30.3 5.2 %all-to-all-done.1 = f32[32,1,128]{2,1,0:T(1,128)S(1)} async-done(((f32[32,1,128]{2,1,0:T(1,128)}), f32[32,1,128]{2,1,0:T(1,128)S(1)}, u32[]{:S(2)}, u32[]{:S(2)}) %all-to-all-start.1) | async-done | bytes 16416 | tf_op jit(solution)/shard_map/all_to_all | solution.py:721
  35.5 0.5 %multiply_reduce_fusion = f32[128]{0:T(128)} fusion(f32[32,128]{1,0:T(8,128)S(1)} %get-tuple-element.33, f32[32,128]{1,0:T(8,128)S(1)} %bitcast.14), kind=kLoop, calls=%fused_computation.1 | loop fusion | flops 8064 | bytes 33280 | tf_op jit(solution)/shard_map/reduce_sum | solution.py:728
  (6 shorter events, 0.1 us)
Async XLA Ops:
  3.1 14.8 %all-to-all-start = ((f32[8,1,4864]{2,1,0:T(1,128)}), f32[8,1,4864]{2,1,0:T(1,128)S(1)}, u32[]{:S(2)}, u32[]{:S(2)}) async-start(f32[8,1,4864]{2,1,0:T(1,128)} %get-tuple-element.19), calls=%async_computation | async-start | bytes 311296 | tf_op jit(solution)/shard_map/all_to_all | solution.py:649
  18.0 3.7 %collective-permute-start = (f32[16,640]{1,0:T(8,128)S(1)}, f32[16,640]{1,0:T(8,128)S(1)}, u32[]{:S(2)}, u32[]{:S(2)}) collective-permute-start(f32[16,640]{1,0:T(8,128)S(1)} %cross.1), channel_id=1, source_target_pairs={{0,8},{8,16},{16,24},{15,7},{23,15},{31,23}} | collective-permute-start | bytes 122888 | tf_op jit(solution)/shard_map/ppermute | solution.py:681
  24.9 10.6 %all-to-all-start.1 = ((f32[32,1,128]{2,1,0:T(1,128)}), f32[32,1,128]{2,1,0:T(1,128)S(1)}, u32[]{:S(2)}, u32[]{:S(2)}) async-start(f32[32,1,128]{2,1,0:T(1,128)} %get-tuple-element.34), calls=%async_computation.1 | async-start | bytes 32768 | tf_op jit(solution)/shard_map/all_to_all | solution.py:721

commit v7 on v6

--- a/solution.py
+++ b/solution.py
@@ -709,8 +709,8 @@
             parts[3], crossed_extra,
         ],
         scratch=[
-            pltpu.VMEM((min(slots, LANES), 4 * LANES), BF16),
-            pltpu.VMEM((min(slots, LANES), 3 * LANES), BF16),
+            pltpu.VMEM((min(slots, 6 * 2 * SUB), 4 * LANES), BF16),
+            pltpu.VMEM((min(slots, 6 * 2 * SUB), 3 * LANES), BF16),
             pltpu.VMEM((stage_rows(48), walkers // SUB, LANES), F32),
             pltpu.VMEM((walkers // SUB * LANES, 4 * LANES), F32),
             pltpu.VMEM((walkers, 4 * LANES), F32),

time: 36.3 us -> 36.3 us (level)
  no operation moved by 1% of the time
where the time goes in v7:
time: 36.3 us; the launch traced here: 36 us
  Pallas kernels  12.2 us (34%)
  starting transfers between devices  12 us (33%)
  waiting for transfers between devices  9.82 us (27%)
  between operations  1.37 us (4%)
  other arithmetic  0.53 us (1%)
    pallas_call x7, Pallas kernels, call(): pl.pallas_call(kernel, out_shape=outs, in_specs=specs, out_specs=[vmem] *...  12.2 us
    all_to_all x1, starting transfers between devices, local(): lax.all_to_all(packed, 'shard', split_axis=0, concat_axis=0, tiled=True)  7.29 us
    all_to_all x1, waiting for transfers between devices, local(): lax.all_to_all(log_power, BOTH, split_axis=0, concat_axis=0, tiled=True)  5.2 us
    all_to_all x1, waiting for transfers between devices, local(): lax.all_to_all(packed, 'shard', split_axis=0, concat_axis=0, tiled=True)  4.62 us
    all_to_all x1, starting transfers between devices, local(): lax.all_to_all(log_power, BOTH, split_axis=0, concat_axis=0, tiled=True)  3.45 us
    ppermute x1, starting transfers between devices, local(): crossed = lax.ppermute(to_cross, BOTH, pairs)  1.29 us
  transfers between devices with their start and end apart: 3, of which 2 were waited for; matrix products, arithmetic and copies ran while one was open for 0% of the time, Pallas kernels for 20%

profile of v7, /device:TPU:0, one launch (start us, length us, event | category | flops | bytes accessed | tf_op | source)
XLA Modules:
  0.0 36.0 jit_solution(5491460254125447585)
XLA Ops:
  1.3 1.9 %pack.1 = (f32[8,1,4864]{2,1,0:T(1,128)}, f32[8,512]{1,0:T(8,128)S(1)}, f32[2,1024]{1,0:T(2,128)S(1)}, f32[1,1024]{1,0:T(1,128)S(1)}, f32[8,640]{1,0:T(8,128)S(1)}) custom-call(f32[6,3,8,16]{3,2,1,0:T(8,128)} %bitcast.12, f32[6,3,8,16]{3,2,1,0:T(8,128)} %bitcast.13, f32[2,1024]{1,0:T(2,128)} %data_hbm.1, bf16[8,128]{1,0:T(8,128)(2,1)} %bitcast.15, ...), custom_call_target="tpu_custom_call" | custom-call | bytes 1048576 | tf_op jit(solution)/shard_map/pack/pallas_call | solution.py:584
  3.1 7.3 %all-to-all-start = ((f32[8,1,4864]{2,1,0:T(1,128)}), f32[8,1,4864]{2,1,0:T(1,128)S(1)}, u32[]{:S(2)}, u32[]{:S(2)}) async-start(f32[8,1,4864]{2,1,0:T(1,128)} %get-tuple-element.19), calls=%async_computation | async-start | bytes 311296 | tf_op jit(solution)/shard_map/all_to_all | solution.py:649
  10.4 0.6 %own_template.1.refs_3_.refs_1_ = f32[8,2048]{1,0:T(8,128)S(1)} custom-call(f32[8,640]{1,0:T(8,128)S(1)} %get-tuple-element.22.rec_ref, f32[2,1024]{1,0:T(2,128)S(1)} %get-tuple-element.20.data_ref.refs_1_), custom_call_target="tpu_custom_call" | custom-call | flops 1000000000 | bytes 1048576 | tf_op jit(solution)/shard_map/own_template/pallas_call | solution.py:584
  11.1 2.3 %waves.1 = (bf16[512,2304]{1,0:T(8,128)(2,1)S(1)}, f32[8,512]{1,0:T(8,128)S(1)}, bf16[512,384]{1,0:T(8,128)(2,1)S(1)}) custom-call(f32[8,512]{1,0:T(8,128)S(1)} %get-tuple-element.25.bins_ref, f32[1,1024]{1,0:T(1,128)S(1)} %get-tuple-element.21.refs_2_.noise_ref), custom_call_target="tpu_custom_call" | custom-call | flops 1000000000 | bytes 1048576 | tf_op jit(solution)/shard_map/waves/pallas_call | solution.py:584
  13.3 4.6 %all-to-all-done = f32[8,1,4864]{2,1,0:T(1,128)S(1)} async-done(((f32[8,1,4864]{2,1,0:T(1,128)}), f32[8,1,4864]{2,1,0:T(1,128)S(1)}, u32[]{:S(2)}, u32[]{:S(2)}) %all-to-all-start) | async-done | bytes 155680 | tf_op jit(solution)/shard_map/all_to_all | solution.py:649
  18.0 1.3 %collective-permute-start = (f32[16,640]{1,0:T(8,128)S(1)}, f32[16,640]{1,0:T(8,128)S(1)}, u32[]{:S(2)}, u32[]{:S(2)}) collective-permute-start(f32[16,640]{1,0:T(8,128)S(1)} %cross.1), channel_id=1, source_target_pairs={{0,8},{8,16},{16,24},{15,7},{23,15},{31,23}} | collective-permute-start | bytes 122888 | tf_op jit(solution)/shard_map/ppermute | solution.py:681
  19.3 2.4 %template.1 = (f32[64,2048]{1,0:T(8,128)S(1)}, bf16[64,2048]{1,0:T(8,128)(2,1)S(1)}) custom-call(f32[8,640]{1,0:T(8,128)S(1)} %slice.23.refs_0_, f32[2,1024]{1,0:T(2,128)S(1)} %get-tuple-element.20.data_ref.refs_1_, f32[1,1024]{1,0:T(1,128)S(1)} %get-tuple-element.21.refs_2_.noise_ref, f32[8,2048]{1,0:T(8,128)S(1)} %own_template.1.refs_3_.refs_1_), custom_call_target="tpu_custom_call" | custom-call | flops 1000000000 | bytes 1048576 | tf_op jit(solution)/shard_map/template/pallas_call | solution.py:584
  21.7 0.0 collective-permute-done
  21.8 3.1 %scores.1 = (f32[64,512]{1,0:T(8,128)S(1)}, f32[64,2048]{1,0:T(8,128)S(1)}, f32[32,1,128]{2,1,0:T(1,128)}) custom-call(bf16[64,2048]{1,0:T(8,128)(2,1)S(1)} %get-tuple-element.23.weighted_ref, f32[64,2048]{1,0:T(8,128)S(1)} %get-tuple-element.24.resid_ref, f32[1,1024]{1,0:T(1,128)S(1)} %get-tuple-element.21.refs_2_.noise_ref, ...), custom_call_target="tpu_custom_call" | custom-call | bytes 1048576 | tf_op jit(solution)/shard_map/scores/pallas_call | solution.py:584
  24.9 3.4 %all-to-all-start.1 = ((f32[32,1,128]{2,1,0:T(1,128)}), f32[32,1,128]{2,1,0:T(1,128)S(1)}, u32[]{:S(2)}, u32[]{:S(2)}) async-start(f32[32,1,128]{2,1,0:T(1,128)} %get-tuple-element.34), calls=%async_computation.1 | async-start | bytes 32768 | tf_op jit(solution)/shard_map/all_to_all | solution.py:721
  28.3 1.9 %outputs.1 = (f32[64,512]{1,0:T(8,128)}, f32[64,2,1024]{2,1,0:T(2,128)}, f32[32,128]{1,0:T(8,128)S(1)}) custom-call(f32[64,512]{1,0:T(8,128)S(1)} %get-tuple-element.29.accept_ref, f32[64,2048]{1,0:T(8,128)S(1)} %get-tuple-element.30.new_ref), custom_call_target="tpu_custom_call" | custom-call | bytes 1048576 | tf_op jit(solution)/shard_map/outputs/pallas_call | solution.py:584
  30.3 5.2 %all-to-all-done.1 = f32[32,1,128]{2,1,0:T(1,128)S(1)} async-done(((f32[32,1,128]{2,1,0:T(1,128)}), f32[32,1,128]{2,1,0:T(1,128)S(1)}, u32[]{:S(2)}, u32[]{:S(2)}) %all-to-all-start.1) | async-done | bytes 16416 | tf_op jit(solution)/shard_map/all_to_all | solution.py:721
  35.5 0.5 %multiply_reduce_fusion = f32[128]{0:T(128)} fusion(f32[32,128]{1,0:T(8,128)S(1)} %get-tuple-element.33, f32[32,128]{1,0:T(8,128)S(1)} %bitcast.14), kind=kLoop, calls=%fused_computation.1 | loop fusion | flops 8064 | bytes 33280 | tf_op jit(solution)/shard_map/reduce_sum | solution.py:728
  (6 shorter events, 0.1 us)
Async XLA Ops:
  3.1 14.8 %all-to-all-start = ((f32[8,1,4864]{2,1,0:T(1,128)}), f32[8,1,4864]{2,1,0:T(1,128)S(1)}, u32[]{:S(2)}, u32[]{:S(2)}) async-start(f32[8,1,4864]{2,1,0:T(1,128)} %get-tuple-element.19), calls=%async_computation | async-start | bytes 311296 | tf_op jit(solution)/shard_map/all_to_all | solution.py:649
  18.0 3.7 %collective-permute-start = (f32[16,640]{1,0:T(8,128)S(1)}, f32[16,640]{1,0:T(8,128)S(1)}, u32[]{:S(2)}, u32[]{:S(2)}) collective-permute-start(f32[16,640]{1,0:T(8,128)S(1)} %cross.1), channel_id=1, source_target_pairs={{0,8},{8,16},{16,24},{15,7},{23,15},{31,23}} | collective-permute-start | bytes 122888 | tf_op jit(solution)/shard_map/ppermute | solution.py:681
  24.9 10.6 %all-to-all-start.1 = ((f32[32,1,128]{2,1,0:T(1,128)}), f32[32,1,128]{2,1,0:T(1,128)S(1)}, u32[]{:S(2)}, u32[]{:S(2)}) async-start(f32[32,1,128]{2,1,0:T(1,128)} %get-tuple-element.34), calls=%async_computation.1 | async-start | bytes 32768 | tf_op jit(solution)/shard_map/all_to_all | solution.py:721
